TPU v7x, 32 devices: a whole 2x2x4 slice. The times are simulated.
32 devices in a mesh: dp: 8 (over y, x, core), fsdp: 4 (over z).
Axes of the slice: x: 2, y: 2, z: 4, core: 2. Of those that a mesh axis runs over, the one named last changes fastest.
Arguments:
- tokens: bfloat16 [8192, 2048], P(('dp', 'fsdp')), may hold values from -6 to 6
- text: bfloat16 [32, 128, 2048], P(('dp', 'fsdp')), may hold values from -6 to 6
- cotangent: bfloat16 [32, 128, 2048], P(('dp', 'fsdp')), may hold values from -6 to 6
- positions: int32 [32, 128], P(('dp', 'fsdp')), may hold values from 0 to 255, as said below
- text_lengths: int32 [32], P(('dp', 'fsdp')), may hold values from 1 to 128, as said below
- mask_embed: bfloat16 [2048], P(('dp', 'fsdp')), may hold values from -6 to 6
- gain_attn: bfloat16 [2048], P(('dp', 'fsdp')), may hold values from 0.099609375 to 1.8984375
- w_qkv: bfloat16 [2048, 6144], P(('dp', 'fsdp')), may hold values from -0.125 to 0.125
- w_attn_out: bfloat16 [2048, 2048], P(('dp', 'fsdp')), may hold values from -1 to 1
- gain_cross: bfloat16 [2048], P(('dp', 'fsdp')), may hold values from 0.099609375 to 1.8984375
- w_cross_q: bfloat16 [2048, 2048], P(('dp', 'fsdp')), may hold values from -0.125 to 0.125
- w_cross_kv: bfloat16 [2048, 4096], P(('dp', 'fsdp')), may hold values from -0.125 to 0.125
- w_cross_out: bfloat16 [2048, 2048], P(('dp', 'fsdp')), may hold values from -0.75 to 0.75
- gain_mlp: bfloat16 [2048], P(('dp', 'fsdp')), may hold values from 0.099609375 to 1.8984375
- w_up: bfloat16 [2048, 8192], P(('dp', 'fsdp')), may hold values from -0.125 to 0.125
- w_down: bfloat16 [8192, 2048], P(('dp', 'fsdp')), may hold values from -0.0625 to 0.0625
Outputs:
- output: bfloat16 [8192, 2048], P(('dp', 'fsdp'))
- grad_tokens: bfloat16 [8192, 2048], P(('dp', 'fsdp'))
- grad_text: bfloat16 [32, 128, 2048], P(('dp', 'fsdp'))
- grad_mask_embed: float32 [2048], P(('dp', 'fsdp'))
- grad_gain_attn: float32 [2048], P(('dp', 'fsdp'))
- grad_w_qkv: float32 [2048, 6144], P(('dp', 'fsdp'))
- grad_w_attn_out: float32 [2048, 2048], P(('dp', 'fsdp'))
- grad_gain_cross: float32 [2048], P(('dp', 'fsdp'))
- grad_w_cross_q: float32 [2048, 2048], P(('dp', 'fsdp'))
- grad_w_cross_kv: float32 [2048, 4096], P(('dp', 'fsdp'))
- grad_w_cross_out: float32 [2048, 2048], P(('dp', 'fsdp'))
- grad_gain_mlp: float32 [2048], P(('dp', 'fsdp'))
- grad_w_up: float32 [2048, 8192], P(('dp', 'fsdp'))
- grad_w_down: float32 [8192, 2048], P(('dp', 'fsdp'))
Inputs may be any that keep to these rules, and one draw needn't show every extreme that they name: Each image's row holds 128 distinct positions. `text_lengths`: some image has all 128 text tokens valid.
All inputs are finite; a program needn't handle non-finite values.
Results may differ from a plain program's by a relative error of at most 0.02.
Values may be sent and summed in bfloat16 or wider, within the bound.
No kernel may reach another device: no remote copies, remote signals or barrier semaphores. Data moves between devices by JAX's collectives and lax.ppermute only.
A program may use at most 576 MiB of HBM per device.

v0:
```python
import functools

import jax
import jax.numpy as jnp
from jax import lax
from jax.experimental import pallas as pl
from jax.experimental.pallas import tpu as pltpu
from jax.sharding import Mesh, PartitionSpec as P

HEADS = 16
HDIM = 128
TILE = 128
PAD = 16
BF = jnp.bfloat16
F32 = jnp.float32
VMEM_BYTES = 60 << 20


def dot(left, right):
    return jnp.dot(left, right, preferred_element_type=F32)


def dot_t(left, right):
    return lax.dot_general(left, right, (((1,), (1,)), ((), ())), preferred_element_type=F32)


def dot_sum(left, right):
    return lax.dot_general(left, right, (((0,), (0,)), ((), ())), preferred_element_type=F32)


def normed(rows):
    centered = rows - jnp.mean(rows, axis=-1, keepdims=True)
    scale = lax.rsqrt(jnp.mean(centered * centered, axis=-1, keepdims=True) + 1e-05)
    return centered * scale, scale


def norm_back(grad, field, scale):
    return scale * (
        grad
        - jnp.mean(grad, axis=-1, keepdims=True)
        - field * jnp.mean(grad * field, axis=-1, keepdims=True)
    )


def xor_order(stack, me, size):
    bit = 1
    while bit < size:
        split = stack.reshape((size // (2 * bit), 2, bit) + stack.shape[1:])
        turned = jnp.concatenate([split[:, 1:], split[:, :1]], axis=1)
        stack = jnp.where((me & bit) != 0, turned, split).reshape(stack.shape)
        bit *= 2
    return stack


def bits_of(size):
    return [1 << k for k in range(size.bit_length() - 1)]


class Layer:
    def __init__(self, tp, planes):
        self.tp, self.planes = tp, planes
        self.t, self.c, self.z = (lax.axis_index(a) for a in ("tp", "core", "fsdp"))


    def hop(self, value, j):
        return lax.ppermute(value, "tp", [(i, i ^ j) for i in range(self.tp)])

    def other_core(self, value):
        return lax.ppermute(value, "core", [(0, 1), (1, 0)])

    def other_plane(self, value, k):
        return lax.ppermute(value, "fsdp", [(i, i ^ k) for i in range(self.planes)])

    def spread(self, value):
        return [value] + [self.hop(value, j) for j in range(1, self.tp)]

    def collect(self, parts):
        return [parts[0]] + [self.hop(parts[j], j) for j in range(1, self.tp)]

    def tp_direct(self, value):
        return jnp.stack([value] + [self.hop(value, j) for j in range(1, self.tp)])

    def tp_parts(self, value):
        return [value] + [self.hop(value, j) for j in range(1, self.tp)]

    def to_owner(self, stack):
        return [stack[0]] + [self.hop(stack[j], j) for j in range(1, self.tp)]

    def to_rows(self, value):
        return lax.all_to_all(value, ("tp", "core", "fsdp"), 0, 0, tiled=True)

    def gather_cz(self, value):
        planes = jnp.stack([value] + [self.other_plane(value, k) for k in range(1, self.planes)])
        return jnp.concatenate([planes, self.other_core(planes)])


    def shuffle(self, shards):
        return lax.all_to_all(column_blocks(self.tp, shards), "tp", 0, 0, tiled=True)

    def gather_blocks(self, shard):
        return lax.all_gather(shard, ("core", "fsdp"), axis=0)


def blocks_kernel(moves, *refs):
    for source, begin, t, at, size in moves:
        refs[-1][t, :, at : at + size] = refs[source][:, begin : begin + size]


def column_blocks(tp, shards):
    moves, at = [], 0
    for source, (shard, kinds) in enumerate(shards):
        size = shard.shape[1] // (kinds * tp)
        for kind in range(kinds):
            moves += [(source, (kind * tp + t) * size, t, at, size) for t in range(tp)]
            at += size
    rows = shards[0][0].shape[0]
    return in_vmem(
        functools.partial(blocks_kernel, moves),
        "column_blocks",
        [shard for shard, _ in shards],
        [((tp, rows, at), BF)],
    )[0]


def block(weights, t, columns):
    part = weights[:, t, :, columns]
    return part.reshape(part.shape[0] * part.shape[1], part.shape[2])


def project(rows, weights, columns):
    tp = weights.shape[1]
    step = rows.shape[1] // tp
    total = dot(rows[:, :step], block(weights, 0, columns))
    for t in range(1, tp):
        total = total + dot(rows[:, t * step : (t + 1) * step], block(weights, t, columns))
    return total


def start_copies(pairs, sems):
    copies = [pltpu.make_async_copy(a, b, sems.at[k]) for k, (a, b) in enumerate(pairs)]
    for copy in copies:
        copy.start()
    return copies


def softmax_head(queries, keys, bias, free, extra):
    scale = HDIM ** (-0.5)
    logits = dot_t(queries, keys[:free]) * scale
    if bias is not None:
        logits = logits + bias
    top = jnp.max(logits, axis=-1, keepdims=True)
    if not extra:
        weighs = jnp.exp(logits - top)
        return weighs / jnp.sum(weighs, axis=-1, keepdims=True), None
    one = dot_t(queries, keys[free:])[:, :1] * scale
    top = jnp.maximum(top, one)
    weighs, one = jnp.exp(logits - top), jnp.exp(one - top) * extra
    total = jnp.sum(weighs, axis=-1, keepdims=True) + one
    return weighs / total, one / total


def self_kernel(tp, local, count, *refs):
    entries, masked_entries, gathered = refs[:tp], refs[tp], refs[tp + 1]
    partial = refs[tp + 2 : 2 * tp + 2]
    packed, mix_out, probs_out, weight, held, mixed, sems = refs[2 * tp + 2 :]
    free, rows, span = entries[0].shape[0], packed.shape[1], local * HDIM
    pairs = [(ref, held.at[i * free : (i + 1) * free]) for i, ref in enumerate(entries)]
    pairs += [(masked_entries, held.at[tp * free :]), (gathered, weight)]
    for copy in start_copies(pairs, sems):
        copy.wait()
    for k in range(3):
        cols = slice(k * span, (k + 1) * span)
        found = project(held[...], weight, cols).astype(BF)
        for i in range(tp):
            packed[i, :free, cols] = found[i * free : (i + 1) * free]
            packed[i, free:, cols] = found[tp * free :]
    probs_out[...] = jnp.zeros_like(probs_out)
    for i in range(tp):
        for h in range(local):
            cols = [slice(k * span + h * HDIM, k * span + (h + 1) * HDIM) for k in range(3)]
            queries, keys, values = (packed[i, :, c] for c in cols)
            probs, one = softmax_head(queries, keys, None, free, float(count))
            probs_out[i, h : h + 1, :free] = probs[free : free + 1]
            probs_out[i, h : h + 1, free:] = jnp.broadcast_to(one[free : free + 1], (1, TILE))
            mixture = dot(probs.astype(BF), values[:free])
            mixture = mixture + one.astype(BF).astype(F32) * values[free : free + 1].astype(F32)
            mixed[i * rows : (i + 1) * rows, cols[0]] = mixture.astype(BF)
        mix_out[i] = mixed[i * rows + free : (i + 1) * rows]
    write_out(tp, mixed, weight, partial)


def write_out(tp, mixed, weight, partial):
    rows, width = partial[0].shape
    span = width // tp
    for t in range(tp):
        added = dot(mixed[...], block(weight, t, slice(3 * span, 4 * span))).astype(BF)
        for i in range(tp):
            partial[i][:, t * span : (t + 1) * span] = added[i * rows : (i + 1) * rows]


def masked_row(last, i, one_entry, one_row):
    last = last.astype(F32)
    one_entry[i : i + 1] = last[:1]
    one_row[i : i + 1] = last[1:2] + last[2:3] + last[3:4]


def cross_kernel(tp, local, *refs):
    entries, text = refs[:tp], refs[tp : 2 * tp]
    bias, gathered = refs[2 * tp : 2 * tp + 2]
    partial = refs[2 * tp + 2 : 3 * tp + 2]
    pair, query_out, mix_out, probs_out, one_entry, one_row = refs[3 * tp + 2 : 3 * tp + 8]
    weight, held, held_text, queries, mixed, sems = refs[3 * tp + 8 :]
    rows, txt, span = entries[0].shape[0], text[0].shape[0], local * HDIM
    free = rows - PAD
    pairs = [(ref, held_text.at[i * txt : (i + 1) * txt]) for i, ref in enumerate(text)]
    pairs += [(ref, held.at[i * rows : (i + 1) * rows]) for i, ref in enumerate(entries)]
    pairs += [(gathered, weight)]
    for copy in start_copies(pairs, sems):
        copy.wait()
    for k in range(2):
        cols = slice(k * span, (k + 1) * span)
        found = project(held_text[...], weight, cols).astype(BF)
        for i in range(tp):
            pair[i, :, cols] = found[i * txt : (i + 1) * txt]
    queries[...] = project(held[...], weight, slice(2 * span, 3 * span)).astype(BF)
    probs_out[...] = jnp.zeros_like(probs_out)
    for i in range(tp):
        masked_row(held[i * rows + free : (i + 1) * rows], i, one_entry, one_row)
        query_out[i] = queries[i * rows + free : (i + 1) * rows]
        for h in range(local):
            cols = slice(h * HDIM, (h + 1) * HDIM)
            keys = pair[i, :, cols]
            values = pair[i, :, span + h * HDIM : span + (h + 1) * HDIM]
            some = queries[i * rows : (i + 1) * rows, cols]
            probs, _ = softmax_head(some, keys, bias[i : i + 1], txt, 0)
            probs_out[i, h : h + 1] = probs[free : free + 1]
            mixed[i * rows : (i + 1) * rows, cols] = dot(probs.astype(BF), values).astype(BF)
        mix_out[i] = mixed[i * rows + free : (i + 1) * rows]
    write_out(tp, mixed, weight, partial)


def gelu_parts(value):
    slope = 0.7978845608
    bent = jnp.tanh(slope * (value + 0.044715 * value * value * value))
    half = 0.5 * (1.0 + bent)
    steep = slope * (1.0 + 3.0 * 0.044715 * value * value)
    return value * half, half + 0.5 * value * (1.0 - bent * bent) * steep


def up_kernel(entries, weight, active):
    active[...] = gelu_parts(project(entries[...], weight, slice(None)))[0].astype(BF)


def mlp_back_kernel(tp, *refs):
    entries_all, grad_active, gathered = refs[:tp], refs[tp], refs[tp + 1]
    active, grad_pre, grad_entry, one_entry, one_row, weight, last, entries, sem = refs[tp + 2 :]
    step, free = entries.shape[1] // tp, entries_all[0].shape[0] - PAD
    ends = [
        pltpu.make_async_copy(ref.at[free:], last.at[i], sem.at[tp + i])
        for i, ref in enumerate(entries_all)
    ]
    for copy in ends:
        copy.start()
    copies = [
        pltpu.make_async_copy(gathered.at[:, t], weight.at[:, t], sem.at[t]) for t in range(tp)
    ]
    for copy in copies:
        copy.start()
    for i, copy in enumerate(ends):
        copy.wait()
        masked_row(last[i], i, one_entry, one_row)
    entries[...] = jnp.zeros_like(entries)
    entries[:tp] = one_entry[...]
    hidden = jnp.zeros(active.shape, F32)
    for t, copy in enumerate(copies):
        copy.wait()
        rows = entries[:, t * step : (t + 1) * step].astype(BF)
        hidden = hidden + dot(rows, block(weight, t, slice(None)))
    value, steep = gelu_parts(hidden)
    active[...] = value.astype(BF)
    grad_pre[...] = (steep * grad_active[...]).astype(BF)
    for t in range(tp):
        back = dot_t(grad_pre[...], block(weight, t, slice(None)))
        grad_entry[:, t * step : (t + 1) * step] = back[:tp]


def summed(parts, i):
    total = parts[0][i : i + 1]
    for j in range(1, len(parts)):
        total = total + parts[j][i ^ j : (i ^ j) + 1]
    return total


def out_back(rows, weights, columns):
    tp = weights.shape[1]
    step = rows.shape[1] // tp
    total = dot_t(rows[:, :step], block(weights, 0, columns))
    for t in range(1, tp):
        total = total + dot_t(rows[:, t * step : (t + 1) * step], block(weights, t, columns))
    return total.astype(BF).astype(F32)


def head_mask(span):
    heads = lax.broadcasted_iota(jnp.int32, (8, span), 0)
    return lax.broadcasted_iota(jnp.int32, (8, span), 1) // HDIM == heads


def row_back(parts, rows, gain, base, i, out, gain_row):
    grad = summed(parts, i)
    field, scale = normed(rows[i : i + 1])
    out[i : i + 1] = base[i : i + 1] + norm_back(grad * gain[...], field, scale)
    if i == 0:
        gain_row[...] = grad * field


def cross_back_kernel(
    tp, base, rows, gain, pair, probs, gathered, *refs,
):
    parts = refs[:tp]
    grad_mid, grad_cmix, scores, grad_cq, grad_entry, gain_row = refs[tp : tp + 6]
    weight, held, sems = refs[tp + 6 :]
    span = weight.shape[3] // 2
    copies = [
        pltpu.make_async_copy(gathered.at[:, :, :, 2 * span :], weight, sems.at[0]),
    ]
    for copy in copies:
        copy.start()
    held[...] = jnp.zeros_like(held)
    for i in range(tp):
        row_back(parts, rows, gain, base, i, held, gain_row)
    grad_mid[...] = held[:tp]
    copies[0].wait()
    mixed = out_back(held[...].astype(BF), weight, slice(span, 2 * span))
    grad_cmix[...] = mixed[:tp]
    mask = head_mask(span)
    held[...] = jnp.zeros_like(held)
    for i in range(tp):
        spread = jnp.where(mask, mixed[i : i + 1], 0.0).astype(BF)
        grad_probs = dot_t(spread, pair[i, :, span:])
        weighs = probs[i]
        grad = weighs * (grad_probs - jnp.sum(grad_probs * weighs, axis=-1, keepdims=True))
        grad = grad.astype(BF)
        scores[i] = grad.astype(F32)
        back = jnp.where(mask, dot(grad, pair[i, :, :span]), 0.0)
        held[i : i + 1, :span] = jnp.sum(back, axis=0, keepdims=True) * HDIM ** (-0.5)
    grad_cq[...] = held[:tp, :span]
    queries = held[:, :span].astype(BF)
    step = grad_entry.shape[1] // tp
    for t in range(tp):
        back = dot_t(queries, block(weight, t, slice(0, span)))
        grad_entry[:, t * step : (t + 1) * step] = back[:tp]


def spread_heads(rows, i, spreads, mask):
    spreads[8 * i : 8 * i + 8] = jnp.where(mask, rows, 0.0)


def text_back_kernel(tp, local, *refs):
    scores, probs, query_one, grad_cmix, kvq = refs[:5]
    cross_one_row, mlp_one, grad_pre, grad_cq, mixed, cross, active, base, grad_mid = refs[5:14]
    text = refs[14 : 14 + tp]
    sent = refs[14 + tp : 14 + 2 * tp]
    lefts, factors, weight, held, keys, values, sems = refs[14 + 2 * tp :]
    span, width, txt = grad_cmix.shape[1], lefts.shape[1], scores.shape[2]
    copy = pltpu.make_async_copy(kvq.at[:, :, :, : 2 * span], weight, sems.at[0])
    copy.start()
    mask = head_mask(span)
    ff = grad_pre.shape[1]
    places, at = [], 0
    for size in (ff, span, span, span, span, span, ff, width, width):
        places.append(slice(at, at + size))
        at += size
    for i in range(tp):
        spread_heads(query_one[i].astype(F32)[:1], i, keys, mask)
        spread_heads(grad_cmix[i : i + 1], i, values, mask)
        both = jnp.concatenate([scores[i], probs[i]], axis=0).astype(BF)
        found = dot(both, text[i][...])
        for kind in range(2):
            begin = (2 * i + kind) * local
            lefts[begin : begin + local] = found[8 * kind : 8 * kind + local]
        sent[i][:, width:] = both
        for k, rows in ((2, query_one), (4, mixed), (5, cross)):
            held[i : i + 1, places[k]] = rows[i].astype(F32)[:1]
    held[:tp, places[0]] = grad_pre[...].astype(F32)[:tp]
    held[:tp, places[1]] = grad_cq[...]
    held[:tp, places[3]] = grad_cmix[...]
    held[:tp, places[6]] = active[...].astype(F32)[:tp]
    held[:tp, places[7]] = base[...]
    held[:tp, places[8]] = grad_mid[...]
    factors[...] = held[:tp].astype(BF)
    begin = 2 * tp * local
    lefts[begin : begin + tp] = cross_one_row[...]
    lefts[begin + tp :] = mlp_one[...]
    copy.wait()
    step = width // tp
    key_spread, value_spread = keys[...].astype(BF), values[...].astype(BF)
    for t in range(tp):
        cols = slice(t * step, (t + 1) * step)
        key_rows = dot_t(key_spread, block(weight, t, slice(0, span))) * HDIM ** (-0.5)
        value_rows = dot_t(value_spread, block(weight, t, slice(span, 2 * span)))
        for i in range(tp):
            eight = slice(8 * i, 8 * i + 8)
            both = jnp.concatenate([key_rows[eight], value_rows[eight]], axis=0)
            sent[i][:, cols] = both.astype(BF)


def self_back_kernel(
    tp, local, base, rows, gain, packed, probs, masked_entries, text_lefts, gathered, *refs,
):
    parts, entries, refs = refs[:tp], refs[tp : 2 * tp], refs[tp:]
    sent = refs[tp : 2 * tp]
    grad_attn, gain_row, payload, factors = refs[2 * tp : 2 * tp + 4]
    weight, held, spreads, lefts, sems = refs[2 * tp + 4 :]
    width = lefts.shape[1]
    span, free = weight.shape[3] // 4, entries[0].shape[0]
    copies = [pltpu.make_async_copy(gathered, weight, sems.at[0])]
    for copy in copies:
        copy.start()
    held[...] = jnp.zeros_like(held)
    for i in range(tp):
        row_back(parts, rows, gain, base, i, held, gain_row)
    grad_attn[...] = held[:tp]
    copies[0].wait()
    mixed = out_back(held[...].astype(BF), weight, slice(3 * span, 4 * span))
    factors[:, :span] = mixed[:tp].astype(BF)
    factors[:, 3 * span :] = grad_attn[...].astype(BF)
    mask = head_mask(span)
    held[...] = jnp.zeros_like(held)
    first = lax.broadcasted_iota(jnp.int32, (PAD, TILE), 1) == 0
    only = first & (lax.broadcasted_iota(jnp.int32, (PAD, TILE), 0) == 0)
    masked_row = masked_entries[:1].astype(F32)
    for i in range(tp):
        spread = jnp.where(mask, mixed[i : i + 1], 0.0)
        spreads[8 * i : 8 * i + 8] = spread
        spread = spread.astype(BF)
        values = packed[i, :, 2 * span :]
        grad_probs, grad_one = dot_t(spread, values[:free]), dot_t(spread, values[free:])[:, :1]
        weighs, one = probs[i, :, :free], probs[i, :, free : free + 1]
        mean = jnp.sum(grad_probs * weighs, axis=-1, keepdims=True) + grad_one * one
        grad = (weighs * (grad_probs - mean)).astype(BF)
        grad_one = (one * (grad_one - mean)).astype(BF).astype(F32)
        keys = packed[i, :, span : 2 * span]
        back = dot(grad, keys[:free]) + grad_one * keys[free : free + 1].astype(F32)
        back = jnp.sum(jnp.where(mask, back, 0.0), axis=0, keepdims=True)
        held[i : i + 1, :span] = back * HDIM ** (-0.5)
        both = jnp.concatenate([grad.astype(F32), weighs], axis=0).astype(BF)
        both_one = jnp.concatenate([grad_one, one], axis=0).astype(BF).astype(F32)
        found = dot(both, entries[i][...]) + both_one * masked_row
        for kind in range(2):
            begin = (2 * i + kind) * local
            lefts[begin : begin + local] = found[8 * kind : 8 * kind + local]
        sent[i][:PAD, width : width + free] = both
        sent[i][:PAD, width + free :] = jnp.where(first, both_one, 0.0).astype(BF)
        sent[i][PAD:, width : width + free] = jnp.zeros((PAD, free), BF)
        sent[i][PAD:, width + free :] = jnp.where(only, 1.0, 0.0).astype(BF)
    lefts[2 * tp * local :] = text_lefts[...]
    own_width = payload.shape[2]
    for d in range(payload.shape[0]):
        payload[d] = lefts[:, d * own_width : (d + 1) * own_width].astype(BF)
    factors[:, span : 2 * span] = held[:tp, :span].astype(BF)
    queries = held[:, :span].astype(BF)
    zero_query = packed[0, free:, :span].astype(F32)[:1]
    factors[:, 2 * span : 3 * span] = jnp.broadcast_to(zero_query, (tp, span)).astype(BF)
    key_spread = jnp.where(mask, zero_query, 0.0).astype(BF)
    value_spread = spreads[...].astype(BF)
    step = width // tp
    empty = jnp.zeros((PAD - 1, step), F32)
    for t in range(tp):
        cols = slice(t * step, (t + 1) * step)
        keys = dot_t(key_spread, block(weight, t, slice(span, 2 * span))) * HDIM ** (-0.5)
        values = dot_t(value_spread, block(weight, t, slice(2 * span, 3 * span)))
        query_rows = dot_t(queries, block(weight, t, slice(0, span)))
        for i in range(tp):
            both = jnp.concatenate([keys, values[8 * i : 8 * i + 8]], axis=0)
            sent[i][:PAD, cols] = both.astype(BF)
            last = jnp.concatenate([query_rows[i : i + 1], empty], axis=0)
            sent[i][PAD:, cols] = last.astype(BF)


def tokens_back_kernel(tp, rows, gain, base, place, gain_c, gain_m, *refs):
    came, came_text, (tokens, text, payload, small) = refs[:tp], refs[tp : 2 * tp], refs[2 * tp :]
    width, free = rows.shape[1], place.shape[1]
    grad, grad_one, grad_text = 0.0, 0.0, 0.0
    for part, text_part in zip(came, came_text):
        back = part[:, :width]
        grad = grad + dot_sum(part[:, width : width + free], back)
        grad_one = grad_one + dot_sum(part[:, width + free :], back)[:1]
        grad_text = grad_text + dot_sum(text_part[:, width:], text_part[:, :width])
    text[...] = grad_text.astype(BF)
    field, scale = normed(rows[:free])
    start = norm_back(grad * gain[...], field, scale)
    tokens[...] = dot(place[...], start.astype(BF)).astype(BF)
    one_field, one_scale = normed(rows[free : free + 1])
    start = norm_back(grad_one * gain[...], one_field, one_scale)
    small[...] = jnp.zeros_like(small)
    small[0:1] = base[0:1] + start
    small[1:2] = jnp.sum(grad * field, axis=0, keepdims=True) + grad_one * one_field
    small[2:3] = gain_c[...]
    small[3:4] = gain_m[...]
    own = payload.shape[2]
    for d in range(payload.shape[0]):
        payload[d] = small[:, d * own : (d + 1) * own]


def stack_kernel(*refs):
    for k, ref in enumerate(refs[:-1]):
        refs[-1][k] = ref[...]


def unpack_kernel(planes, others, right, group, held):
    count, tp = planes.shape[:2]
    for k in range(count):
        held[k * tp : (k + 1) * tp] = planes[k].astype(F32)
        held[(count + k) * tp : (count + k + 1) * tp] = others[k].astype(F32)
    right[...] = held[:, : right.shape[1]].astype(BF)
    group[...] = held[:, right.shape[1] :].astype(BF)


def aligned(right, corner, tp):
    count = right.shape[0]
    out = lax.broadcasted_iota(jnp.int32, (count, count), 0)
    into = lax.broadcasted_iota(jnp.int32, (count, count), 1)
    same = (out // tp == (corner ^ (into // tp))) & (out % tp == into % tp)
    return dot(same.astype(BF), right).astype(BF)


def cross_columns_kernel(local, place, text_left, one_left, *refs):
    right, (grad_kv, grad_cq, grad_up) = refs[:-3], refs[-3:]
    tp, span = len(right), local * HDIM
    ff = right[0].shape[1] - 3 * span
    for j in range(tp):
        at = place[0] ^ j
        rows = aligned(right[j][...], place[1], tp)
        columns = pl.ds(pl.multiple_of(at * span, span), span)
        grad_cq[:, columns] = dot_sum(one_left[at, 0], rows[:, ff : ff + span])
        wide = pl.ds(pl.multiple_of(at * ff, ff), ff)
        grad_up[:, wide] = dot_sum(one_left[at, 1], rows[:, :ff])
        for h in range(local):
            for kind in range(2):
                start = ff + (1 + kind) * span + h * HDIM
                outer = dot_sum(text_left[at, kind, h], rows[:, start : start + HDIM])
                if kind == 0:
                    outer = outer * HDIM ** (-0.5)
                begin = kind * tp * span + at * span + h * HDIM
                grad_kv[:, pl.ds(pl.multiple_of(begin, HDIM), HDIM)] = outer


def self_columns_kernel(local, place, left, entry, *refs):
    right, grad_qkv = refs[:-1], refs[-1]
    tp, span = len(right), local * HDIM
    ones = jnp.ones((right[0].shape[0], HDIM), BF)
    for j in range(tp):
        at = place[0] ^ j
        rows = aligned(right[j][:, :span], place[1], tp)
        total = jnp.sum(right[j][:, span : 2 * span].astype(F32), axis=0, keepdims=True)
        queries = right[j][:, 2 * span :].astype(F32)[:1] * HDIM ** (-0.5)
        grad_qkv[:, pl.ds(pl.multiple_of(at * span, span), span)] = entry[...] * total
        for h in range(local):
            cols = slice(h * HDIM, (h + 1) * HDIM)
            keys = dot_sum(left[at, 0, h], ones) * queries[:, cols]
            begin = tp * span + at * span + h * HDIM
            grad_qkv[:, pl.ds(pl.multiple_of(begin, HDIM), HDIM)] = keys
            begin = 2 * tp * span + at * span + h * HDIM
            values = dot_sum(left[at, 1, h], rows[:, cols])
            grad_qkv[:, pl.ds(pl.multiple_of(begin, HDIM), HDIM)] = values


def whole_spec():
    return pl.BlockSpec(memory_space=pl.ANY)


def in_vmem(kernel, name, operands, out_shape, scratch_shapes=(), held=()):
    spaces = dict(held)
    return pl.pallas_call(
        kernel,
        in_specs=[
            pl.BlockSpec(memory_space=spaces.get(k, pltpu.VMEM)) for k in range(len(operands))
        ],
        out_specs=[pl.BlockSpec(memory_space=pltpu.VMEM)] * len(out_shape),
        out_shape=[jax.ShapeDtypeStruct(shape, dtype) for shape, dtype in out_shape],
        scratch_shapes=scratch_shapes,
        compiler_params=pltpu.CompilerParams(vmem_limit_bytes=VMEM_BYTES),
        name=name,
    )(*operands)


def self_forward(local, count, entries, masked_entries, gathered):
    tp, (free, width) = len(entries), entries[0].shape
    span, rows = local * HDIM, free + PAD
    found = in_vmem(
        functools.partial(self_kernel, tp, local, count),
        "self_attention",
        [*entries, masked_entries, gathered],
        [((rows, width), BF)] * tp
        + [((tp, rows, 3 * span), BF), ((tp, PAD, span), BF), ((tp, 8, free + TILE), F32)],
        [
            pltpu.VMEM(gathered.shape, BF),
            pltpu.VMEM((tp * free + PAD, width), BF),
            pltpu.VMEM((tp * rows, span), BF),
            pltpu.SemaphoreType.DMA((tp + 2,)),
        ],
        [(k, pl.ANY) for k in range(tp + 2)],
    )
    return found[:tp], *found[tp:]


def cross_forward(local, entries, text, bias, gathered):
    tp, (rows, width) = len(entries), entries[0].shape
    txt, span = text[0].shape[0], local * HDIM
    found = in_vmem(
        functools.partial(cross_kernel, tp, local),
        "cross_attention",
        [*entries, *text, bias, gathered],
        [((rows, width), BF)] * tp
        + [
            ((tp, txt, 2 * span), BF),
            ((tp, PAD, span), BF),
            ((tp, PAD, span), BF),
            ((tp, 8, txt), F32),
            ((tp, width), F32),
            ((tp, width), F32),
        ],
        [
            pltpu.VMEM(gathered.shape, BF),
            pltpu.VMEM((tp * rows, width), BF),
            pltpu.VMEM((tp * txt, width), BF),
            pltpu.VMEM((tp * rows, span), BF),
            pltpu.VMEM((tp * rows, span), BF),
            pltpu.SemaphoreType.DMA((2 * tp + 1,)),
        ],
        [(k, pl.ANY) for k in range(2 * tp + 2) if k != 2 * tp],
    )
    return found[:tp], *found[tp:]


def down_kernel(tp, active, weight, *partial):
    rows = partial[0].shape[0]
    part = weight[...]
    added = dot(active[...], part.reshape(-1, part.shape[2])).astype(BF)
    for i in range(tp):
        partial[i][...] = added[i * rows : (i + 1) * rows]


def mlp_down(tp, active, gathered):
    blocks, own, width = gathered.shape
    rows, step = active.shape[0] // tp, 512
    return pl.pallas_call(
        functools.partial(down_kernel, tp),
        grid=(width // step,),
        in_specs=[
            pl.BlockSpec(active.shape, lambda i: (0, 0)),
            pl.BlockSpec((blocks, own, step), lambda i: (0, 0, i)),
        ],
        out_specs=[pl.BlockSpec((rows, step), lambda i: (0, i))] * tp,
        out_shape=[jax.ShapeDtypeStruct((rows, width), BF)] * tp,
        compiler_params=pltpu.CompilerParams(vmem_limit_bytes=VMEM_BYTES),
        name="mlp_down",
    )(active, gathered)


def mlp_up(entries, gathered):
    rows, width = entries.shape
    blocks, tp, own, ff = gathered.shape
    step = min(ff, 512)
    return pl.pallas_call(
        up_kernel,
        grid=(ff // step,),
        in_specs=[
            pl.BlockSpec((rows, width), lambda i: (0, 0)),
            pl.BlockSpec((blocks, tp, own, step), lambda i: (0, 0, 0, i)),
        ],
        out_specs=pl.BlockSpec((rows, step), lambda i: (0, i)),
        out_shape=jax.ShapeDtypeStruct((rows, ff), BF),
        compiler_params=pltpu.CompilerParams(vmem_limit_bytes=VMEM_BYTES),
        name="mlp_up",
    )(entries, gathered)


def mlp_back(entries, grad_active, gathered):
    tp, width = len(entries), entries[0].shape[1]
    ff = gathered.shape[3]
    return in_vmem(
        functools.partial(mlp_back_kernel, tp),
        "mlp_back",
        [*entries, grad_active, gathered],
        [
            ((PAD, ff), BF),
            ((PAD, ff), BF),
            ((tp, width), F32),
            ((tp, width), F32),
            ((tp, width), F32),
        ],
        [
            pltpu.VMEM(gathered.shape, BF),
            pltpu.VMEM((tp, PAD, width), BF),
            pltpu.VMEM((PAD, width), F32),
            pltpu.SemaphoreType.DMA((2 * tp,)),
        ],
        [(k, pl.ANY) for k in range(tp + 2) if k != tp],
    )


def cross_back(base, rows, gain, pair, probs, gathered, parts):
    tp, width = base.shape
    blocks, _, own, columns = gathered.shape
    span = columns // 4
    return in_vmem(
        functools.partial(cross_back_kernel, tp),
        "cross_back",
        [base, rows, gain[None], pair, probs, gathered, *parts],
        [
            ((tp, width), F32),
            ((tp, span), F32),
            (probs.shape, F32),
            ((tp, span), F32),
            ((tp, width), F32),
            ((1, width), F32),
        ],
        [
            pltpu.VMEM((blocks, tp, own, 2 * span), BF),
            pltpu.VMEM((8, width), F32),
            pltpu.SemaphoreType.DMA((1,)),
        ],
        ((5, pl.ANY),),
    )


def text_back(local, scores, probs, query_one, grad_cmix, kvq, rest, text):
    tp, span = grad_cmix.shape
    blocks, _, own, _ = kvq.shape
    (txt, width), ff = text[0].shape, rest[2].shape[1]
    found = in_vmem(
        functools.partial(text_back_kernel, tp, local),
        "text_back",
        [scores, probs, query_one, grad_cmix, kvq, *rest, *text],
        [((PAD, width + txt), BF)] * tp
        + [((2 * tp * (local + 1), width), F32), ((tp, 2 * ff + 5 * span + 2 * width), BF)],
        [
            pltpu.VMEM((blocks, tp, own, 2 * span), BF),
            pltpu.VMEM((8, 2 * ff + 5 * span + 2 * width), F32),
            pltpu.VMEM((8 * tp, span), F32),
            pltpu.VMEM((8 * tp, span), F32),
            pltpu.SemaphoreType.DMA((1,)),
        ],
        ((4, pl.ANY),),
    )
    return found[:tp], *found[tp:]


def self_back(local, world, base, rows, gain, packed, probs, masked_entries, text_lefts, gathered, parts, entries):
    tp, width = base.shape
    _, _, own, columns = gathered.shape
    span, free = columns // 4, entries[0].shape[0]
    count = 2 * tp * (2 * local + 1)
    found = in_vmem(
        functools.partial(self_back_kernel, tp, local),
        "self_back",
        [base, rows, gain[None], packed, probs, masked_entries, text_lefts, gathered, *parts, *entries],
        [((2 * PAD, width + free + TILE), BF)] * tp
        + [
            ((tp, width), F32),
            ((1, width), F32),
            ((world, count, own), BF),
            ((tp, 3 * span + width), BF),
        ],
        [
            pltpu.VMEM(gathered.shape, BF),
            pltpu.VMEM((8, width), F32),
            pltpu.VMEM((8 * tp, span), F32),
            pltpu.VMEM((count, width), F32),
            pltpu.SemaphoreType.DMA((1,)),
        ],
        ((7, pl.ANY),),
    )
    return found[:tp], *found[tp:]


def stacked(pieces):
    shape = (len(pieces),) + pieces[0].shape
    return in_vmem(stack_kernel, "stack", pieces, [(shape, BF)])[0]


def unpack(planes, others, cut):
    count, tp, wide = planes.shape
    rows = 2 * count * tp
    return in_vmem(
        unpack_kernel,
        "unpack",
        [planes, others],
        [((rows, cut), BF), ((rows, wide - cut), BF)],
        [pltpu.VMEM((rows, wide), F32)],
    )


def join_kernel(free, base, gain, *refs):
    parts, (total, entries) = refs[:-2], refs[-2:]
    value = base[...]
    for part in parts:
        value = value + part[...].astype(F32)
    total[...] = value
    found = normed(value)[0] * gain[...]
    entries[...] = found.astype(BF)

    @pl.when(pl.program_id(0) == pl.num_programs(0) - 1)
    def _():
        at = value.shape[0] - PAD
        row = value[at : at + 1]
        spot = lax.broadcasted_iota(jnp.int32, (PAD, value.shape[1]), 0)
        last = found[at:]
        for k in range(3):
            part = row.astype(BF).astype(F32)
            last = jnp.where(spot == k + 1, part, last)
            row = row - part
        entries[at:] = last.astype(BF)


def join(base, parts, gain):
    rows, width = base.shape
    step = PAD * 3 if rows % (PAD * 3) == 0 else PAD
    block = pl.BlockSpec((step, width), lambda i: (i, 0))
    return pl.pallas_call(
        functools.partial(join_kernel, rows - PAD),
        grid=(rows // step,),
        in_specs=[block, pl.BlockSpec((1, width), lambda i: (0, 0))] + [block] * len(parts),
        out_specs=[block, block],
        out_shape=[
            jax.ShapeDtypeStruct((rows, width), F32),
            jax.ShapeDtypeStruct((rows, width), BF),
        ],
        compiler_params=pltpu.CompilerParams(vmem_limit_bytes=VMEM_BYTES),
        name="join",
    )(base, gain[None], *parts)


def shards(
    tp,
    planes,
    tokens,
    text,
    cotangent,
    positions,
    text_lengths,
    mask_embed,
    gain_attn,
    w_qkv,
    w_attn_out,
    gain_cross,
    w_cross_q,
    w_cross_kv,
    w_cross_out,
    gain_mlp,
    w_up,
    w_down,
):
    me = Layer(tp, planes)
    seq, width = tokens.shape
    masked_count = positions.shape[1]
    free = seq - masked_count
    txt = text.shape[1]
    local = HEADS // tp
    rows = free + PAD
    device = (me.t * 2 + me.c) * planes + me.z
    world = tp * 2 * planes
    own = width // world

    def after(value, earlier):
        return lax.optimization_barrier((value, earlier))[0]

    span = local * HDIM

    qkv_sent = me.shuffle([(w_qkv, 3)])
    attn_w = jnp.concatenate([qkv_sent, column_blocks(tp, [(w_attn_out, 1)])], axis=2)
    attn_w = me.gather_blocks(attn_w)

    def natural(value):
        split = value.reshape(value.shape[:-1] + (2 * planes, tp, own))
        return split.swapaxes(-3, -2).reshape(value.shape)

    cot_sum = jnp.sum(cotangent[0].astype(F32), axis=0)
    vectors = jnp.concatenate([mask_embed, gain_attn, gain_cross, gain_mlp]).astype(F32)
    fill = TILE - vectors.shape[0] % TILE
    length = jnp.broadcast_to(text_lengths.astype(F32), (fill,))
    gathered = me.tp_direct(me.gather_cz(jnp.concatenate([cot_sum, vectors, length])))
    others = after((w_cross_kv, w_cross_q, w_cross_out), (gathered, qkv_sent))
    kvq_sent = me.shuffle([(others[0], 2), (others[1], 1)])
    cross_sent = jnp.concatenate([kvq_sent, column_blocks(tp, [(others[2], 1)])], axis=2)
    vectors = gathered[:, :, width : width + 4 * own].reshape(world, 4, own)
    vectors = xor_order(vectors, device, world).transpose(1, 0, 2).reshape(4, width)
    embed, gain_a, gain_c, gain_m = vectors[0], vectors[1], vectors[2], vectors[3]
    lengths = gathered[:, 0, width + 4 * own :][:, :1]
    text_bias = jnp.where(
        lax.broadcasted_iota(jnp.int32, (tp, txt), 1).astype(F32) < lengths, 0.0, -1e30
    )
    cot_group = gathered[:, 0, :width]

    spots = lax.broadcasted_iota(jnp.int32, (masked_count, seq), 1)
    masked = jnp.sum((positions[0][:, None] == spots).astype(F32), axis=0)
    below = lax.broadcasted_iota(jnp.int32, (seq, seq), 0) <= lax.broadcasted_iota(
        jnp.int32, (seq, seq), 1
    )
    rank = dot((1.0 - masked).astype(BF)[None, :], below.astype(BF))[0]
    ranks = lax.broadcasted_iota(jnp.int32, (free, seq), 0).astype(F32) + 1.0
    pick = ((rank[None, :] == ranks) & (masked[None, :] == 0.0)).astype(BF)
    place = jnp.concatenate(
        [pick.T, masked[:, None].astype(BF), jnp.zeros((seq, PAD - 1), BF)], axis=1
    )
    start_free = dot(pick, tokens)
    start = jnp.concatenate([start_free, jnp.broadcast_to(embed[None], (PAD, width))])

    cot_rows = gathered[:, :, :width].reshape(world, width)
    high = cot_rows.astype(BF)
    low = (cot_rows - high.astype(F32)).astype(BF)
    through = dot_t(jnp.concatenate([high, low]), w_down)
    through = through[:world] + through[world:]
    through = through.reshape(tp, 2 * planes, -1).transpose(1, 0, 2)
    through = xor_order(through, me.c * planes + me.z, 2 * planes)
    through = lax.all_to_all(after(through, kvq_sent), ("core", "fsdp"), 0, 0, tiled=True)
    grad_active = through.transpose(1, 0, 2).reshape(tp, -1)

    field_a, scale_a = normed(start)
    entries = (field_a * gain_a[None]).astype(BF)
    entries_all = me.spread(entries[:free])
    text_rows = me.spread(after(text[0], entries_all))
    up_sent = me.shuffle([(after(w_up, (entries_all, kvq_sent)), 1)])
    cross_w = me.gather_blocks(after(cross_sent, (attn_w, entries_all, up_sent)))
    partial, packed, mixed_one, probs_one = self_forward(
        local, masked_count, entries_all, entries[free:], attn_w
    )
    after_attn, cross_entries = join(after(start, (grad_active, place)), me.collect(after(tuple(partial), text_rows)), gain_c)

    cross_all = me.spread(cross_entries)
    up = me.gather_blocks(after(up_sent, (cross_w, cross_all)))
    partial, pair, query_one, cross_one, cross_probs_one, cross_entry, attn_stream = cross_forward(
        local, cross_all, text_rows, text_bias, cross_w
    )
    after_cross, mlp_entries = join(after_attn, me.collect(partial), gain_m)

    mlp_all = me.spread(mlp_entries)
    down = me.gather_blocks(after(w_down, (up, mlp_all)))

    active_one, grad_pre, grad_entry, mlp_one, cross_stream = mlp_back(
        mlp_all, jnp.pad(grad_active, ((0, PAD - tp), (0, 0))), up
    )
    grad_mid, grad_cmix, scores, grad_cq, grad_entry, grad_gain_m = cross_back(
        cot_group, cross_stream, gain_m, pair, cross_probs_one, cross_w, me.tp_parts(grad_entry)
    )
    text_sent, text_lefts, early_factors = text_back(
        local,
        scores,
        cross_probs_one,
        query_one,
        grad_cmix,
        cross_w,
        [
            cross_entry,
            mlp_one,
            grad_pre,
            grad_cq,
            mixed_one,
            cross_one,
            active_one,
            cot_group,
            grad_mid,
        ],
        text_rows,
    )
    sent, grad_attn, grad_gain_c, payload, late_factors = self_back(
        local,
        world,
        grad_mid,
        attn_stream,
        gain_c,
        packed,
        probs_one,
        entries[free:],
        text_lefts,
        attn_w,
        me.tp_parts(grad_entry),
        entries_all,
    )
    came = me.to_owner(sent)
    came_text = me.to_owner(text_sent)

    corner = me.c * planes + me.z
    ff = grad_pre.shape[1]

    def gather_factors(factors, cut):
        planes_of = stacked([factors] + [me.other_plane(factors, k) for k in range(1, planes)])
        right, group = unpack(planes_of, me.other_core(planes_of), cut)
        return [right] + [me.hop(right, j) for j in range(1, tp)], group

    def mine(stack):
        size = stack.shape[1] // (2 * planes)
        return lax.dynamic_slice_in_dim(stack, corner * size, size, axis=1)

    early_right, group = gather_factors(early_factors, ff + 3 * span)
    cuts = [span, 2 * span, 2 * span + ff, 2 * span + ff + width]
    mixed_f, cross_f, active_f, cot_f, mid_f = jnp.split(group, cuts, axis=1)
    grad_w_cout = dot_sum(mine(cross_f), mid_f)
    grad_w_down = dot_sum(mine(active_f), cot_f)

    late_right, attn_f = gather_factors(late_factors, 3 * span)
    lefts = me.to_rows(payload)

    active = mlp_up(jnp.concatenate(after(tuple(mlp_all), grad_attn)), up)
    partial = mlp_down(tp, after(active, (early_right, late_right, lefts)), down)
    output = sum(part.astype(F32) for part in me.collect(partial))
    output = dot(place, (after_cross + output).astype(BF)).astype(BF)

    grad_tokens, grad_text, small = in_vmem(
        functools.partial(tokens_back_kernel, tp),
        "tokens_back",
        [start, gain_a[None], grad_attn, pick.T, grad_gain_c, grad_gain_m, *after(tuple(came), partial), *came_text],
        [((seq, width), BF), ((txt, width), BF), ((world, 8, own), F32)],
        [pltpu.VMEM((8, width), F32)],
    )
    small = jnp.sum(me.to_rows(small), axis=0)

    heads = 2 * tp * local
    lefts = after(lefts, partial)
    attn_left, text_left = (
        lefts[:, k * heads : (k + 1) * heads]
        .reshape(tp, 2 * planes, tp, 2, local, own)
        .transpose(0, 3, 4, 1, 2, 5)
        .reshape(tp, 2, local, world, own)
        for k in range(2)
    )
    one_left = lefts[:, 2 * heads :].reshape(tp, 2 * planes, 2, tp, own)
    one_left = one_left.transpose(0, 2, 1, 3, 4).reshape(tp, 2, world, own)
    place_at = jnp.stack([me.t, corner]).astype(jnp.int32)
    held = ((0, pltpu.SMEM),)
    grad_w_kv, grad_w_cq, grad_w_up = in_vmem(
        functools.partial(cross_columns_kernel, local),
        "cross_columns",
        [place_at, text_left, one_left, *early_right],
        [((own, 2 * width), F32), ((own, width), F32), ((own, tp * ff), F32)],
        held=held,
    )
    entry_own = lax.dynamic_slice_in_dim(entries[free], device * own, own).astype(F32)
    (grad_w_qkv,) = in_vmem(
        functools.partial(self_columns_kernel, local),
        "self_columns",
        [place_at, attn_left, entry_own[:, None], *late_right],
        [((own, 3 * width), F32)],
        held=held,
    )
    grad_w_out = dot_sum(mine(mixed_f), attn_f)
    return (
        output,
        grad_tokens,
        grad_text[None],
        small[0],
        small[1],
        grad_w_qkv,
        grad_w_out,
        small[2],
        grad_w_cq,
        grad_w_kv,
        grad_w_cout,
        small[3],
        grad_w_up,
        grad_w_down,
    )


def solution(mesh):
    tp, planes = mesh.shape["dp"] // 2, mesh.shape["fsdp"]
    fine = Mesh(mesh.devices.reshape(tp, 2, planes), ("tp", "core", "fsdp"))
    every = ("tp", "core", "fsdp")
    one, two, three = P(every), P(every, None), P(every, None, None)

    def layer(*arguments):
        return shards(tp, planes, *arguments)

    return jax.shard_map(
        layer,
        mesh=fine,
        in_specs=(two, three, three, two, one, one, one, two, two, one, two, two, two, one, two, two),
        out_specs=(two, two, three, one, one, two, two, one, two, two, two, one, two, two),
        check_vma=False,
    )
```

profile of v0, /device:TPU:0, one launch (start us, length us, event | category | flops | bytes accessed | tf_op | source)
XLA Modules:
  0.0 443.9 jit_solution(8438328805338919714)
XLA Ops:
  7.2 2.2 column_blocks.5
  9.3 5.2 %all-to-all-start = ((bf16[4,64,1536]{2,1,0:T(8,128)(2,1)}), bf16[4,64,1536]{2,1,0:T(8,128)(2,1)S(1)}, u32[]{:S(2)}, u32[]{:S(2)}) async-start(bf16[4,64,1536]{2,1,0:T(8,128)(2,1)} %column_blocks.5), calls=%async_computation | async-start | bytes 1572864 | tf_op jit(solution)/shard_map/all_to_all | solution.py:98
  14.5 1.7 column_blocks.7
  16.2 9.1 %all-to-all-done = bf16[4,64,1536]{2,1,0:T(8,128)(2,1)S(1)} async-done(((bf16[4,64,1536]{2,1,0:T(8,128)(2,1)}), bf16[4,64,1536]{2,1,0:T(8,128)(2,1)S(1)}, u32[]{:S(2)}, u32[]{:S(2)}) %all-to-all-start) | async-done | bytes 786464 | tf_op jit(solution)/shard_map/all_to_all | solution.py:98
  25.3 2.1 pad_maximum_fusion.2
  28.3 1.7 collective-permute-start
  30.0 2.6 collective-permute-start.1
  34.6 3.5 collective-permute-done.2
  43.5 3.0 collective-permute-done.5
  50.1 2.0 column_blocks.6
  52.2 3.5 all-to-all-start.1
  57.0 2.0 collective-permute-start.7
  60.6 18.5 %collective-permute-done.7.refs_1_.refs_5_ = bf16[128,2048]{1,0:T(8,128)(2,1)S(1)} collective-permute-done((bf16[128,2048]{1,0:T(8,128)(2,1)S(1)}, bf16[128,2048]{1,0:T(8,128)(2,1)S(1)}, u32[]{:S(2)}, u32[]{:S(2)}) %collective-permute-start.7) | collective-permute-done | bytes 524320 | tf_op jit(solution)/shard_map/ppermute | solution.py:66
  79.1 11.1 %collective-permute-done.9.refs_3_.refs_7_ = bf16[128,2048]{1,0:T(8,128)(2,1)S(1)} collective-permute-done((bf16[128,2048]{1,0:T(8,128)(2,1)S(1)}, bf16[128,2048]{1,0:T(8,128)(2,1)S(1)}, u32[]{:S(2)}, u32[]{:S(2)}) %collective-permute-start.9) | collective-permute-done | bytes 524320 | tf_op jit(solution)/shard_map/ppermute | solution.py:66
  90.2 2.5 column_blocks.9
  92.7 3.5 all-to-all-start.3
  96.4 1.7 column_blocks.8
  98.1 2.1 pad_maximum_fusion.3
  100.2 9.3 %all-to-all-done.3 = bf16[4,64,2048]{2,1,0:T(8,128)(2,1)S(1)} async-done(((bf16[4,64,2048]{2,1,0:T(8,128)(2,1)}), bf16[4,64,2048]{2,1,0:T(8,128)(2,1)S(1)}, u32[]{:S(2)}, u32[]{:S(2)}) %all-to-all-start.3) | async-done | bytes 1048608 | tf_op jit(solution)/shard_map/all_to_all | solution.py:98
  117.4 18.1 %self_attention.1 = (bf16[144,2048]{1,0:T(8,128)(2,1)}, bf16[144,2048]{1,0:T(8,128)(2,1)}, bf16[144,2048]{1,0:T(8,128)(2,1)}, bf16[144,2048]{1,0:T(8,128)(2,1)},...) custom-call(bf16[128,2048]{1,0:T(8,128)(2,1)} %copy-done.2, ...), custom_call_target="tpu_custom_call" | custom-call | tf_op jit(solution)/shard_map/self_attention/pallas_call | solution.py:574
  135.5 4.9 %collective-permute-done.11.refs_6_.refs_16_ = bf16[128,2048]{1,0:T(8,128)(2,1)S(1)} collective-permute-done((bf16[128,2048]{1,0:T(8,128)(2,1)S(1)}, bf16[128,2048]{1,0:T(8,128)(2,1)S(1)}, u32[]{:S(2)}, u32[]{:S(2)}) %collective-permute-start.11) | collective-permute-done | bytes 524320 | tf_op jit(solution)/shard_map/ppermute | solution.py:66
  144.6 3.3 all-to-all-start.2
  150.9 4.7 %all-to-all-done.2 = f32[8,4,256]{2,1,0:T(4,128)S(1)} async-done(((f32[8,4,256]{2,1,0:T(4,128)}), f32[8,4,256]{2,1,0:T(4,128)S(1)}, u32[]{:S(2)}, u32[]{:S(2)}) %all-to-all-start.2) | async-done | bytes 32800 | tf_op jit(solution)/shard_map/all_to_all | solution.py:917
  156.9 12.0 %collective-permute-done.14.refs_2_ = bf16[144,2048]{1,0:T(8,128)(2,1)S(1)} collective-permute-done((bf16[144,2048]{1,0:T(8,128)(2,1)}, bf16[144,2048]{1,0:T(8,128)(2,1)S(1)}, u32[]{:S(2)}, u32[]{:S(2)}) %collective-permute-start.14) | collective-permute-done | bytes 589856 | tf_op jit(solution)/shard_map/ppermute | solution.py:66
  169.7 4.5 %join.2 = (f32[144,2048]{1,0:T(8,128)}, bf16[144,2048]{1,0:T(8,128)(2,1)}) custom-call(f32[144,2048]{1,0:T(8,128)} %get-tuple-element.101.base.rows, f32[1,2048]{1,0:T(1,128)} %slice.144.gain, bf16[144,2048]{1,0:T(8,128)(2,1)} %get-tuple-element.107.refs_0_, bf16[144,2048]{1,0:T(8,128)(2,1)} %copy-done.23, bf16[144,2048]{1,0:T(8,128)(2,1)} %copy-done.24, ...), custom_call_target="tpu_custom_call" | custom-call | tf_op jit(solution)/shard_map/join/pallas_call | solution.py:821
  177.8 13.0 %collective-permute-done.16.refs_1_ = bf16[144,2048]{1,0:T(8,128)(2,1)S(1)} collective-permute-done((bf16[144,2048]{1,0:T(8,128)(2,1)}, bf16[144,2048]{1,0:T(8,128)(2,1)S(1)}, u32[]{:S(2)}, u32[]{:S(2)}) %collective-permute-start.16) | collective-permute-done | bytes 589856 | tf_op jit(solution)/shard_map/ppermute | solution.py:66
  190.8 9.3 %collective-permute-done.17.refs_2_ = bf16[144,2048]{1,0:T(8,128)(2,1)S(1)} collective-permute-done((bf16[144,2048]{1,0:T(8,128)(2,1)}, bf16[144,2048]{1,0:T(8,128)(2,1)S(1)}, u32[]{:S(2)}, u32[]{:S(2)}) %collective-permute-start.17) | collective-permute-done | bytes 589856 | tf_op jit(solution)/shard_map/ppermute | solution.py:66
  201.9 14.6 %cross_attention.1 = (bf16[144,2048]{1,0:T(8,128)(2,1)}, bf16[144,2048]{1,0:T(8,128)(2,1)}, bf16[144,2048]{1,0:T(8,128)(2,1)}, bf16[144,2048]{1,0:T(8,128)(2,1)}...) custom-call(bf16[144,2048]{1,0:T(8,128)(2,1)} %get-tuple-element.112, ...), custom_call_target="tpu_custom_call" | custom-call | tf_op jit(solution)/shard_map/cross_attention/pallas_call | solution.py:574
  218.2 1.8 collective-permute-start.21
  220.7 12.3 %collective-permute-done.19.refs_1_ = bf16[144,2048]{1,0:T(8,128)(2,1)S(1)} collective-permute-done((bf16[144,2048]{1,0:T(8,128)(2,1)}, bf16[144,2048]{1,0:T(8,128)(2,1)S(1)}, u32[]{:S(2)}, u32[]{:S(2)}) %collective-permute-start.19) | collective-permute-done | bytes 589856 | tf_op jit(solution)/shard_map/ppermute | solution.py:66
  233.0 8.4 %collective-permute-done.20.refs_2_ = bf16[144,2048]{1,0:T(8,128)(2,1)S(1)} collective-permute-done((bf16[144,2048]{1,0:T(8,128)(2,1)}, bf16[144,2048]{1,0:T(8,128)(2,1)S(1)}, u32[]{:S(2)}, u32[]{:S(2)}) %collective-permute-start.20) | collective-permute-done | bytes 589856 | tf_op jit(solution)/shard_map/ppermute | solution.py:66
  242.4 4.5 %join.3 = (f32[144,2048]{1,0:T(8,128)}, bf16[144,2048]{1,0:T(8,128)(2,1)}) custom-call(f32[144,2048]{1,0:T(8,128)} %get-tuple-element.111.base, f32[1,2048]{1,0:T(1,128)} %slice.149.gain, bf16[144,2048]{1,0:T(8,128)(2,1)} %get-tuple-element.116.refs_0_, bf16[144,2048]{1,0:T(8,128)(2,1)} %copy-done.25, bf16[144,2048]{1,0:T(8,128)(2,1)} %copy-done.26, ...), custom_call_target="tpu_custom_call" | custom-call | tf_op jit(solution)/shard_map/join/pallas_call | solution.py:821
  248.5 1.9 collective-permute-start.24
  250.5 11.7 %collective-permute-done.22.refs_1_ = bf16[144,2048]{1,0:T(8,128)(2,1)S(1)} collective-permute-done((bf16[144,2048]{1,0:T(8,128)(2,1)}, bf16[144,2048]{1,0:T(8,128)(2,1)S(1)}, u32[]{:S(2)}, u32[]{:S(2)}) %collective-permute-start.22) | collective-permute-done | bytes 589856 | tf_op jit(solution)/shard_map/ppermute | solution.py:66
  262.1 7.6 %collective-permute-done.23.refs_2_ = bf16[144,2048]{1,0:T(8,128)(2,1)S(1)} collective-permute-done((bf16[144,2048]{1,0:T(8,128)(2,1)}, bf16[144,2048]{1,0:T(8,128)(2,1)S(1)}, u32[]{:S(2)}, u32[]{:S(2)}) %collective-permute-start.23) | collective-permute-done | bytes 589856 | tf_op jit(solution)/shard_map/ppermute | solution.py:66
  269.7 10.5 %all-gather.13.cloned.1.call-done = bf16[32,64,2048]{2,1,0:T(8,128)(2,1)} async-done(((bf16[4,64,2048]{2,1,0:T(8,128)(2,1)}), bf16[32,64,2048]{2,1,0:T(8,128)(2,1)}) %all-gather.13.cloned.1.call-update) | async-done | bytes 8388624 | tf_op jit(solution)/shard_map/all_gather | solution.py:101
  280.9 7.8 %mlp_back.1 = (bf16[16,2048]{1,0:T(8,128)(2,1)}, bf16[16,2048]{1,0:T(8,128)(2,1)}, f32[4,2048]{1,0:T(4,128)}, f32[4,2048]{1,0:T(4,128)}, f32[4,2048]{1,0:T(4,128)}) custom-call(bf16[144,2048]{1,0:T(8,128)(2,1)} %get-tuple-element.144.refs_0_, bf16[144,2048]{1,0:T(8,128)(2,1)} %copy-done.6, bf16[144,2048]{1,0:T(8,128)(2,1)} %copy-done.8, ...), custom_call_target="tpu_custom_call" | custom-call | tf_op jit(solution)/shard_map/mlp_back/pallas_call | solution.py:574
  294.3 2.4 collective-permute-done.27.refs_3_
  297.3 6.6 %cross_back.1 = (f32[4,2048]{1,0:T(4,128)}, f32[4,512]{1,0:T(4,128)}, f32[4,8,128]{2,1,0:T(8,128)}, f32[4,512]{1,0:T(4,128)}, f32[4,2048]{1,0:T(4,128)}, /*index=5*/f32[1,2048]{1,0:T(1,128)}) custom-call(f32[4,2048]{1,0:T(4,128)} %slice_bitcast_fusion.base.refs_12_, f32[4,2048]{1,0:T(4,128)} %get-tuple-element.123.rows, f32[1,2048]{1,0:T(1,128)} %slice.149.gain, ...), custom_call_target="tpu_custom_call" | custom-call | tf_op jit(solution)/shard_map/cross_back/pallas_call | solution.py:574
  305.0 2.5 collective-permute-start.30
  307.5 6.1 %text_back.1 = (bf16[16,2176]{1,0:T(8,128)(2,1)}, bf16[16,2176]{1,0:T(8,128)(2,1)}, bf16[16,2176]{1,0:T(8,128)(2,1)}, bf16[16,2176]{1,0:T(8,128)(2,1)}, f32[40,2048]{1,0:T(8,128)}, /*index=5*/bf16[4,10752]{1,0:T(4,128)(2,1)}) custom-call(f32[4,8,128]{2,1,0:T(8,128)} %get-tuple-element.131.refs_0_, f32[4,8,128]{2,1,0:T(8,128)} %get-tuple-element.125.probs.refs_1_, ...), custom_call_target="tpu_custom_call" | custom-call | tf_op jit(solution)/shard_map/text_back/pallas_call | solution.py:574
  315.2 2.9 collective-permute-start.33
  319.3 10.8 %self_back.1 = (bf16[32,2304]{1,0:T(8,128)(2,1)}, bf16[32,2304]{1,0:T(8,128)(2,1)}, bf16[32,2304]{1,0:T(8,128)(2,1)}, bf16[32,2304]{1,0:T(8,128)(2,1)}, f32[4,20...) custom-call(f32[4,2048]{1,0:T(4,128)} %get-tuple-element.127.refs_13_.base, ...), custom_call_target="tpu_custom_call" | custom-call | tf_op jit(solution)/shard_map/self_back/pallas_call | solution.py:574
  331.7 2.9 collective-permute-start.40
  335.9 1.8 stack.54.planes
  343.9 9.9 %mlp_up.1.active = bf16[576,2048]{1,0:T(8,128)(2,1)} custom-call(bf16[576,2048]{1,0:T(8,128)(2,1)} %pad_maximum_fusion.entries, bf16[8,4,64,2048]{3,2,1,0:T(8,128)(2,1)} %bitcast.122), custom_call_target="tpu_custom_call" | custom-call | tf_op jit(solution)/shard_map/mlp_up/pallas_call | solution.py:665
  354.9 4.2 all-to-all-start.4
  359.7 1.7 unpack.3
  361.4 1.9 collective-permute-start.42
  365.7 2.1 unpack.2
  367.8 1.9 collective-permute-start.35
  372.1 2.8 fusion.6
  378.5 1.7 collective-permute-start.50
  381.5 2.0 fusion.8
  383.6 7.7 %collective-permute-done.37.refs_3_ = bf16[32,3584]{1,0:T(8,128)(2,1)S(1)} collective-permute-done((bf16[32,3584]{1,0:T(8,128)(2,1)S(1)}, bf16[32,3584]{1,0:T(8,128)(2,1)S(1)}, u32[]{:S(2)}, u32[]{:S(2)}) %collective-permute-start.37) | collective-permute-done | bytes 229408 | tf_op jit(solution)/shard_map/ppermute | solution.py:66
  392.1 9.1 %mlp_down.1 = (bf16[144,2048]{1,0:T(8,128)(2,1)}, bf16[144,2048]{1,0:T(8,128)(2,1)}, bf16[144,2048]{1,0:T(8,128)(2,1)}, bf16[144,2048]{1,0:T(8,128)(2,1)}) custom-call(bf16[576,2048]{1,0:T(8,128)(2,1)} %mlp_up.1.active, bf16[8,256,2048]{2,1,0:T(8,128)(2,1)} %bitcast.123), custom_call_target="tpu_custom_call" | custom-call | tf_op jit(solution)/shard_map/mlp_down/pallas_call | solution.py:647
  401.3 1.7 collective-permute-start.53
  408.3 5.0 %tokens_back.1 = (bf16[256,2048]{1,0:T(8,128)(2,1)}, bf16[128,2048]{1,0:T(8,128)(2,1)}, f32[32,8,64]{2,1,0:T(8,128)}) custom-call(f32[144,2048]{1,0:T(8,128)} %get-tuple-element.101.base.rows, f32[1,2048]{1,0:T(1,128)} %slice.153.gain, f32[4,2048]{1,0:T(4,128)} %get-tuple-element.143.base, bf16[256,128]{1,0:T(8,128)(2,1)} %copy-done.29, ...), custom_call_target="tpu_custom_call" | custom-call | tf_op jit(solution)/shard_map/tokens_back/pallas_call | solution.py:574
  413.3 1.7 reshape.285
  414.9 4.1 all-to-all-start.5
  422.4 3.1 self_columns.1
  425.5 4.5 %cross_columns.1 = (f32[64,4096]{1,0:T(8,128)}, f32[64,2048]{1,0:T(8,128)}, f32[64,8192]{1,0:T(8,128)}) custom-call(s32[2]{0:T(128)} %pad_add_fusion.place, bf16[4,2,4,32,64]{4,3,2,1,0:T(8,128)(2,1)} %bitcast.136, bf16[4,2,32,64]{3,2,1,0:T(8,128)(2,1)} %bitcast.148, bf16[32,3584]{1,0:T(8,128)(2,1)} %get-tuple-element.149.refs_0_, ...), custom_call_target="tpu_custom_call" | custom-call | tf_op jit(solution)/shard_map/cross_columns/pallas_call | solution.py:574
  429.9 2.1 all-to-all-done.5
  434.0 2.9 convolution_convert_fusion
  (359 shorter events, 84.0 us)
Async XLA Ops:
  9.3 16.0 %all-to-all-start = ((bf16[4,64,1536]{2,1,0:T(8,128)(2,1)}), bf16[4,64,1536]{2,1,0:T(8,128)(2,1)S(1)}, u32[]{:S(2)}, u32[]{:S(2)}) async-start(bf16[4,64,1536]{2,1,0:T(8,128)(2,1)} %column_blocks.5), calls=%async_computation | async-start | bytes 1572864 | tf_op jit(solution)/shard_map/all_to_all | solution.py:98
  14.5 95.4 %all-gather.9.cloned.1.call-start = ((), (), s32[]{:S(2)}) async-start(), calls=%async_computation.6 | async-start | bytes 9437184 | tf_op jit(solution)/shard_map/all_gather | solution.py:101
  28.3 4.8 %collective-permute-start = (f32[2432]{0:T(1024)S(1)}, f32[2432]{0:T(1024)S(1)}, u32[]{:S(2)}, u32[]{:S(2)}) collective-permute-start(f32[2432]{0:T(1024)S(1)} %pad_maximum_fusion.14), channel_id=1, source_target_pairs={{0,1},{1,0},{2,3},{3,2},{4,5},{5,4},{6,7},{7,6},{8,9},{9,8},{10,11... | collective-permute-start | bytes 29192 | tf_op jit(solution)/shard_map/ppermute | solution.py:72
  30.0 4.6 %collective-permute-start.1 = (f32[2432]{0:T(1024)S(1)}, f32[2432]{0:T(1024)S(1)}, u32[]{:S(2)}, u32[]{:S(2)}) collective-permute-start(f32[2432]{0:T(1024)S(1)} %pad_maximum_fusion.14), channel_id=1, source_target_pairs={{0,2},{1,3},{2,0},{3,1},{4,6},{5,7},{6,4},{7,5},{8,10},{9,11},{10,... | collective-permute-start | bytes 29192 | tf_op jit(solution)/shard_map/ppermute | solution.py:72
  32.6 5.5 %collective-permute-start.2 = (f32[2432]{0:T(1024)S(1)}, f32[2432]{0:T(1024)S(1)}, u32[]{:S(2)}, u32[]{:S(2)}) collective-permute-start(f32[2432]{0:T(1024)S(1)} %pad_maximum_fusion.14), channel_id=1, source_target_pairs={{0,3},{1,2},{2,1},{3,0},{4,7},{5,6},{6,5},{7,4},{8,11},{9,10},{10,... | collective-permute-start | bytes 29192 | tf_op jit(solution)/shard_map/ppermute | solution.py:72
  38.1 1.3 collective-permute-start.3
  39.5 7.4 %collective-permute-start.6 = (f32[8,2432]{1,0:T(8,128)S(1)}, f32[8,2432]{1,0:T(8,128)S(1)}, u32[]{:S(2)}, u32[]{:S(2)}) collective-permute-start(f32[8,2432]{1,0:T(8,128)S(1)} %concatenate.111), channel_id=1, source_target_pairs={{0,24},{8,16},{16,8},{24,0},{1,25},{9,17},{17,9},{25,1},{2,26},{10... | collective-permute-start | bytes 233480 | tf_op jit(solution)/shard_map/ppermute | solution.py:66
  41.0 5.5 %collective-permute-start.5 = (f32[8,2432]{1,0:T(8,128)S(1)}, f32[8,2432]{1,0:T(8,128)S(1)}, u32[]{:S(2)}, u32[]{:S(2)}) collective-permute-start(f32[8,2432]{1,0:T(8,128)S(1)} %concatenate.111), channel_id=1, source_target_pairs={{0,16},{8,24},{16,0},{24,8},{1,17},{9,25},{17,1},{25,9},{2,18},{10... | collective-permute-start | bytes 233480 | tf_op jit(solution)/shard_map/ppermute | solution.py:66
  42.4 4.4 collective-permute-start.4
  52.2 38.1 %all-to-all-start.1 = ((bf16[4,64,1536]{2,1,0:T(8,128)(2,1)}), bf16[4,64,1536]{2,1,0:T(8,128)(2,1)S(1)}, u32[]{:S(2)}, u32[]{:S(2)}) async-start(bf16[4,64,1536]{2,1,0:T(8,128)(2,1)} %column_blocks.6), calls=%async_computation.1 | async-start | bytes 1572864 | tf_op jit(solution)/shard_map/all_to_all | solution.py:98
  57.0 22.1 %collective-permute-start.7 = (bf16[128,2048]{1,0:T(8,128)(2,1)S(1)}, bf16[128,2048]{1,0:T(8,128)(2,1)S(1)}, u32[]{:S(2)}, u32[]{:S(2)}) collective-permute-start(bf16[128,2048]{1,0:T(8,128)(2,1)S(1)} %slice.185.refs_0_.refs_4_), channel_id=1, source_target_pairs={{0,8},{8,0},{16,24},{24,16},{1,9},{9,1},{17,25},{25,17},{2,10},{10... | collective-permute-start | bytes 1572872 | tf_op jit(solution)/shard_map/ppermute | solution.py:66
  59.0 20.1 %collective-permute-start.8 = (bf16[128,2048]{1,0:T(8,128)(2,1)S(1)}, bf16[128,2048]{1,0:T(8,128)(2,1)S(1)}, u32[]{:S(2)}, u32[]{:S(2)}) collective-permute-start(bf16[128,2048]{1,0:T(8,128)(2,1)S(1)} %slice.185.refs_0_.refs_4_), channel_id=1, source_target_pairs={{0,16},{8,24},{16,0},{24,8},{1,17},{9,25},{17,1},{25,9},{2,18},{10... | collective-permute-start | bytes 1572872 | tf_op jit(solution)/shard_map/ppermute | solution.py:66
  60.5 29.7 %collective-permute-start.9 = (bf16[128,2048]{1,0:T(8,128)(2,1)S(1)}, bf16[128,2048]{1,0:T(8,128)(2,1)S(1)}, u32[]{:S(2)}, u32[]{:S(2)}) collective-permute-start(bf16[128,2048]{1,0:T(8,128)(2,1)S(1)} %slice.185.refs_0_.refs_4_), channel_id=1, source_target_pairs={{0,24},{8,16},{16,8},{24,0},{1,25},{9,17},{17,9},{25,1},{2,26},{10... | collective-permute-start | bytes 1572872 | tf_op jit(solution)/shard_map/ppermute | solution.py:66
  92.7 16.8 %all-to-all-start.3 = ((bf16[4,64,2048]{2,1,0:T(8,128)(2,1)}), bf16[4,64,2048]{2,1,0:T(8,128)(2,1)S(1)}, u32[]{:S(2)}, u32[]{:S(2)}) async-start(bf16[4,64,2048]{2,1,0:T(8,128)(2,1)} %column_blocks.9), calls=%async_computation.3 | async-start | bytes 2097152 | tf_op jit(solution)/shard_map/all_to_all | solution.py:98
  96.2 103.9 %all-gather.11.cloned.1.call-start = ((), (), s32[]{:S(2)}) async-start(), calls=%async_computation.7 | async-start | bytes 9437184 | tf_op jit(solution)/shard_map/all_gather | solution.py:101
  113.8 21.7 %collective-permute-start.10 = (bf16[128,2048]{1,0:T(8,128)(2,1)S(1)}, bf16[128,2048]{1,0:T(8,128)(2,1)S(1)}, u32[]{:S(2)}, u32[]{:S(2)}) collective-permute-start(bf16[128,2048]{1,0:T(8,128)(2,1)S(1)} %bitcast.126), channel_id=1, source_target_pairs={{0,8},{8,0},{16,24},{24,16},{1,9},{9,1},{17,25},{25,17},{2,10},{10... | collective-permute-start | bytes 1572872 | tf_op jit(solution)/shard_map/ppermute | solution.py:66
  115.3 25.0 %collective-permute-start.11 = (bf16[128,2048]{1,0:T(8,128)(2,1)S(1)}, bf16[128,2048]{1,0:T(8,128)(2,1)S(1)}, u32[]{:S(2)}, u32[]{:S(2)}) collective-permute-start(bf16[128,2048]{1,0:T(8,128)(2,1)S(1)} %bitcast.127), channel_id=1, source_target_pairs={{0,16},{8,24},{16,0},{24,8},{1,17},{9,25},{17,1},{25,9},{2,18},{10... | collective-permute-start | bytes 1572872 | tf_op jit(solution)/shard_map/ppermute | solution.py:66
  116.8 23.6 %collective-permute-start.12 = (bf16[128,2048]{1,0:T(8,128)(2,1)S(1)}, bf16[128,2048]{1,0:T(8,128)(2,1)S(1)}, u32[]{:S(2)}, u32[]{:S(2)}) collective-permute-start(bf16[128,2048]{1,0:T(8,128)(2,1)S(1)} %bitcast.128), channel_id=1, source_target_pairs={{0,24},{8,16},{16,8},{24,0},{1,25},{9,17},{17,9},{25,1},{2,26},{10... | collective-permute-start | bytes 1572872 | tf_op jit(solution)/shard_map/ppermute | solution.py:66
  140.4 16.5 %collective-permute-start.13 = (bf16[144,2048]{1,0:T(8,128)(2,1)}, bf16[144,2048]{1,0:T(8,128)(2,1)S(1)}, u32[]{:S(2)}, u32[]{:S(2)}) collective-permute-start(bf16[144,2048]{1,0:T(8,128)(2,1)} %get-tuple-element.108), channel_id=1, source_target_pairs={{0,8},{8,0},{16,24},{24,16},{1,9},{9,1},{17,25},{25,17},{2,10},{10... | collective-permute-start | bytes 1769480 | tf_op jit(solution)/shard_map/ppermute | solution.py:66
  141.6 27.3 %collective-permute-start.14 = (bf16[144,2048]{1,0:T(8,128)(2,1)}, bf16[144,2048]{1,0:T(8,128)(2,1)S(1)}, u32[]{:S(2)}, u32[]{:S(2)}) collective-permute-start(bf16[144,2048]{1,0:T(8,128)(2,1)} %get-tuple-element.109), channel_id=1, source_target_pairs={{0,16},{8,24},{16,0},{24,8},{1,17},{9,25},{17,1},{25,9},{2,18},{10... | collective-permute-start | bytes 1769480 | tf_op jit(solution)/shard_map/ppermute | solution.py:66
  142.5 26.4 %collective-permute-start.15 = (bf16[144,2048]{1,0:T(8,128)(2,1)}, bf16[144,2048]{1,0:T(8,128)(2,1)}, u32[]{:S(2)}, u32[]{:S(2)}) collective-permute-start(bf16[144,2048]{1,0:T(8,128)(2,1)} %get-tuple-element.110), channel_id=1, source_target_pairs={{0,24},{8,16},{16,8},{24,0},{1,25},{9,17},{17,9},{25,1},{2,26},{10... | collective-permute-start | bytes 1769480 | tf_op jit(solution)/shard_map/ppermute | solution.py:66
  144.6 11.1 %all-to-all-start.2 = ((f32[8,4,256]{2,1,0:T(4,128)}), f32[8,4,256]{2,1,0:T(4,128)S(1)}, u32[]{:S(2)}, u32[]{:S(2)}) async-start(f32[8,4,256]{2,1,0:T(4,128)} %fusion.23), calls=%async_computation.2 | async-start | bytes 65536 | tf_op jit(solution)/shard_map/all_to_all | solution.py:917
  147.9 132.2 %all-gather.13.cloned.1.call-start = ((), (), s32[]{:S(2)}) async-start(), calls=%async_computation.8 | async-start | bytes 9437184 | tf_op jit(solution)/shard_map/all_gather | solution.py:101
  174.3 16.5 %collective-permute-start.16 = (bf16[144,2048]{1,0:T(8,128)(2,1)}, bf16[144,2048]{1,0:T(8,128)(2,1)S(1)}, u32[]{:S(2)}, u32[]{:S(2)}) collective-permute-start(bf16[144,2048]{1,0:T(8,128)(2,1)} %get-tuple-element.112.refs_0_), channel_id=1, source_target_pairs={{0,8},{8,0},{16,24},{24,16},{1,9},{9,1},{17,25},{25,17},{2,10},{10... | collective-permute-start | bytes 1769480 | tf_op jit(solution)/shard_map/ppermute | solution.py:66
  174.9 25.2 %collective-permute-start.17 = (bf16[144,2048]{1,0:T(8,128)(2,1)}, bf16[144,2048]{1,0:T(8,128)(2,1)S(1)}, u32[]{:S(2)}, u32[]{:S(2)}) collective-permute-start(bf16[144,2048]{1,0:T(8,128)(2,1)} %get-tuple-element.112.refs_0_), channel_id=1, source_target_pairs={{0,16},{8,24},{16,0},{24,8},{1,17},{9,25},{17,1},{25,9},{2,18},{10... | collective-permute-start | bytes 1769480 | tf_op jit(solution)/shard_map/ppermute | solution.py:66
  176.4 23.7 %collective-permute-start.18 = (bf16[144,2048]{1,0:T(8,128)(2,1)}, bf16[144,2048]{1,0:T(8,128)(2,1)S(1)}, u32[]{:S(2)}, u32[]{:S(2)}) collective-permute-start(bf16[144,2048]{1,0:T(8,128)(2,1)} %get-tuple-element.112.refs_0_), channel_id=1, source_target_pairs={{0,24},{8,16},{16,8},{24,0},{1,25},{9,17},{17,9},{25,1},{2,26},{10... | collective-permute-start | bytes 1769480 | tf_op jit(solution)/shard_map/ppermute | solution.py:66
  200.2 191.9 %all-gather.15.cloned.1.call-start = ((), (), s32[]{:S(2)}) async-start(), calls=%async_computation.9 | async-start | bytes 9437184 | tf_op jit(solution)/shard_map/all_gather | solution.py:101
  216.5 16.5 %collective-permute-start.19 = (bf16[144,2048]{1,0:T(8,128)(2,1)}, bf16[144,2048]{1,0:T(8,128)(2,1)S(1)}, u32[]{:S(2)}, u32[]{:S(2)}) collective-permute-start(bf16[144,2048]{1,0:T(8,128)(2,1)} %get-tuple-element.117), channel_id=1, source_target_pairs={{0,8},{8,0},{16,24},{24,16},{1,9},{9,1},{17,25},{25,17},{2,10},{10... | collective-permute-start | bytes 1769480 | tf_op jit(solution)/shard_map/ppermute | solution.py:66
  217.7 23.7 %collective-permute-start.20 = (bf16[144,2048]{1,0:T(8,128)(2,1)}, bf16[144,2048]{1,0:T(8,128)(2,1)S(1)}, u32[]{:S(2)}, u32[]{:S(2)}) collective-permute-start(bf16[144,2048]{1,0:T(8,128)(2,1)} %get-tuple-element.118), channel_id=1, source_target_pairs={{0,16},{8,24},{16,0},{24,8},{1,17},{9,25},{17,1},{25,9},{2,18},{10... | collective-permute-start | bytes 1769480 | tf_op jit(solution)/shard_map/ppermute | solution.py:66
  218.2 23.2 %collective-permute-start.21 = (bf16[144,2048]{1,0:T(8,128)(2,1)}, bf16[144,2048]{1,0:T(8,128)(2,1)S(1)}, u32[]{:S(2)}, u32[]{:S(2)}) collective-permute-start(bf16[144,2048]{1,0:T(8,128)(2,1)} %get-tuple-element.119), channel_id=1, source_target_pairs={{0,24},{8,16},{16,8},{24,0},{1,25},{9,17},{17,9},{25,1},{2,26},{10... | collective-permute-start | bytes 1769480 | tf_op jit(solution)/shard_map/ppermute | solution.py:66
  247.0 15.1 %collective-permute-start.22 = (bf16[144,2048]{1,0:T(8,128)(2,1)}, bf16[144,2048]{1,0:T(8,128)(2,1)S(1)}, u32[]{:S(2)}, u32[]{:S(2)}) collective-permute-start(bf16[144,2048]{1,0:T(8,128)(2,1)} %get-tuple-element.144.refs_0_), channel_id=1, source_target_pairs={{0,8},{8,0},{16,24},{24,16},{1,9},{9,1},{17,25},{25,17},{2,10},{10... | collective-permute-start | bytes 1769480 | tf_op jit(solution)/shard_map/ppermute | solution.py:66
  247.3 22.4 %collective-permute-start.23 = (bf16[144,2048]{1,0:T(8,128)(2,1)}, bf16[144,2048]{1,0:T(8,128)(2,1)S(1)}, u32[]{:S(2)}, u32[]{:S(2)}) collective-permute-start(bf16[144,2048]{1,0:T(8,128)(2,1)} %get-tuple-element.144.refs_0_), channel_id=1, source_target_pairs={{0,16},{8,24},{16,0},{24,8},{1,17},{9,25},{17,1},{25,9},{2,18},{10... | collective-permute-start | bytes 1769480 | tf_op jit(solution)/shard_map/ppermute | solution.py:66
  248.5 21.2 %collective-permute-start.24 = (bf16[144,2048]{1,0:T(8,128)(2,1)}, bf16[144,2048]{1,0:T(8,128)(2,1)S(1)}, u32[]{:S(2)}, u32[]{:S(2)}) collective-permute-start(bf16[144,2048]{1,0:T(8,128)(2,1)} %get-tuple-element.144.refs_0_), channel_id=1, source_target_pairs={{0,24},{8,16},{16,8},{24,0},{1,25},{9,17},{17,9},{25,1},{2,26},{10... | collective-permute-start | bytes 1769480 | tf_op jit(solution)/shard_map/ppermute | solution.py:66
  288.6 4.9 %collective-permute-start.25 = (f32[4,2048]{1,0:T(4,128)}, f32[4,2048]{1,0:T(4,128)S(1)}, u32[]{:S(2)}, u32[]{:S(2)}) collective-permute-start(f32[4,2048]{1,0:T(4,128)} %get-tuple-element.126.refs_0_), channel_id=1, source_target_pairs={{0,8},{8,0},{16,24},{24,16},{1,9},{9,1},{17,25},{25,17},{2,10},{10... | collective-permute-start | bytes 98312 | tf_op jit(solution)/shard_map/ppermute | solution.py:66
  290.2 4.1 collective-permute-start.26
  291.7 5.0 %collective-permute-start.27 = (f32[4,2048]{1,0:T(4,128)}, f32[4,2048]{1,0:T(4,128)S(1)}, u32[]{:S(2)}, u32[]{:S(2)}) collective-permute-start(f32[4,2048]{1,0:T(4,128)} %get-tuple-element.126.refs_0_), channel_id=1, source_target_pairs={{0,24},{8,16},{16,8},{24,0},{1,25},{9,17},{17,9},{25,1},{2,26},{10... | collective-permute-start | bytes 98312 | tf_op jit(solution)/shard_map/ppermute | solution.py:66
  303.9 11.3 %collective-permute-start.28 = (f32[4,2048]{1,0:T(4,128)}, f32[4,2048]{1,0:T(4,128)S(1)}, u32[]{:S(2)}, u32[]{:S(2)}) collective-permute-start(f32[4,2048]{1,0:T(4,128)} %get-tuple-element.142.refs_0_), channel_id=1, source_target_pairs={{0,8},{8,0},{16,24},{24,16},{1,9},{9,1},{17,25},{25,17},{2,10},{10... | collective-permute-start | bytes 98312 | tf_op jit(solution)/shard_map/ppermute | solution.py:66
  304.5 14.2 %collective-permute-start.29 = (f32[4,2048]{1,0:T(4,128)}, f32[4,2048]{1,0:T(4,128)S(1)}, u32[]{:S(2)}, u32[]{:S(2)}) collective-permute-start(f32[4,2048]{1,0:T(4,128)} %get-tuple-element.142.refs_0_), channel_id=1, source_target_pairs={{0,16},{8,24},{16,0},{24,8},{1,17},{9,25},{17,1},{25,9},{2,18},{10... | collective-permute-start | bytes 98312 | tf_op jit(solution)/shard_map/ppermute | solution.py:66
  305.0 13.7 %collective-permute-start.30 = (f32[4,2048]{1,0:T(4,128)}, f32[4,2048]{1,0:T(4,128)S(1)}, u32[]{:S(2)}, u32[]{:S(2)}) collective-permute-start(f32[4,2048]{1,0:T(4,128)} %get-tuple-element.142.refs_0_), channel_id=1, source_target_pairs={{0,24},{8,16},{16,8},{24,0},{1,25},{9,17},{17,9},{25,1},{2,26},{10... | collective-permute-start | bytes 98312 | tf_op jit(solution)/shard_map/ppermute | solution.py:66
  313.6 18.0 %collective-permute-start.31 = (bf16[4,10752]{1,0:T(4,128)(2,1)}, bf16[4,10752]{1,0:T(4,128)(2,1)S(1)}, u32[]{:S(2)}, u32[]{:S(2)}) collective-permute-start(bf16[4,10752]{1,0:T(4,128)(2,1)} %get-tuple-element.148.refs_0_), channel_id=1, source_target_pairs={{0,1},{1,0},{2,3},{3,2},{4,5},{5,4},{6,7},{7,6},{8,9},{9,8},{10,11... | collective-permute-start | bytes 258056 | tf_op jit(solution)/shard_map/ppermute | solution.py:72
  313.7 20.9 %collective-permute-start.32 = (bf16[4,10752]{1,0:T(4,128)(2,1)}, bf16[4,10752]{1,0:T(4,128)(2,1)S(1)}, u32[]{:S(2)}, u32[]{:S(2)}) collective-permute-start(bf16[4,10752]{1,0:T(4,128)(2,1)} %get-tuple-element.148.refs_0_), channel_id=1, source_target_pairs={{0,2},{1,3},{2,0},{3,1},{4,6},{5,7},{6,4},{7,5},{8,10},{9,11},{10,... | collective-permute-start | bytes 258056 | tf_op jit(solution)/shard_map/ppermute | solution.py:72
  315.2 19.4 %collective-permute-start.33 = (bf16[4,10752]{1,0:T(4,128)(2,1)}, bf16[4,10752]{1,0:T(4,128)(2,1)S(1)}, u32[]{:S(2)}, u32[]{:S(2)}) collective-permute-start(bf16[4,10752]{1,0:T(4,128)(2,1)} %get-tuple-element.148.refs_0_), channel_id=1, source_target_pairs={{0,3},{1,2},{2,1},{3,0},{4,7},{5,6},{6,5},{7,4},{8,11},{9,10},{10,... | collective-permute-start | bytes 258056 | tf_op jit(solution)/shard_map/ppermute | solution.py:72
  330.1 8.9 %collective-permute-start.38 = (bf16[4,3584]{1,0:T(4,128)(2,1)}, bf16[4,3584]{1,0:T(4,128)(2,1)S(1)}, u32[]{:S(2)}, u32[]{:S(2)}) collective-permute-start(bf16[4,3584]{1,0:T(4,128)(2,1)} %get-tuple-element.150.refs_0_), channel_id=1, source_target_pairs={{0,1},{1,0},{2,3},{3,2},{4,5},{5,4},{6,7},{7,6},{8,9},{9,8},{10,11... | collective-permute-start | bytes 86024 | tf_op jit(solution)/shard_map/ppermute | solution.py:72
  330.2 8.9 %collective-permute-start.39 = (bf16[4,3584]{1,0:T(4,128)(2,1)}, bf16[4,3584]{1,0:T(4,128)(2,1)S(1)}, u32[]{:S(2)}, u32[]{:S(2)}) collective-permute-start(bf16[4,3584]{1,0:T(4,128)(2,1)} %get-tuple-element.150.refs_0_), channel_id=1, source_target_pairs={{0,2},{1,3},{2,0},{3,1},{4,6},{5,7},{6,4},{7,5},{8,10},{9,11},{10,... | collective-permute-start | bytes 86024 | tf_op jit(solution)/shard_map/ppermute | solution.py:72
  331.7 7.5 %collective-permute-start.40 = (bf16[4,3584]{1,0:T(4,128)(2,1)}, bf16[4,3584]{1,0:T(4,128)(2,1)S(1)}, u32[]{:S(2)}, u32[]{:S(2)}) collective-permute-start(bf16[4,3584]{1,0:T(4,128)(2,1)} %get-tuple-element.150.refs_0_), channel_id=1, source_target_pairs={{0,3},{1,2},{2,1},{3,0},{4,7},{5,6},{6,5},{7,4},{8,11},{9,10},{10,... | collective-permute-start | bytes 86024 | tf_op jit(solution)/shard_map/ppermute | solution.py:72
  337.6 27.3 %collective-permute-start.34 = (bf16[4,4,10752]{2,1,0:T(4,128)(2,1)}, bf16[4,4,10752]{2,1,0:T(4,128)(2,1)S(1)}, u32[]{:S(2)}, u32[]{:S(2)}) collective-permute-start(bf16[4,4,10752]{2,1,0:T(4,128)(2,1)} %stack.54.planes), channel_id=1, source_target_pairs={{0,4},{4,0},{1,5},{5,1},{2,6},{6,2},{3,7},{7,3},{8,12},{12,8},{9,1... | collective-permute-start | bytes 1032200 | tf_op jit(solution)/shard_map/ppermute | solution.py:69
  341.8 17.3 %collective-permute-start.41 = (bf16[4,4,3584]{2,1,0:T(4,128)(2,1)}, bf16[4,4,3584]{2,1,0:T(4,128)(2,1)S(1)}, u32[]{:S(2)}, u32[]{:S(2)}) collective-permute-start(bf16[4,4,3584]{2,1,0:T(4,128)(2,1)} %stack.55.planes), channel_id=1, source_target_pairs={{0,4},{4,0},{1,5},{5,1},{2,6},{6,2},{3,7},{7,3},{8,12},{12,8},{9,1... | collective-permute-start | bytes 344072 | tf_op jit(solution)/shard_map/ppermute | solution.py:69
  354.9 37.3 %all-to-all-start.4 = ((bf16[32,72,64]{1,2,0:T(8,128)(2,1)}), bf16[32,72,64]{1,2,0:T(8,128)(2,1)S(1)}, u32[]{:S(2)}, u32[]{:S(2)}) async-start(bf16[32,72,64]{1,2,0:T(8,128)(2,1)} %copy.250), calls=%async_computation.4 | async-start | bytes 1048576 | tf_op jit(solution)/shard_map/all_to_all | solution.py:90
  361.4 14.2 %collective-permute-start.42 = (bf16[32,1536]{1,0:T(8,128)(2,1)}, bf16[32,1536]{1,0:T(8,128)(2,1)S(1)}, u32[]{:S(2)}, u32[]{:S(2)}) collective-permute-start(bf16[32,1536]{1,0:T(8,128)(2,1)} %get-tuple-element.151.refs_0_), channel_id=1, source_target_pairs={{0,8},{8,0},{16,24},{24,16},{1,9},{9,1},{17,25},{25,17},{2,10},{10... | collective-permute-start | bytes 294920 | tf_op jit(solution)/shard_map/ppermute | solution.py:66
  363.3 13.0 %collective-permute-start.43 = (bf16[32,1536]{1,0:T(8,128)(2,1)}, bf16[32,1536]{1,0:T(8,128)(2,1)S(1)}, u32[]{:S(2)}, u32[]{:S(2)}) collective-permute-start(bf16[32,1536]{1,0:T(8,128)(2,1)} %get-tuple-element.151.refs_0_), channel_id=1, source_target_pairs={{0,16},{8,24},{16,0},{24,8},{1,17},{9,25},{17,1},{25,9},{2,18},{10... | collective-permute-start | bytes 294920 | tf_op jit(solution)/shard_map/ppermute | solution.py:66
  364.8 13.0 %collective-permute-start.44 = (bf16[32,1536]{1,0:T(8,128)(2,1)}, bf16[32,1536]{1,0:T(8,128)(2,1)S(1)}, u32[]{:S(2)}, u32[]{:S(2)}) collective-permute-start(bf16[32,1536]{1,0:T(8,128)(2,1)} %get-tuple-element.151.refs_0_), channel_id=1, source_target_pairs={{0,24},{8,16},{16,8},{24,0},{1,25},{9,17},{17,9},{25,1},{2,26},{10... | collective-permute-start | bytes 294920 | tf_op jit(solution)/shard_map/ppermute | solution.py:66
  367.8 10.7 %collective-permute-start.35 = (bf16[32,3584]{1,0:T(8,128)(2,1)}, bf16[32,3584]{1,0:T(8,128)(2,1)S(1)}, u32[]{:S(2)}, u32[]{:S(2)}) collective-permute-start(bf16[32,3584]{1,0:T(8,128)(2,1)} %get-tuple-element.149.refs_0_), channel_id=1, source_target_pairs={{0,8},{8,0},{16,24},{24,16},{1,9},{9,1},{17,25},{25,17},{2,10},{10... | collective-permute-start | bytes 688136 | tf_op jit(solution)/shard_map/ppermute | solution.py:66
  369.7 10.5 %collective-permute-start.36 = (bf16[32,3584]{1,0:T(8,128)(2,1)}, bf16[32,3584]{1,0:T(8,128)(2,1)S(1)}, u32[]{:S(2)}, u32[]{:S(2)}) collective-permute-start(bf16[32,3584]{1,0:T(8,128)(2,1)} %get-tuple-element.149.refs_0_), channel_id=1, source_target_pairs={{0,16},{8,24},{16,0},{24,8},{1,17},{9,25},{17,1},{25,9},{2,18},{10... | collective-permute-start | bytes 688136 | tf_op jit(solution)/shard_map/ppermute | solution.py:66
  375.7 25.6 %collective-permute-start.51 = (bf16[16,2176]{1,0:T(8,128)(2,1)S(1)}, bf16[16,2176]{1,0:T(8,128)(2,1)S(1)}, u32[]{:S(2)}, u32[]{:S(2)}) collective-permute-start(bf16[16,2176]{1,0:T(8,128)(2,1)S(1)} %copy-done.75), channel_id=1, source_target_pairs={{0,8},{8,0},{16,24},{24,16},{1,9},{9,1},{17,25},{25,17},{2,10},{10... | collective-permute-start | bytes 208904 | tf_op jit(solution)/shard_map/ppermute | solution.py:66
  376.3 26.7 %collective-permute-start.48 = (bf16[32,2304]{1,0:T(8,128)(2,1)S(1)}, bf16[32,2304]{1,0:T(8,128)(2,1)S(1)}, u32[]{:S(2)}, u32[]{:S(2)}) collective-permute-start(bf16[32,2304]{1,0:T(8,128)(2,1)S(1)} %copy-done.73), channel_id=1, source_target_pairs={{0,8},{8,0},{16,24},{24,16},{1,9},{9,1},{17,25},{25,17},{2,10},{10... | collective-permute-start | bytes 442376 | tf_op jit(solution)/shard_map/ppermute | solution.py:66
  377.8 26.4 %collective-permute-start.49 = (bf16[32,2304]{1,0:T(8,128)(2,1)S(1)}, bf16[32,2304]{1,0:T(8,128)(2,1)S(1)}, u32[]{:S(2)}, u32[]{:S(2)}) collective-permute-start(bf16[32,2304]{1,0:T(8,128)(2,1)S(1)} %copy-done.72), channel_id=1, source_target_pairs={{0,16},{8,24},{16,0},{24,8},{1,17},{9,25},{17,1},{25,9},{2,18},{10... | collective-permute-start | bytes 442376 | tf_op jit(solution)/shard_map/ppermute | solution.py:66
  378.5 27.0 %collective-permute-start.50 = (bf16[32,2304]{1,0:T(8,128)(2,1)S(1)}, bf16[32,2304]{1,0:T(8,128)(2,1)S(1)}, u32[]{:S(2)}, u32[]{:S(2)}) collective-permute-start(bf16[32,2304]{1,0:T(8,128)(2,1)S(1)} %copy-done.71), channel_id=1, source_target_pairs={{0,24},{8,16},{16,8},{24,0},{1,25},{9,17},{17,9},{25,1},{2,26},{10... | collective-permute-start | bytes 442376 | tf_op jit(solution)/shard_map/ppermute | solution.py:66
  380.1 11.2 %collective-permute-start.37 = (bf16[32,3584]{1,0:T(8,128)(2,1)S(1)}, bf16[32,3584]{1,0:T(8,128)(2,1)S(1)}, u32[]{:S(2)}, u32[]{:S(2)}) collective-permute-start(bf16[32,3584]{1,0:T(8,128)(2,1)S(1)} %copy-done.36), channel_id=1, source_target_pairs={{0,24},{8,16},{16,8},{24,0},{1,25},{9,17},{17,9},{25,1},{2,26},{10... | collective-permute-start | bytes 688136 | tf_op jit(solution)/shard_map/ppermute | solution.py:66
  391.3 16.3 %collective-permute-start.52 = (bf16[16,2176]{1,0:T(8,128)(2,1)}, bf16[16,2176]{1,0:T(8,128)(2,1)S(1)}, u32[]{:S(2)}, u32[]{:S(2)}) collective-permute-start(bf16[16,2176]{1,0:T(8,128)(2,1)} %get-tuple-element.171), channel_id=1, source_target_pairs={{0,16},{8,24},{16,0},{24,8},{1,17},{9,25},{17,1},{25,9},{2,18},{10... | collective-permute-start | bytes 208904 | tf_op jit(solution)/shard_map/ppermute | solution.py:66
  401.3 6.4 %collective-permute-start.53 = (bf16[16,2176]{1,0:T(8,128)(2,1)S(1)}, bf16[16,2176]{1,0:T(8,128)(2,1)S(1)}, u32[]{:S(2)}, u32[]{:S(2)}) collective-permute-start(bf16[16,2176]{1,0:T(8,128)(2,1)S(1)} %copy-done.74), channel_id=1, source_target_pairs={{0,24},{8,16},{16,8},{24,0},{1,25},{9,17},{17,9},{25,1},{2,26},{10... | collective-permute-start | bytes 208904 | tf_op jit(solution)/shard_map/ppermute | solution.py:66
  403.0 31.0 %collective-permute-start.47 = (bf16[144,2048]{1,0:T(8,128)(2,1)}, bf16[144,2048]{1,0:T(8,128)(2,1)S(1)}, u32[]{:S(2)}, u32[]{:S(2)}) collective-permute-start(bf16[144,2048]{1,0:T(8,128)(2,1)} %get-tuple-element.158), channel_id=1, source_target_pairs={{0,24},{8,16},{16,8},{24,0},{1,25},{9,17},{17,9},{25,1},{2,26},{10... | collective-permute-start | bytes 1769480 | tf_op jit(solution)/shard_map/ppermute | solution.py:66
  404.3 29.7 %collective-permute-start.46 = (bf16[144,2048]{1,0:T(8,128)(2,1)}, bf16[144,2048]{1,0:T(8,128)(2,1)}, u32[]{:S(2)}, u32[]{:S(2)}) collective-permute-start(bf16[144,2048]{1,0:T(8,128)(2,1)} %get-tuple-element.157), channel_id=1, source_target_pairs={{0,16},{8,24},{16,0},{24,8},{1,17},{9,25},{17,1},{25,9},{2,18},{10... | collective-permute-start | bytes 1769480 | tf_op jit(solution)/shard_map/ppermute | solution.py:66
  405.5 28.5 %collective-permute-start.45 = (bf16[144,2048]{1,0:T(8,128)(2,1)}, bf16[144,2048]{1,0:T(8,128)(2,1)}, u32[]{:S(2)}, u32[]{:S(2)}) collective-permute-start(bf16[144,2048]{1,0:T(8,128)(2,1)} %get-tuple-element.156), channel_id=1, source_target_pairs={{0,8},{8,0},{16,24},{24,16},{1,9},{9,1},{17,25},{25,17},{2,10},{10... | collective-permute-start | bytes 1769480 | tf_op jit(solution)/shard_map/ppermute | solution.py:66
  414.9 17.1 %all-to-all-start.5 = ((f32[32,1,512]{2,1,0:T(1,128)}), f32[32,1,512]{2,1,0:T(1,128)S(1)}, u32[]{:S(2)}, u32[]{:S(2)}) async-start(f32[32,1,512]{2,1,0:T(1,128)} %reshape.285), calls=%async_computation.5 | async-start | bytes 131072 | tf_op jit(solution)/shard_map/all_to_all | solution.py:90
  (77 other events, 790.0 us)
Sparse Core Ops, SparseCore 0:
  27.5 82.3 all-gather.8
  112.1 81.2 all-gather.10
  200.3 79.8 all-gather.12
  281.6 100.9 all-gather.14
where the time goes:
time: 449 us; the launch traced here: 444 us
  waiting for transfers between devices  167 us (37%)
  Pallas kernels  122 us (27%)
  starting transfers between devices  88.8 us (20%)
  local copies, waits for them, and re-layouts  27.6 us (6%)
  between operations  16.1 us (4%)
  other arithmetic  13.7 us (3%)
  matrix products  9.76 us (2%)
    ppermute x42, waiting for transfers between devices, hop(): return lax.ppermute(value, 'tp', [(i, i ^ j) for i in range(self.tp)])  124 us
    pallas_call x18, Pallas kernels, in_vmem(): pl.pallas_call(kernel, in_specs=[pl.BlockSpec(memory_space=spaces.get(k,...  93.5 us
    ppermute x42, starting transfers between devices, hop(): return lax.ppermute(value, 'tp', [(i, i ^ j) for i in range(self.tp)])  50.6 us
    all_to_all x3, waiting for transfers between devices, shuffle(): lax.all_to_all(column_blocks(self.tp, shards), 'tp', 0, 0, tiled=True)  18.4 us
    ppermute x9, starting transfers between devices, other_plane(): return lax.ppermute(value, 'fsdp', [(i, i ^ k) for i in range(self.planes)])  13.3 us
    all_to_all x3, starting transfers between devices, shuffle(): lax.all_to_all(column_blocks(self.tp, shards), 'tp', 0, 0, tiled=True)  12.2 us
    all_gather x4, waiting for transfers between devices, gather_blocks(): return lax.all_gather(shard, ('core', 'fsdp'), axis=0)  10.9 us
    unnamed x156, local copies, waits for them, and re-layouts  9.97 us
  transfers between devices with their start and end apart: 64, of which 25 were waited for; matrix products, arithmetic and copies ran while one was open for 9% of the time, Pallas kernels for 27%

commit v1 on v0

--- a/solution.py
+++ b/solution.py
@@ -14,6 +14,7 @@
 BF = jnp.bfloat16
 F32 = jnp.float32
 VMEM_BYTES = 60 << 20
+COST = pl.CostEstimate(flops=1, bytes_accessed=1, transcendentals=0)
 
 
 def dot(left, right):
@@ -247,8 +248,17 @@
     return value * half, half + 0.5 * value * (1.0 - bent * bent) * steep
 
 
-def up_kernel(entries, weight, active):
-    active[...] = gelu_parts(project(entries[...], weight, slice(None)))[0].astype(BF)
+def up_kernel(tp, *refs):
+    entries, (weight, active, held, sems) = refs[:tp], refs[tp:]
+    rows = entries[0].shape[0]
+
+    @pl.when(pl.program_id(0) == 0)
+    def _():
+        pairs = [(ref, held.at[i * rows : (i + 1) * rows]) for i, ref in enumerate(entries)]
+        for copy in start_copies(pairs, sems):
+            copy.wait()
+
+    active[...] = gelu_parts(project(held[...], weight, slice(None)))[0].astype(BF)
 
 
 def mlp_back_kernel(tp, *refs):
@@ -357,17 +367,17 @@
 
 def text_back_kernel(tp, local, *refs):
     scores, probs, query_one, grad_cmix, kvq = refs[:5]
-    cross_one_row, mlp_one, grad_pre, grad_cq, mixed, cross, active, base, grad_mid = refs[5:14]
-    text = refs[14 : 14 + tp]
-    sent = refs[14 + tp : 14 + 2 * tp]
-    lefts, factors, weight, held, keys, values, sems = refs[14 + 2 * tp :]
+    cross_one_row, mlp_one, grad_pre, grad_cq, mixed, cross, active, grad_mid = refs[5:13]
+    text = refs[13 : 13 + tp]
+    sent = refs[13 + tp : 13 + 2 * tp]
+    lefts, factors, weight, held, keys, values, sems = refs[13 + 2 * tp :]
     span, width, txt = grad_cmix.shape[1], lefts.shape[1], scores.shape[2]
     copy = pltpu.make_async_copy(kvq.at[:, :, :, : 2 * span], weight, sems.at[0])
     copy.start()
     mask = head_mask(span)
     ff = grad_pre.shape[1]
     places, at = [], 0
-    for size in (ff, span, span, span, span, span, ff, width, width):
+    for size in (ff, span, span, span, span, span, ff, width):
         places.append(slice(at, at + size))
         at += size
     for i in range(tp):
@@ -385,8 +395,7 @@
     held[:tp, places[1]] = grad_cq[...]
     held[:tp, places[3]] = grad_cmix[...]
     held[:tp, places[6]] = active[...].astype(F32)[:tp]
-    held[:tp, places[7]] = base[...]
-    held[:tp, places[8]] = grad_mid[...]
+    held[:tp, places[7]] = grad_mid[...]
     factors[...] = held[:tp].astype(BF)
     begin = 2 * tp * local
     lefts[begin : begin + tp] = cross_one_row[...]
@@ -405,30 +414,34 @@
 
 
 def self_back_kernel(
-    tp, local, base, rows, gain, packed, probs, masked_entries, text_lefts, gathered, *refs,
+    tp, local, base, rows, gain, packed, probs, masked_entries, text_lefts, text_factors,
+    gain_a, embed, gain_m_row, gathered, *refs,
 ):
-    parts, entries, refs = refs[:tp], refs[tp : 2 * tp], refs[tp:]
-    sent = refs[tp : 2 * tp]
-    grad_attn, gain_row, payload, factors = refs[2 * tp : 2 * tp + 4]
-    weight, held, spreads, lefts, sems = refs[2 * tp + 4 :]
+    parts, entries, text_sent = refs[:tp], refs[tp : 2 * tp], refs[2 * tp : 3 * tp]
+    sent, refs = refs[3 * tp : 4 * tp], refs[4 * tp :]
+    payload, factors, weight, held, spreads, lefts, small, sems = refs
     width = lefts.shape[1]
     span, free = weight.shape[3] // 4, entries[0].shape[0]
-    copies = [pltpu.make_async_copy(gathered, weight, sems.at[0])]
-    for copy in copies:
-        copy.start()
+    copy = pltpu.make_async_copy(gathered, weight, sems.at[0])
+    copy.start()
+    ff = (text_factors.shape[1] - 5 * span - width) // 2
+    cut = ff + 3 * span
+    factors[:, :cut] = text_factors[:, :cut]
+    factors[:, cut + 3 * span : -width] = text_factors[:, cut:]
+    small[...] = jnp.zeros_like(small)
+    small[3:4] = gain_m_row[...]
     held[...] = jnp.zeros_like(held)
     for i in range(tp):
-        row_back(parts, rows, gain, base, i, held, gain_row)
-    grad_attn[...] = held[:tp]
-    copies[0].wait()
+        row_back(parts, rows, gain, base, i, held, small.at[2:3])
+    small[0:1] = held[0:1]
+    factors[:, -width:] = held[:tp].astype(BF)
+    copy.wait()
     mixed = out_back(held[...].astype(BF), weight, slice(3 * span, 4 * span))
-    factors[:, :span] = mixed[:tp].astype(BF)
-    factors[:, 3 * span :] = grad_attn[...].astype(BF)
+    factors[:, cut : cut + span] = mixed[:tp].astype(BF)
     mask = head_mask(span)
     held[...] = jnp.zeros_like(held)
-    first = lax.broadcasted_iota(jnp.int32, (PAD, TILE), 1) == 0
-    only = first & (lax.broadcasted_iota(jnp.int32, (PAD, TILE), 0) == 0)
     masked_row = masked_entries[:1].astype(F32)
+    ones = []
     for i in range(tp):
         spread = jnp.where(mask, mixed[i : i + 1], 0.0)
         spreads[8 * i : 8 * i + 8] = spread
@@ -439,6 +452,7 @@
         mean = jnp.sum(grad_probs * weighs, axis=-1, keepdims=True) + grad_one * one
         grad = (weighs * (grad_probs - mean)).astype(BF)
         grad_one = (one * (grad_one - mean)).astype(BF).astype(F32)
+        ones.append((grad_one, one))
         keys = packed[i, :, span : 2 * span]
         back = dot(grad, keys[:free]) + grad_one * keys[free : free + 1].astype(F32)
         back = jnp.sum(jnp.where(mask, back, 0.0), axis=0, keepdims=True)
@@ -449,57 +463,61 @@
         for kind in range(2):
             begin = (2 * i + kind) * local
             lefts[begin : begin + local] = found[8 * kind : 8 * kind + local]
-        sent[i][:PAD, width : width + free] = both
-        sent[i][:PAD, width + free :] = jnp.where(first, both_one, 0.0).astype(BF)
-        sent[i][PAD:, width : width + free] = jnp.zeros((PAD, free), BF)
-        sent[i][PAD:, width + free :] = jnp.where(only, 1.0, 0.0).astype(BF)
-    lefts[2 * tp * local :] = text_lefts[...]
-    own_width = payload.shape[2]
-    for d in range(payload.shape[0]):
-        payload[d] = lefts[:, d * own_width : (d + 1) * own_width].astype(BF)
-    factors[:, span : 2 * span] = held[:tp, :span].astype(BF)
+        sent[i][:PAD, width:] = both
+        sent[i][PAD:] = text_sent[i][...]
+    factors[:, cut + span : cut + 2 * span] = held[:tp, :span].astype(BF)
     queries = held[:, :span].astype(BF)
     zero_query = packed[0, free:, :span].astype(F32)[:1]
-    factors[:, 2 * span : 3 * span] = jnp.broadcast_to(zero_query, (tp, span)).astype(BF)
+    factors[:, cut + 2 * span : cut + 3 * span] = jnp.broadcast_to(zero_query, (tp, span)).astype(BF)
     key_spread = jnp.where(mask, zero_query, 0.0).astype(BF)
     value_spread = spreads[...].astype(BF)
     step = width // tp
-    empty = jnp.zeros((PAD - 1, step), F32)
+    field, scale = normed(embed[...])
     for t in range(tp):
         cols = slice(t * step, (t + 1) * step)
         keys = dot_t(key_spread, block(weight, t, slice(span, 2 * span))) * HDIM ** (-0.5)
         values = dot_t(value_spread, block(weight, t, slice(2 * span, 3 * span)))
         query_rows = dot_t(queries, block(weight, t, slice(0, span)))
+        masked_grad, gain_grad = 0.0, 0.0
         for i in range(tp):
-            both = jnp.concatenate([keys, values[8 * i : 8 * i + 8]], axis=0)
-            sent[i][:PAD, cols] = both.astype(BF)
-            last = jnp.concatenate([query_rows[i : i + 1], empty], axis=0)
-            sent[i][PAD:, cols] = last.astype(BF)
-
-
-def tokens_back_kernel(tp, rows, gain, base, place, gain_c, gain_m, *refs):
-    came, came_text, (tokens, text, payload, small) = refs[:tp], refs[tp : 2 * tp], refs[2 * tp :]
+            mine = values[8 * i : 8 * i + 8]
+            sent[i][:PAD, cols] = jnp.concatenate([keys, mine], axis=0).astype(BF)
+            last = query_rows[i : i + 1]
+            found = ones[i][0] * keys + ones[i][1] * mine
+            masked_grad = masked_grad + last + jnp.sum(found, axis=0, keepdims=True)
+            for kind, rows_back in enumerate((keys, mine)):
+                begin = (2 * i + kind) * local
+                found = lefts[begin : begin + local, cols] * rows_back[:local]
+                gain_grad = gain_grad + jnp.sum(found, axis=0, keepdims=True)
+        gain_grad = gain_grad / gain_a[:, cols]
+        rows_sum = jnp.sum(query_rows[:tp], axis=0, keepdims=True)
+        small[1:2, cols] = gain_grad + rows_sum * field[:, cols]
+        held[0:1, cols] = masked_grad
+    small[0:1] = small[0:1] + norm_back(held[0:1] * gain_a[...], field, scale)
+    begin = 2 * tp * local
+    lefts[begin : begin + text_lefts.shape[0]] = text_lefts[...]
+    begin += text_lefts.shape[0]
+    high = small[:4].astype(BF).astype(F32)
+    lefts[begin : begin + 4] = high
+    lefts[begin + 4 : begin + 8] = small[:4] - high
+    half, own = lefts.shape[0] // 2, payload.shape[2] // 2
+    for d in range(payload.shape[0]):
+        cols = slice(d * own, (d + 1) * own)
+        both = jnp.concatenate([lefts[:half, cols], lefts[half:, cols]], axis=1)
+        payload[d] = both.astype(BF)
+
+
+def tokens_back_kernel(tp, rows, gain, place, *refs):
+    came, (tokens, text) = refs[:tp], refs[tp:]
     width, free = rows.shape[1], place.shape[1]
-    grad, grad_one, grad_text = 0.0, 0.0, 0.0
-    for part, text_part in zip(came, came_text):
-        back = part[:, :width]
-        grad = grad + dot_sum(part[:, width : width + free], back)
-        grad_one = grad_one + dot_sum(part[:, width + free :], back)[:1]
-        grad_text = grad_text + dot_sum(text_part[:, width:], text_part[:, :width])
+    grad, grad_text = 0.0, 0.0
+    for part in came:
+        grad = grad + dot_sum(part[:PAD, width:], part[:PAD, :width])
+        grad_text = grad_text + dot_sum(part[PAD:, width:], part[PAD:, :width])
     text[...] = grad_text.astype(BF)
     field, scale = normed(rows[:free])
     start = norm_back(grad * gain[...], field, scale)
     tokens[...] = dot(place[...], start.astype(BF)).astype(BF)
-    one_field, one_scale = normed(rows[free : free + 1])
-    start = norm_back(grad_one * gain[...], one_field, one_scale)
-    small[...] = jnp.zeros_like(small)
-    small[0:1] = base[0:1] + start
-    small[1:2] = jnp.sum(grad * field, axis=0, keepdims=True) + grad_one * one_field
-    small[2:3] = gain_c[...]
-    small[3:4] = gain_m[...]
-    own = payload.shape[2]
-    for d in range(payload.shape[0]):
-        payload[d] = small[:, d * own : (d + 1) * own]
 
 
 def stack_kernel(*refs):
@@ -524,45 +542,36 @@
     return dot(same.astype(BF), right).astype(BF)
 
 
-def cross_columns_kernel(local, place, text_left, one_left, *refs):
-    right, (grad_kv, grad_cq, grad_up) = refs[:-3], refs[-3:]
+def columns_kernel(local, place, attn_left, text_left, one_left, entry, *refs):
+    right, (grad_qkv, grad_kv, grad_cq, grad_up) = refs[:-4], refs[-4:]
     tp, span = len(right), local * HDIM
-    ff = right[0].shape[1] - 3 * span
+    ff = right[0].shape[1] - 6 * span
+    ones = jnp.ones((right[0].shape[0], HDIM), BF)
+    scale = HDIM ** (-0.5)
+
+    def at_columns(begin, size):
+        return pl.ds(pl.multiple_of(begin, HDIM), size)
+
     for j in range(tp):
         at = place[0] ^ j
         rows = aligned(right[j][...], place[1], tp)
-        columns = pl.ds(pl.multiple_of(at * span, span), span)
-        grad_cq[:, columns] = dot_sum(one_left[at, 0], rows[:, ff : ff + span])
-        wide = pl.ds(pl.multiple_of(at * ff, ff), ff)
-        grad_up[:, wide] = dot_sum(one_left[at, 1], rows[:, :ff])
-        for h in range(local):
-            for kind in range(2):
-                start = ff + (1 + kind) * span + h * HDIM
-                outer = dot_sum(text_left[at, kind, h], rows[:, start : start + HDIM])
-                if kind == 0:
-                    outer = outer * HDIM ** (-0.5)
-                begin = kind * tp * span + at * span + h * HDIM
-                grad_kv[:, pl.ds(pl.multiple_of(begin, HDIM), HDIM)] = outer
-
-
-def self_columns_kernel(local, place, left, entry, *refs):
-    right, grad_qkv = refs[:-1], refs[-1]
-    tp, span = len(right), local * HDIM
-    ones = jnp.ones((right[0].shape[0], HDIM), BF)
-    for j in range(tp):
-        at = place[0] ^ j
-        rows = aligned(right[j][:, :span], place[1], tp)
-        total = jnp.sum(right[j][:, span : 2 * span].astype(F32), axis=0, keepdims=True)
-        queries = right[j][:, 2 * span :].astype(F32)[:1] * HDIM ** (-0.5)
-        grad_qkv[:, pl.ds(pl.multiple_of(at * span, span), span)] = entry[...] * total
+        part = [rows[:, ff + k * span : ff + (k + 1) * span] for k in range(6)]
+        grad_up[:, at_columns(at * ff, ff)] = dot_sum(one_left[at, 1], rows[:, :ff])
+        grad_cq[:, at_columns(at * span, span)] = dot_sum(one_left[at, 0], part[0])
+        total = jnp.sum(part[4].astype(F32), axis=0, keepdims=True)
+        grad_qkv[:, at_columns(at * span, span)] = entry[...] * total
+        queries = part[5].astype(F32)[:1] * scale
         for h in range(local):
             cols = slice(h * HDIM, (h + 1) * HDIM)
-            keys = dot_sum(left[at, 0, h], ones) * queries[:, cols]
-            begin = tp * span + at * span + h * HDIM
-            grad_qkv[:, pl.ds(pl.multiple_of(begin, HDIM), HDIM)] = keys
-            begin = 2 * tp * span + at * span + h * HDIM
-            values = dot_sum(left[at, 1, h], rows[:, cols])
-            grad_qkv[:, pl.ds(pl.multiple_of(begin, HDIM), HDIM)] = values
+            begin = at * span + h * HDIM
+            outer = dot_sum(text_left[at, 0, h], part[1][:, cols])
+            grad_kv[:, at_columns(begin, HDIM)] = outer * scale
+            outer = dot_sum(text_left[at, 1, h], part[2][:, cols])
+            grad_kv[:, at_columns(tp * span + begin, HDIM)] = outer
+            outer = dot_sum(attn_left[at, 0, h], ones) * queries[:, cols]
+            grad_qkv[:, at_columns(tp * span + begin, HDIM)] = outer
+            outer = dot_sum(attn_left[at, 1, h], part[3][:, cols])
+            grad_qkv[:, at_columns(2 * tp * span + begin, HDIM)] = outer
 
 
 def whole_spec():
@@ -580,6 +589,7 @@
         out_shape=[jax.ShapeDtypeStruct(shape, dtype) for shape, dtype in out_shape],
         scratch_shapes=scratch_shapes,
         compiler_params=pltpu.CompilerParams(vmem_limit_bytes=VMEM_BYTES),
+        cost_estimate=COST,
         name=name,
     )(*operands)
 
@@ -633,47 +643,51 @@
     return found[:tp], *found[tp:]
 
 
-def down_kernel(tp, active, weight, *partial):
-    rows = partial[0].shape[0]
-    part = weight[...]
-    added = dot(active[...], part.reshape(-1, part.shape[2])).astype(BF)
-    for i in range(tp):
-        partial[i][...] = added[i * rows : (i + 1) * rows]
+def down_kernel(tp, active, gathered, *refs):
+    partial, (weight, sems) = refs[:tp], refs[tp:]
+    rows, width = partial[0].shape
+    step = min(512, width)
+    parts = [slice(at, at + step) for at in range(0, width, step)]
+    copies = start_copies([(gathered.at[:, :, cols], weight.at[:, :, cols]) for cols in parts], sems)
+    for cols, copy in zip(parts, copies):
+        copy.wait()
+        part = weight[:, :, cols]
+        added = dot(active[...], part.reshape(-1, step)).astype(BF)
+        for i in range(tp):
+            partial[i][:, cols] = added[i * rows : (i + 1) * rows]
 
 
 def mlp_down(tp, active, gathered):
-    blocks, own, width = gathered.shape
-    rows, step = active.shape[0] // tp, 512
-    return pl.pallas_call(
+    rows, width = active.shape[0] // tp, gathered.shape[2]
+    return in_vmem(
         functools.partial(down_kernel, tp),
-        grid=(width // step,),
-        in_specs=[
-            pl.BlockSpec(active.shape, lambda i: (0, 0)),
-            pl.BlockSpec((blocks, own, step), lambda i: (0, 0, i)),
-        ],
-        out_specs=[pl.BlockSpec((rows, step), lambda i: (0, i))] * tp,
-        out_shape=[jax.ShapeDtypeStruct((rows, width), BF)] * tp,
-        compiler_params=pltpu.CompilerParams(vmem_limit_bytes=VMEM_BYTES),
-        name="mlp_down",
-    )(active, gathered)
+        "mlp_down",
+        [active, gathered],
+        [((rows, width), BF)] * tp,
+        [pltpu.VMEM(gathered.shape, BF), pltpu.SemaphoreType.DMA((width // min(512, width),))],
+        ((1, pl.ANY),),
+    )
 
 
 def mlp_up(entries, gathered):
-    rows, width = entries.shape
-    blocks, tp, own, ff = gathered.shape
+    tp, (rows, width) = len(entries), entries[0].shape
+    blocks, _, own, ff = gathered.shape
     step = min(ff, 512)
     return pl.pallas_call(
-        up_kernel,
+        functools.partial(up_kernel, tp),
         grid=(ff // step,),
-        in_specs=[
-            pl.BlockSpec((rows, width), lambda i: (0, 0)),
-            pl.BlockSpec((blocks, tp, own, step), lambda i: (0, 0, 0, i)),
-        ],
-        out_specs=pl.BlockSpec((rows, step), lambda i: (0, i)),
-        out_shape=jax.ShapeDtypeStruct((rows, ff), BF),
+        in_specs=[whole_spec()] * tp
+        + [pl.BlockSpec((blocks, tp, own, step), lambda i: (0, 0, 0, i))],
+        out_specs=pl.BlockSpec((tp * rows, step), lambda i: (0, i)),
+        out_shape=jax.ShapeDtypeStruct((tp * rows, ff), BF),
+        scratch_shapes=[
+            pltpu.VMEM((tp * rows, width), BF),
+            pltpu.SemaphoreType.DMA((tp,)),
+        ],
         compiler_params=pltpu.CompilerParams(vmem_limit_bytes=VMEM_BYTES),
+        cost_estimate=COST,
         name="mlp_up",
-    )(entries, gathered)
+    )(*entries, gathered)
 
 
 def mlp_back(entries, grad_active, gathered):
@@ -734,10 +748,10 @@
         "text_back",
         [scores, probs, query_one, grad_cmix, kvq, *rest, *text],
         [((PAD, width + txt), BF)] * tp
-        + [((2 * tp * (local + 1), width), F32), ((tp, 2 * ff + 5 * span + 2 * width), BF)],
+        + [((2 * tp * (local + 1), width), F32), ((tp, 2 * ff + 5 * span + width), BF)],
         [
             pltpu.VMEM((blocks, tp, own, 2 * span), BF),
-            pltpu.VMEM((8, 2 * ff + 5 * span + 2 * width), F32),
+            pltpu.VMEM((8, 2 * ff + 5 * span + width), F32),
             pltpu.VMEM((8 * tp, span), F32),
             pltpu.VMEM((8 * tp, span), F32),
             pltpu.SemaphoreType.DMA((1,)),
@@ -747,30 +761,28 @@
     return found[:tp], *found[tp:]
 
 
-def self_back(local, world, base, rows, gain, packed, probs, masked_entries, text_lefts, gathered, parts, entries):
-    tp, width = base.shape
+def self_back(local, world, small_operands, gathered, parts, entries, text_sent):
+    tp, width = small_operands[0].shape
+    text_lefts, text_factors = small_operands[6], small_operands[7]
     _, _, own, columns = gathered.shape
     span, free = columns // 4, entries[0].shape[0]
-    count = 2 * tp * (2 * local + 1)
+    count = 2 * tp * local + text_lefts.shape[0] + 8
+    operands = [*small_operands, gathered, *parts, *entries, *text_sent]
     found = in_vmem(
         functools.partial(self_back_kernel, tp, local),
         "self_back",
-        [base, rows, gain[None], packed, probs, masked_entries, text_lefts, gathered, *parts, *entries],
-        [((2 * PAD, width + free + TILE), BF)] * tp
-        + [
-            ((tp, width), F32),
-            ((1, width), F32),
-            ((world, count, own), BF),
-            ((tp, 3 * span + width), BF),
-        ],
+        operands,
+        [((2 * PAD, width + free), BF)] * tp
+        + [((world, count // 2, 2 * own), BF), ((tp, text_factors.shape[1] + 3 * span + width), BF)],
         [
             pltpu.VMEM(gathered.shape, BF),
             pltpu.VMEM((8, width), F32),
             pltpu.VMEM((8 * tp, span), F32),
             pltpu.VMEM((count, width), F32),
+            pltpu.VMEM((8, width), F32),
             pltpu.SemaphoreType.DMA((1,)),
         ],
-        ((7, pl.ANY),),
+        ((len(small_operands), pl.ANY),),
     )
     return found[:tp], *found[tp:]
 
@@ -828,6 +840,7 @@
             jax.ShapeDtypeStruct((rows, width), BF),
         ],
         compiler_params=pltpu.CompilerParams(vmem_limit_bytes=VMEM_BYTES),
+        cost_estimate=COST,
         name="join",
     )(base, gain[None], *parts)
 
@@ -919,12 +932,13 @@
 
     field_a, scale_a = normed(start)
     entries = (field_a * gain_a[None]).astype(BF)
+    masked_entries = entries[free:]
     entries_all = me.spread(entries[:free])
     text_rows = me.spread(after(text[0], entries_all))
     up_sent = me.shuffle([(after(w_up, (entries_all, kvq_sent)), 1)])
-    cross_w = me.gather_blocks(after(cross_sent, (attn_w, entries_all, up_sent)))
+    cross_w = me.gather_blocks(after(cross_sent, (attn_w, entries_all, up_sent, place, masked_entries, text_bias)))
     partial, packed, mixed_one, probs_one = self_forward(
-        local, masked_count, entries_all, entries[free:], attn_w
+        local, masked_count, entries_all, masked_entries, attn_w
     )
     after_attn, cross_entries = join(after(start, (grad_active, place)), me.collect(after(tuple(partial), text_rows)), gain_c)
 
@@ -944,7 +958,7 @@
     grad_mid, grad_cmix, scores, grad_cq, grad_entry, grad_gain_m = cross_back(
         cot_group, cross_stream, gain_m, pair, cross_probs_one, cross_w, me.tp_parts(grad_entry)
     )
-    text_sent, text_lefts, early_factors = text_back(
+    text_sent, text_lefts, text_factors = text_back(
         local,
         scores,
         cross_probs_one,
@@ -959,65 +973,66 @@
             mixed_one,
             cross_one,
             active_one,
-            cot_group,
             grad_mid,
         ],
         text_rows,
     )
-    sent, grad_attn, grad_gain_c, payload, late_factors = self_back(
+    sent, payload, factors = self_back(
         local,
         world,
-        grad_mid,
-        attn_stream,
-        gain_c,
-        packed,
-        probs_one,
-        entries[free:],
-        text_lefts,
+        [
+            grad_mid,
+            attn_stream,
+            gain_c[None],
+            packed,
+            probs_one,
+            masked_entries,
+            text_lefts,
+            text_factors,
+            gain_a[None],
+            embed[None],
+            grad_gain_m,
+        ],
         attn_w,
         me.tp_parts(grad_entry),
         entries_all,
+        text_sent,
     )
     came = me.to_owner(sent)
-    came_text = me.to_owner(text_sent)
 
     corner = me.c * planes + me.z
     ff = grad_pre.shape[1]
-
-    def gather_factors(factors, cut):
-        planes_of = stacked([factors] + [me.other_plane(factors, k) for k in range(1, planes)])
-        right, group = unpack(planes_of, me.other_core(planes_of), cut)
-        return [right] + [me.hop(right, j) for j in range(1, tp)], group
+    active = mlp_up(after(tuple(mlp_all), payload), up)
+    pieces = [factors] + [me.other_plane(factors, k) for k in range(1, planes)]
+    planes_of = stacked(after(tuple(pieces), (active, came)))
+    lefts = me.to_rows(after(payload, planes_of))
+    right, group = unpack(planes_of, me.other_core(planes_of), ff + 6 * span)
+    right = [right] + [me.hop(right, j) for j in range(1, tp)]
 
     def mine(stack):
         size = stack.shape[1] // (2 * planes)
         return lax.dynamic_slice_in_dim(stack, corner * size, size, axis=1)
 
-    early_right, group = gather_factors(early_factors, ff + 3 * span)
     cuts = [span, 2 * span, 2 * span + ff, 2 * span + ff + width]
-    mixed_f, cross_f, active_f, cot_f, mid_f = jnp.split(group, cuts, axis=1)
+    mixed_f, cross_f, active_f, mid_f, attn_f = jnp.split(group, cuts, axis=1)
+    cot_f = gathered[:, :, :width].astype(BF).swapaxes(0, 1).reshape(world, width)
+    grad_w_out = dot_sum(mine(mixed_f), attn_f)
     grad_w_cout = dot_sum(mine(cross_f), mid_f)
     grad_w_down = dot_sum(mine(active_f), cot_f)
-
-    late_right, attn_f = gather_factors(late_factors, 3 * span)
-    lefts = me.to_rows(payload)
-
-    active = mlp_up(jnp.concatenate(after(tuple(mlp_all), grad_attn)), up)
-    partial = mlp_down(tp, after(active, (early_right, late_right, lefts)), down)
-    output = sum(part.astype(F32) for part in me.collect(partial))
-    output = dot(place, (after_cross + output).astype(BF)).astype(BF)
-
-    grad_tokens, grad_text, small = in_vmem(
+    active = after(active, (right[0], lefts, grad_w_out, grad_w_cout, grad_w_down))
+    partial = mlp_down(tp, active, down)
+    collected = me.collect(partial)
+
+    grad_tokens, grad_text = in_vmem(
         functools.partial(tokens_back_kernel, tp),
         "tokens_back",
-        [start, gain_a[None], grad_attn, pick.T, grad_gain_c, grad_gain_m, *after(tuple(came), partial), *came_text],
-        [((seq, width), BF), ((txt, width), BF), ((world, 8, own), F32)],
-        [pltpu.VMEM((8, width), F32)],
-    )
-    small = jnp.sum(me.to_rows(small), axis=0)
+        [start, gain_a[None], pick.T, *after(tuple(came), partial)],
+        [((seq, width), BF), ((txt, width), BF)],
+    )
 
     heads = 2 * tp * local
     lefts = after(lefts, partial)
+    lefts = jnp.concatenate([lefts[:, :, :own], lefts[:, :, own:]], axis=1)
     attn_left, text_left = (
         lefts[:, k * heads : (k + 1) * heads]
         .reshape(tp, 2 * planes, tp, 2, local, own)
@@ -1025,26 +1040,23 @@
         .reshape(tp, 2, local, world, own)
         for k in range(2)
     )
-    one_left = lefts[:, 2 * heads :].reshape(tp, 2 * planes, 2, tp, own)
+    one_left = lefts[:, 2 * heads : 2 * heads + 2 * tp].reshape(tp, 2 * planes, 2, tp, own)
     one_left = one_left.transpose(0, 2, 1, 3, 4).reshape(tp, 2, world, own)
+    small = jnp.sum(lefts[:, 2 * heads + 2 * tp :].astype(F32), axis=0)
+    small = small[:4] + small[4:]
+    entry_own = lax.dynamic_slice_in_dim(entries[free], device * own, own).astype(F32)
     place_at = jnp.stack([me.t, corner]).astype(jnp.int32)
-    held = ((0, pltpu.SMEM),)
-    grad_w_kv, grad_w_cq, grad_w_up = in_vmem(
-        functools.partial(cross_columns_kernel, local),
-        "cross_columns",
-        [place_at, text_left, one_left, *early_right],
-        [((own, 2 * width), F32), ((own, width), F32), ((own, tp * ff), F32)],
-        held=held,
-    )
-    entry_own = lax.dynamic_slice_in_dim(entries[free], device * own, own).astype(F32)
-    (grad_w_qkv,) = in_vmem(
-        functools.partial(self_columns_kernel, local),
-        "self_columns",
-        [place_at, attn_left, entry_own[:, None], *late_right],
-        [((own, 3 * width), F32)],
-        held=held,
-    )
-    grad_w_out = dot_sum(mine(mixed_f), attn_f)
+    grad_w_qkv, grad_w_kv, grad_w_cq, grad_w_up = in_vmem(
+        functools.partial(columns_kernel, local),
+        "columns",
+        [place_at, attn_left, text_left, one_left, entry_own[:, None], *right],
+        [((own, 3 * width), F32), ((own, 2 * width), F32), ((own, width), F32), ((own, tp * ff), F32)],
+        held=((0, pltpu.SMEM),),
+    )
+
+    collected = after(tuple(collected), (grad_tokens, grad_w_qkv, small))
+    output = sum(part.astype(F32) for part in collected)
+    output = dot(place, (after_cross + output).astype(BF)).astype(BF)
     return (
         output,
         grad_tokens,

time: 449 us -> 431 us (0.960)
  starting transfers between devices: 88.8 us -> 71.1 us
  waiting for transfers between devices: 167 us -> 184 us
  local copies, waits for them, and re-layouts: 27.6 us -> 18.7 us
  Pallas kernels: 122 us -> 117 us
    ppermute x42 -> x36, waiting for transfers between devices: 124 us -> 133 us  [hop(): return lax.ppermute(value, 'tp', [(i, i ^ j) for i in range(self.tp)])]
    pallas_call x2 -> x1, Pallas kernels: 19 us -> 11 us  [mlp_up(): pl.pallas_call(functools.partial(up_kernel, tp), grid=(ff // step,), in_s...]
    ppermute x42 -> x36, starting transfers between devices: 50.6 us -> 42.7 us  [hop(): return lax.ppermute(value, 'tp', [(i, i ^ j) for i in range(self.tp)])]
    ppermute x9 -> x6, starting transfers between devices: 13.3 us -> 6.66 us  [other_plane(): return lax.ppermute(value, 'fsdp', [(i, i ^ k) for i in range(self.planes)])]
    ppermute x9 -> x6, waiting for transfers between devices: 4.98 us -> 11.2 us  [other_plane(): return lax.ppermute(value, 'fsdp', [(i, i ^ k) for i in range(self.planes)])]
    unnamed x156 -> x94, local copies, waits for them, and re-layouts: 9.97 us -> 6.03 us
    pallas_call x18 -> x16, Pallas kernels: 93.5 us -> 96.7 us  [in_vmem(): pl.pallas_call(kernel, in_specs=[pl.BlockSpec(memory_space=spaces.get(k,...]
  transfers between devices with their start and end apart: 64 -> 53, of which waited for: 25 -> 28; matrix products, arithmetic and copies ran while one was open for 9% -> 6% of each run, Pallas kernels for 27% -> 27%
where the time goes in v1:
time: 431 us; the launch traced here: 425 us
  waiting for transfers between devices  184 us (43%)
  Pallas kernels  117 us (27%)
  starting transfers between devices  71.1 us (16%)
  local copies, waits for them, and re-layouts  18.7 us (4%)
  between operations  15.9 us (4%)
  matrix products  9.47 us (2%)
  other arithmetic  9.21 us (2%)
    ppermute x36, waiting for transfers between devices, hop(): return lax.ppermute(value, 'tp', [(i, i ^ j) for i in range(self.tp)])  133 us
    pallas_call x16, Pallas kernels, in_vmem(): pl.pallas_call(kernel, in_specs=[pl.BlockSpec(memory_space=spaces.get(k,...  96.7 us
    ppermute x36, starting transfers between devices, hop(): return lax.ppermute(value, 'tp', [(i, i ^ j) for i in range(self.tp)])  42.7 us
    all_to_all x3, waiting for transfers between devices, shuffle(): lax.all_to_all(column_blocks(self.tp, shards), 'tp', 0, 0, tiled=True)  16.9 us
    all_gather x4, waiting for transfers between devices, gather_blocks(): return lax.all_gather(shard, ('core', 'fsdp'), axis=0)  14.3 us
    all_to_all x3, starting transfers between devices, shuffle(): lax.all_to_all(column_blocks(self.tp, shards), 'tp', 0, 0, tiled=True)  12.2 us
    ppermute x6, waiting for transfers between devices, other_plane(): return lax.ppermute(value, 'fsdp', [(i, i ^ k) for i in range(self.planes)])  11.2 us
    pallas_call x1, Pallas kernels, mlp_up(): pl.pallas_call(functools.partial(up_kernel, tp), grid=(ff // step,), in_s...  11 us
  transfers between devices with their start and end apart: 53, of which 28 were waited for; matrix products, arithmetic and copies ran while one was open for 6% of the time, Pallas kernels for 27%

profile of v1, /device:TPU:0, one launch (start us, length us, event | category | flops | bytes accessed | tf_op | source)
XLA Modules:
  0.0 424.8 jit_solution(5226167199525918788)
XLA Ops:
  7.2 2.2 column_blocks.5
  9.3 5.2 %all-to-all-start = ((bf16[4,64,1536]{2,1,0:T(8,128)(2,1)}), bf16[4,64,1536]{2,1,0:T(8,128)(2,1)S(1)}, u32[]{:S(2)}, u32[]{:S(2)}) async-start(bf16[4,64,1536]{2,1,0:T(8,128)(2,1)} %column_blocks.5), calls=%async_computation | async-start | bytes 1572864 | tf_op jit(solution)/shard_map/all_to_all | solution.py:99
  14.5 1.7 column_blocks.7
  16.2 9.1 %all-to-all-done = bf16[4,64,1536]{2,1,0:T(8,128)(2,1)S(1)} async-done(((bf16[4,64,1536]{2,1,0:T(8,128)(2,1)}), bf16[4,64,1536]{2,1,0:T(8,128)(2,1)S(1)}, u32[]{:S(2)}, u32[]{:S(2)}) %all-to-all-start) | async-done | bytes 786464 | tf_op jit(solution)/shard_map/all_to_all | solution.py:99
  25.3 2.1 pad_maximum_fusion.1
  28.3 1.7 collective-permute-start
  30.0 2.6 collective-permute-start.1
  34.6 3.5 collective-permute-done.2
  39.5 1.5 collective-permute-start.6
  43.7 2.8 collective-permute-done.5
  49.2 2.1 column_blocks.6
  51.3 3.5 all-to-all-start.1
  56.1 2.0 collective-permute-start.7
  60.5 17.7 %collective-permute-done.7.refs_1_.refs_5_ = bf16[128,2048]{1,0:T(8,128)(2,1)S(1)} collective-permute-done((bf16[128,2048]{1,0:T(8,128)(2,1)S(1)}, bf16[128,2048]{1,0:T(8,128)(2,1)S(1)}, u32[]{:S(2)}, u32[]{:S(2)}) %collective-permute-start.7) | collective-permute-done | bytes 524320 | tf_op jit(solution)/shard_map/ppermute | solution.py:67
  79.0 10.4 %collective-permute-done.9.refs_3_.refs_7_ = bf16[128,2048]{1,0:T(8,128)(2,1)} collective-permute-done((bf16[128,2048]{1,0:T(8,128)(2,1)S(1)}, bf16[128,2048]{1,0:T(8,128)(2,1)}, u32[]{:S(2)}, u32[]{:S(2)}) %collective-permute-start.9) | collective-permute-done | bytes 524320 | tf_op jit(solution)/shard_map/ppermute | solution.py:67
  89.5 2.3 column_blocks.9
  91.7 3.5 all-to-all-start.3
  96.9 1.7 column_blocks.8
  98.6 2.1 pad_maximum_fusion.2
  100.7 7.7 %all-to-all-done.3 = bf16[4,64,2048]{2,1,0:T(8,128)(2,1)S(1)} async-done(((bf16[4,64,2048]{2,1,0:T(8,128)(2,1)}), bf16[4,64,2048]{2,1,0:T(8,128)(2,1)S(1)}, u32[]{:S(2)}, u32[]{:S(2)}) %all-to-all-start.3) | async-done | bytes 1048608 | tf_op jit(solution)/shard_map/all_to_all | solution.py:99
  108.4 1.5 all-gather.9.cloned.1.call-done
  111.7 1.6 collective-permute-start.10
  115.3 17.8 %self_attention.1 = (bf16[144,2048]{1,0:T(8,128)(2,1)}, bf16[144,2048]{1,0:T(8,128)(2,1)}, bf16[144,2048]{1,0:T(8,128)(2,1)}, bf16[144,2048]{1,0:T(8,128)(2,1)},...) custom-call(bf16[128,2048]{1,0:T(8,128)(2,1)} %copy-done.2, ...), custom_call_target="tpu_custom_call" | custom-call | flops 1 | bytes 1 | tf_op jit(solution)/shard_map/self_attention/pallas_call | solution.py:583
  133.1 5.2 %collective-permute-done.11.refs_6_.refs_15_ = bf16[128,2048]{1,0:T(8,128)(2,1)S(1)} collective-permute-done((bf16[128,2048]{1,0:T(8,128)(2,1)S(1)}, bf16[128,2048]{1,0:T(8,128)(2,1)S(1)}, u32[]{:S(2)}, u32[]{:S(2)}) %collective-permute-start.11) | collective-permute-done | bytes 524320 | tf_op jit(solution)/shard_map/ppermute | solution.py:67
  142.5 3.3 all-to-all-start.2
  146.6 5.5 %all-to-all-done.2 = f32[8,4,256]{2,1,0:T(4,128)S(1)} async-done(((f32[8,4,256]{2,1,0:T(4,128)}), f32[8,4,256]{2,1,0:T(4,128)S(1)}, u32[]{:S(2)}, u32[]{:S(2)}) %all-to-all-start.2) | async-done | bytes 32800 | tf_op jit(solution)/shard_map/all_to_all | solution.py:930
  152.0 2.8 collective-permute-done.13.refs_1_
  154.8 12.1 %collective-permute-done.14.refs_2_ = bf16[144,2048]{1,0:T(8,128)(2,1)} collective-permute-done((bf16[144,2048]{1,0:T(8,128)(2,1)}, bf16[144,2048]{1,0:T(8,128)(2,1)}, u32[]{:S(2)}, u32[]{:S(2)}) %collective-permute-start.14) | collective-permute-done | bytes 589856 | tf_op jit(solution)/shard_map/ppermute | solution.py:67
  166.9 4.5 %join.2 = (f32[144,2048]{1,0:T(8,128)}, bf16[144,2048]{1,0:T(8,128)(2,1)}) custom-call(f32[144,2048]{1,0:T(8,128)} %get-tuple-element.106.base.rows, f32[1,2048]{1,0:T(1,128)} %slice.164.gain, bf16[144,2048]{1,0:T(8,128)(2,1)} %get-tuple-element.112.refs_0_, bf16[144,2048]{1,0:T(8,128)(2,1)} %copy-done.20, ...), custom_call_target="tpu_custom_call" | custom-call | flops 1 | bytes 1 | tf_op jit(solution)/shard_map/join/pallas_call | solution.py:833
  175.0 13.0 %collective-permute-done.16.refs_1_ = bf16[144,2048]{1,0:T(8,128)(2,1)S(1)} collective-permute-done((bf16[144,2048]{1,0:T(8,128)(2,1)}, bf16[144,2048]{1,0:T(8,128)(2,1)S(1)}, u32[]{:S(2)}, u32[]{:S(2)}) %collective-permute-start.16) | collective-permute-done | bytes 589856 | tf_op jit(solution)/shard_map/ppermute | solution.py:67
  188.0 10.0 %collective-permute-done.17.refs_2_ = bf16[144,2048]{1,0:T(8,128)(2,1)S(1)} collective-permute-done((bf16[144,2048]{1,0:T(8,128)(2,1)}, bf16[144,2048]{1,0:T(8,128)(2,1)S(1)}, u32[]{:S(2)}, u32[]{:S(2)}) %collective-permute-start.17) | collective-permute-done | bytes 589856 | tf_op jit(solution)/shard_map/ppermute | solution.py:67
  199.0 14.1 %cross_attention.1 = (bf16[144,2048]{1,0:T(8,128)(2,1)}, bf16[144,2048]{1,0:T(8,128)(2,1)}, bf16[144,2048]{1,0:T(8,128)(2,1)}, bf16[144,2048]{1,0:T(8,128)(2,1)}...) custom-call(bf16[144,2048]{1,0:T(8,128)(2,1)} %get-tuple-element.117, ...), custom_call_target="tpu_custom_call" | custom-call | flops 1 | bytes 1 | tf_op jit(solution)/shard_map/cross_attention/pallas_call | solution.py:583
  215.0 1.7 collective-permute-start.21
  217.4 12.3 %collective-permute-done.19.refs_1_ = bf16[144,2048]{1,0:T(8,128)(2,1)S(1)} collective-permute-done((bf16[144,2048]{1,0:T(8,128)(2,1)}, bf16[144,2048]{1,0:T(8,128)(2,1)S(1)}, u32[]{:S(2)}, u32[]{:S(2)}) %collective-permute-start.19) | collective-permute-done | bytes 589856 | tf_op jit(solution)/shard_map/ppermute | solution.py:67
  229.7 9.3 %collective-permute-done.20.refs_2_ = bf16[144,2048]{1,0:T(8,128)(2,1)S(1)} collective-permute-done((bf16[144,2048]{1,0:T(8,128)(2,1)}, bf16[144,2048]{1,0:T(8,128)(2,1)S(1)}, u32[]{:S(2)}, u32[]{:S(2)}) %collective-permute-start.20) | collective-permute-done | bytes 589856 | tf_op jit(solution)/shard_map/ppermute | solution.py:67
  240.0 4.5 %join.3 = (f32[144,2048]{1,0:T(8,128)}, bf16[144,2048]{1,0:T(8,128)(2,1)}) custom-call(f32[144,2048]{1,0:T(8,128)} %get-tuple-element.116.base, f32[1,2048]{1,0:T(1,128)} %slice.169.gain, bf16[144,2048]{1,0:T(8,128)(2,1)} %get-tuple-element.121.refs_0_, bf16[144,2048]{1,0:T(8,128)(2,1)} %copy-done.21, bf16[144,2048]{1,0:T(8,128)(2,1)} %copy-done.22, ...), custom_call_target="tpu_custom_call" | custom-call | flops 1 | bytes 1 | tf_op jit(solution)/shard_map/join/pallas_call | solution.py:833
  246.1 1.9 collective-permute-start.24
  248.0 12.4 %collective-permute-done.22.refs_1_ = bf16[144,2048]{1,0:T(8,128)(2,1)S(1)} collective-permute-done((bf16[144,2048]{1,0:T(8,128)(2,1)}, bf16[144,2048]{1,0:T(8,128)(2,1)S(1)}, u32[]{:S(2)}, u32[]{:S(2)}) %collective-permute-start.22) | collective-permute-done | bytes 589856 | tf_op jit(solution)/shard_map/ppermute | solution.py:67
  260.4 7.9 %collective-permute-done.23.refs_2_ = bf16[144,2048]{1,0:T(8,128)(2,1)S(1)} collective-permute-done((bf16[144,2048]{1,0:T(8,128)(2,1)}, bf16[144,2048]{1,0:T(8,128)(2,1)S(1)}, u32[]{:S(2)}, u32[]{:S(2)}) %collective-permute-start.23) | collective-permute-done | bytes 589856 | tf_op jit(solution)/shard_map/ppermute | solution.py:67
  268.3 9.8 %all-gather.13.cloned.1.call-done = bf16[32,64,2048]{2,1,0:T(8,128)(2,1)} async-done(((bf16[4,64,2048]{2,1,0:T(8,128)(2,1)}), bf16[32,64,2048]{2,1,0:T(8,128)(2,1)}) %all-gather.13.cloned.1.call-update) | async-done | bytes 8388624 | tf_op jit(solution)/shard_map/all_gather | solution.py:102
  278.8 7.8 %mlp_back.1 = (bf16[16,2048]{1,0:T(8,128)(2,1)}, bf16[16,2048]{1,0:T(8,128)(2,1)}, f32[4,2048]{1,0:T(4,128)}, f32[4,2048]{1,0:T(4,128)}, f32[4,2048]{1,0:T(4,128)}) custom-call(bf16[144,2048]{1,0:T(8,128)(2,1)} %get-tuple-element.155.refs_0_, bf16[144,2048]{1,0:T(8,128)(2,1)} %copy-done.5, bf16[144,2048]{1,0:T(8,128)(2,1)} %copy-done.6, ...), custom_call_target="tpu_custom_call" | custom-call | flops 1 | bytes 1 | tf_op jit(solution)/shard_map/mlp_back/pallas_call | solution.py:583
  286.6 1.6 collective-permute-start.25
  292.3 2.4 collective-permute-done.27.refs_3_
  295.3 6.6 %cross_back.1 = (f32[4,2048]{1,0:T(4,128)}, f32[4,512]{1,0:T(4,128)}, f32[4,8,128]{2,1,0:T(8,128)}, f32[4,512]{1,0:T(4,128)}, f32[4,2048]{1,0:T(4,128)}, /*index=5*/f32[1,2048]{1,0:T(1,128)}) custom-call(f32[4,2048]{1,0:T(4,128)} %slice_bitcast_fusion.base, f32[4,2048]{1,0:T(4,128)} %get-tuple-element.128.rows, f32[1,2048]{1,0:T(1,128)} %slice.169.gain, ...), custom_call_target="tpu_custom_call" | custom-call | flops 1 | bytes 1 | tf_op jit(solution)/shard_map/cross_back/pallas_call | solution.py:583
  303.0 2.5 collective-permute-start.30
  306.8 6.2 %text_back.1 = (bf16[16,2176]{1,0:T(8,128)(2,1)}, bf16[16,2176]{1,0:T(8,128)(2,1)}, bf16[16,2176]{1,0:T(8,128)(2,1)}, bf16[16,2176]{1,0:T(8,128)(2,1)}, f32[40,2048]{1,0:T(8,128)}, /*index=5*/bf16[4,8704]{1,0:T(4,128)(2,1)}) custom-call(f32[4,8,128]{2,1,0:T(8,128)} %get-tuple-element.136.refs_0_, f32[4,8,128]{2,1,0:T(8,128)} %get-tuple-element.130.probs.refs_1_, ...), custom_call_target="tpu_custom_call" | custom-call | flops 1 | bytes 1 | tf_op jit(solution)/shard_map/text_back/pallas_call | solution.py:583
  313.6 11.0 %self_back.1 = (bf16[32,2176]{1,0:T(8,128)(2,1)}, bf16[32,2176]{1,0:T(8,128)(2,1)}, bf16[32,2176]{1,0:T(8,128)(2,1)}, bf16[32,2176]{1,0:T(8,128)(2,1)}, bf16[32,...) custom-call(f32[4,2048]{1,0:T(4,128)} %get-tuple-element.132.refs_12_.base, f32[4,2048]{1,0:T(4,128)} %get-tuple-element.133.rows, ...), custom_call_target="tpu_custom_call" | custom-call | flops 1 | bytes 1 | tf_op jit(solution)/shard_map/self_back/pallas_call | solution.py:583
  325.8 2.5 collective-permute-start.36
  329.7 6.2 %collective-permute-done.31.refs_1_ = bf16[4,12288]{1,0:T(4,128)(2,1)S(1)} collective-permute-done((bf16[4,12288]{1,0:T(4,128)(2,1)}, bf16[4,12288]{1,0:T(4,128)(2,1)S(1)}, u32[]{:S(2)}, u32[]{:S(2)}) %collective-permute-start.31) | collective-permute-done | bytes 98336 | tf_op jit(solution)/shard_map/ppermute | solution.py:73
  337.2 11.0 %mlp_up.1.active = bf16[576,2048]{1,0:T(8,128)(2,1)} custom-call(bf16[144,2048]{1,0:T(8,128)(2,1)} %get-tuple-element.155.refs_0_, bf16[144,2048]{1,0:T(8,128)(2,1)} %copy-done.5, bf16[144,2048]{1,0:T(8,128)(2,1)} %copy-done.6, bf16[144,2048]{1,0:T(8,128)(2,1)} %copy-done.7, bf16[8,4,64,2048]{3,2,1,0:T(8,128)(2,1)} %bitcast.124), custom_call_target="tpu_custom_call" | custom-call | flops 1 | bytes 1 | tf_op jit(solution)/shard_map/mlp_up/pallas_call | solution.py:676
  348.9 1.8 stack.53.planes
  351.5 5.7 %all-to-all-start.4 = ((bf16[32,40,128]{2,1,0:T(8,128)(2,1)}), bf16[32,40,128]{2,1,0:T(8,128)(2,1)S(1)}, u32[]{:S(2)}, u32[]{:S(2)}) async-start(bf16[32,40,128]{2,1,0:T(8,128)(2,1)} %get-tuple-element.169), calls=%async_computation.4 | async-start | bytes 655360 | tf_op jit(solution)/shard_map/all_to_all | solution.py:91
  358.0 2.2 unpack.1
  360.3 1.9 collective-permute-start.41
  364.6 2.0 fusion.8
  367.5 1.8 fusion.24
  369.3 2.0 fusion.6
  372.4 3.0 all-gather.15.cloned.1.call-done
  375.4 10.1 %mlp_down.1 = (bf16[144,2048]{1,0:T(8,128)(2,1)}, bf16[144,2048]{1,0:T(8,128)(2,1)}, bf16[144,2048]{1,0:T(8,128)(2,1)}, bf16[144,2048]{1,0:T(8,128)(2,1)}) custom-call(bf16[576,2048]{1,0:T(8,128)(2,1)} %mlp_up.1.active, bf16[8,256,2048]{2,1,0:T(8,128)(2,1)} %bitcast.125), custom_call_target="tpu_custom_call" | custom-call | flops 1 | bytes 1 | tf_op jit(solution)/shard_map/mlp_down/pallas_call | solution.py:583
  385.5 1.5 collective-permute-start.38
  389.4 4.2 tokens_back.1
  395.9 5.1 %columns.1 = (f32[64,6144]{1,0:T(8,128)}, f32[64,4096]{1,0:T(8,128)}, f32[64,2048]{1,0:T(8,128)}, f32[64,8192]{1,0:T(8,128)}) custom-call(s32[2]{0:T(128)} %pad_add_fusion.place, bf16[4,2,4,32,64]{4,3,2,1,0:T(8,128)(2,1)} %bitcast.139, bf16[4,2,4,32,64]{4,3,2,1,0:T(8,128)(2,1)} %bitcast.140, bf16[4,2,32,64]{3,2,1,0:T(8,128)(2,1)} %bitcast.150, ...), custom_call_target="tpu_custom_call" | custom-call | flops 1 | bytes 1 | tf_op jit(solution)/shard_map/columns/pallas_call | solution.py:583
  401.9 13.1 %collective-permute-done.39 = bf16[144,2048]{1,0:T(8,128)(2,1)S(1)} collective-permute-done((bf16[144,2048]{1,0:T(8,128)(2,1)}, bf16[144,2048]{1,0:T(8,128)(2,1)S(1)}, u32[]{:S(2)}, u32[]{:S(2)}) %collective-permute-start.39) | collective-permute-done | bytes 589856 | tf_op jit(solution)/shard_map/ppermute | solution.py:67
  415.1 2.7 convolution_convert_fusion
  (273 shorter events, 57.5 us)
Async XLA Ops:
  7.2 35.9 %copy-start = (bf16[256,2048]{1,0:T(8,128)(2,1)S(1)}, bf16[256,2048]{1,0:T(8,128)(2,1)}, u32[]{:S(2)}) copy-start(bf16[256,2048]{1,0:T(8,128)(2,1)} %param.16) | copy-start | bytes 3145732
  9.3 16.0 %all-to-all-start = ((bf16[4,64,1536]{2,1,0:T(8,128)(2,1)}), bf16[4,64,1536]{2,1,0:T(8,128)(2,1)S(1)}, u32[]{:S(2)}, u32[]{:S(2)}) async-start(bf16[4,64,1536]{2,1,0:T(8,128)(2,1)} %column_blocks.5), calls=%async_computation | async-start | bytes 1572864 | tf_op jit(solution)/shard_map/all_to_all | solution.py:99
  14.5 95.4 %all-gather.9.cloned.1.call-start = ((), (), s32[]{:S(2)}) async-start(), calls=%async_computation.5 | async-start | bytes 9437184 | tf_op jit(solution)/shard_map/all_gather | solution.py:102
  28.3 4.8 %collective-permute-start = (f32[2432]{0:T(1024)S(1)}, f32[2432]{0:T(1024)S(1)}, u32[]{:S(2)}, u32[]{:S(2)}) collective-permute-start(f32[2432]{0:T(1024)S(1)} %pad_maximum_fusion.14), channel_id=1, source_target_pairs={{0,1},{1,0},{2,3},{3,2},{4,5},{5,4},{6,7},{7,6},{8,9},{9,8},{10,11... | collective-permute-start | bytes 29192 | tf_op jit(solution)/shard_map/ppermute | solution.py:73
  30.0 4.6 %collective-permute-start.1 = (f32[2432]{0:T(1024)S(1)}, f32[2432]{0:T(1024)S(1)}, u32[]{:S(2)}, u32[]{:S(2)}) collective-permute-start(f32[2432]{0:T(1024)S(1)} %pad_maximum_fusion.14), channel_id=1, source_target_pairs={{0,2},{1,3},{2,0},{3,1},{4,6},{5,7},{6,4},{7,5},{8,10},{9,11},{10,... | collective-permute-start | bytes 29192 | tf_op jit(solution)/shard_map/ppermute | solution.py:73
  32.6 5.5 %collective-permute-start.2 = (f32[2432]{0:T(1024)S(1)}, f32[2432]{0:T(1024)S(1)}, u32[]{:S(2)}, u32[]{:S(2)}) collective-permute-start(f32[2432]{0:T(1024)S(1)} %pad_maximum_fusion.14), channel_id=1, source_target_pairs={{0,3},{1,2},{2,1},{3,0},{4,7},{5,6},{6,5},{7,4},{8,11},{9,10},{10,... | collective-permute-start | bytes 29192 | tf_op jit(solution)/shard_map/ppermute | solution.py:73
  38.1 1.3 collective-permute-start.3
  39.5 7.4 %collective-permute-start.6 = (f32[8,2432]{1,0:T(8,128)S(1)}, f32[8,2432]{1,0:T(8,128)S(1)}, u32[]{:S(2)}, u32[]{:S(2)}) collective-permute-start(f32[8,2432]{1,0:T(8,128)S(1)} %concatenate.111), channel_id=1, source_target_pairs={{0,24},{8,16},{16,8},{24,0},{1,25},{9,17},{17,9},{25,1},{2,26},{10... | collective-permute-start | bytes 233480 | tf_op jit(solution)/shard_map/ppermute | solution.py:67
  41.0 5.5 %collective-permute-start.5 = (f32[8,2432]{1,0:T(8,128)S(1)}, f32[8,2432]{1,0:T(8,128)S(1)}, u32[]{:S(2)}, u32[]{:S(2)}) collective-permute-start(f32[8,2432]{1,0:T(8,128)S(1)} %concatenate.111), channel_id=1, source_target_pairs={{0,16},{8,24},{16,0},{24,8},{1,17},{9,25},{17,1},{25,9},{2,18},{10... | collective-permute-start | bytes 233480 | tf_op jit(solution)/shard_map/ppermute | solution.py:67
  42.4 4.4 %collective-permute-start.4 = (f32[8,2432]{1,0:T(8,128)S(1)}, f32[8,2432]{1,0:T(8,128)S(1)}, u32[]{:S(2)}, u32[]{:S(2)}) collective-permute-start(f32[8,2432]{1,0:T(8,128)S(1)} %concatenate.111), channel_id=1, source_target_pairs={{0,8},{8,0},{16,24},{24,16},{1,9},{9,1},{17,25},{25,17},{2,10},{10... | collective-permute-start | bytes 233480 | tf_op jit(solution)/shard_map/ppermute | solution.py:67
  51.3 38.2 %all-to-all-start.1 = ((bf16[4,64,1536]{2,1,0:T(8,128)(2,1)}), bf16[4,64,1536]{2,1,0:T(8,128)(2,1)S(1)}, u32[]{:S(2)}, u32[]{:S(2)}) async-start(bf16[4,64,1536]{2,1,0:T(8,128)(2,1)} %column_blocks.6), calls=%async_computation.1 | async-start | bytes 1572864 | tf_op jit(solution)/shard_map/all_to_all | solution.py:99
  56.1 35.7 %copy-start.2 = (bf16[128,2048]{1,0:T(8,128)(2,1)}, bf16[128,2048]{1,0:T(8,128)(2,1)S(1)}, u32[]{:S(2)}) copy-start(bf16[128,2048]{1,0:T(8,128)(2,1)S(1)} %slice.211.refs_0_.refs_4_) | copy-start | bytes 1572868
  56.1 22.1 %collective-permute-start.7 = (bf16[128,2048]{1,0:T(8,128)(2,1)S(1)}, bf16[128,2048]{1,0:T(8,128)(2,1)S(1)}, u32[]{:S(2)}, u32[]{:S(2)}) collective-permute-start(bf16[128,2048]{1,0:T(8,128)(2,1)S(1)} %slice.211.refs_0_.refs_4_), channel_id=1, source_target_pairs={{0,8},{8,0},{16,24},{24,16},{1,9},{9,1},{17,25},{25,17},{2,10},{10... | collective-permute-start | bytes 1572872 | tf_op jit(solution)/shard_map/ppermute | solution.py:67
  58.1 20.1 %collective-permute-start.8 = (bf16[128,2048]{1,0:T(8,128)(2,1)S(1)}, bf16[128,2048]{1,0:T(8,128)(2,1)S(1)}, u32[]{:S(2)}, u32[]{:S(2)}) collective-permute-start(bf16[128,2048]{1,0:T(8,128)(2,1)S(1)} %slice.211.refs_0_.refs_4_), channel_id=1, source_target_pairs={{0,16},{8,24},{16,0},{24,8},{1,17},{9,25},{17,1},{25,9},{2,18},{10... | collective-permute-start | bytes 1572872 | tf_op jit(solution)/shard_map/ppermute | solution.py:67
  59.6 29.9 %collective-permute-start.9 = (bf16[128,2048]{1,0:T(8,128)(2,1)S(1)}, bf16[128,2048]{1,0:T(8,128)(2,1)}, u32[]{:S(2)}, u32[]{:S(2)}) collective-permute-start(bf16[128,2048]{1,0:T(8,128)(2,1)S(1)} %slice.211.refs_0_.refs_4_), channel_id=1, source_target_pairs={{0,24},{8,16},{16,8},{24,0},{1,25},{9,17},{17,9},{25,1},{2,26},{10... | collective-permute-start | bytes 1572872 | tf_op jit(solution)/shard_map/ppermute | solution.py:67
  59.8 40.9 %copy-start.18 = (bf16[256,128]{1,0:T(8,128)(2,1)}, bf16[256,128]{1,0:T(8,128)(2,1)S(1)}, u32[]{:S(2)}) copy-start(bf16[256,128]{1,0:T(8,128)(2,1)S(1)} %and_convert_fusion.place) | copy-start | bytes 196612
  78.2 13.5 %copy-start.8 = (bf16[128,2048]{1,0:T(8,128)(2,1)}, bf16[128,2048]{1,0:T(8,128)(2,1)S(1)}, u32[]{:S(2)}) copy-start(bf16[128,2048]{1,0:T(8,128)(2,1)S(1)} %collective-permute-done.7.refs_1_.refs_5_) | copy-start | bytes 1572868
  91.7 16.7 %all-to-all-start.3 = ((bf16[4,64,2048]{2,1,0:T(8,128)(2,1)}), bf16[4,64,2048]{2,1,0:T(8,128)(2,1)S(1)}, u32[]{:S(2)}, u32[]{:S(2)}) async-start(bf16[4,64,2048]{2,1,0:T(8,128)(2,1)} %column_blocks.9), calls=%async_computation.3 | async-start | bytes 2097152 | tf_op jit(solution)/shard_map/all_to_all | solution.py:99
  95.3 102.8 %all-gather.11.cloned.1.call-start = ((), (), s32[]{:S(2)}) async-start(), calls=%async_computation.6 | async-start | bytes 9437184 | tf_op jit(solution)/shard_map/all_gather | solution.py:102
  111.7 21.4 %collective-permute-start.10 = (bf16[128,2048]{1,0:T(8,128)(2,1)S(1)}, bf16[128,2048]{1,0:T(8,128)(2,1)S(1)}, u32[]{:S(2)}, u32[]{:S(2)}) collective-permute-start(bf16[128,2048]{1,0:T(8,128)(2,1)S(1)} %bitcast.128), channel_id=1, source_target_pairs={{0,8},{8,0},{16,24},{24,16},{1,9},{9,1},{17,25},{25,17},{2,10},{10... | collective-permute-start | bytes 1572872 | tf_op jit(solution)/shard_map/ppermute | solution.py:67
  113.3 25.0 %collective-permute-start.11 = (bf16[128,2048]{1,0:T(8,128)(2,1)S(1)}, bf16[128,2048]{1,0:T(8,128)(2,1)S(1)}, u32[]{:S(2)}, u32[]{:S(2)}) collective-permute-start(bf16[128,2048]{1,0:T(8,128)(2,1)S(1)} %bitcast.129), channel_id=1, source_target_pairs={{0,16},{8,24},{16,0},{24,8},{1,17},{9,25},{17,1},{25,9},{2,18},{10... | collective-permute-start | bytes 1572872 | tf_op jit(solution)/shard_map/ppermute | solution.py:67
  114.7 23.6 %collective-permute-start.12 = (bf16[128,2048]{1,0:T(8,128)(2,1)S(1)}, bf16[128,2048]{1,0:T(8,128)(2,1)S(1)}, u32[]{:S(2)}, u32[]{:S(2)}) collective-permute-start(bf16[128,2048]{1,0:T(8,128)(2,1)S(1)} %bitcast.130), channel_id=1, source_target_pairs={{0,24},{8,16},{16,8},{24,0},{1,25},{9,17},{17,9},{25,1},{2,26},{10... | collective-permute-start | bytes 1572872 | tf_op jit(solution)/shard_map/ppermute | solution.py:67
  133.1 38.4 %copy-start.11 = (bf16[128,2048]{1,0:T(8,128)(2,1)}, bf16[128,2048]{1,0:T(8,128)(2,1)S(1)}, u32[]{:S(2)}) copy-start(bf16[128,2048]{1,0:T(8,128)(2,1)S(1)} %collective-permute-done.10.refs_5_.refs_14_) | copy-start | bytes 1572868
  138.3 33.2 %copy-start.12 = (bf16[128,2048]{1,0:T(8,128)(2,1)}, bf16[128,2048]{1,0:T(8,128)(2,1)S(1)}, u32[]{:S(2)}) copy-start(bf16[128,2048]{1,0:T(8,128)(2,1)S(1)} %collective-permute-done.11.refs_6_.refs_15_) | copy-start | bytes 1572868
  138.3 33.2 %copy-start.13 = (bf16[128,2048]{1,0:T(8,128)(2,1)}, bf16[128,2048]{1,0:T(8,128)(2,1)S(1)}, u32[]{:S(2)}) copy-start(bf16[128,2048]{1,0:T(8,128)(2,1)S(1)} %collective-permute-done.12.refs_7_.refs_16_) | copy-start | bytes 1572868
  138.3 16.5 %collective-permute-start.13 = (bf16[144,2048]{1,0:T(8,128)(2,1)}, bf16[144,2048]{1,0:T(8,128)(2,1)S(1)}, u32[]{:S(2)}, u32[]{:S(2)}) collective-permute-start(bf16[144,2048]{1,0:T(8,128)(2,1)} %get-tuple-element.113), channel_id=1, source_target_pairs={{0,8},{8,0},{16,24},{24,16},{1,9},{9,1},{17,25},{25,17},{2,10},{10... | collective-permute-start | bytes 1769480 | tf_op jit(solution)/shard_map/ppermute | solution.py:67
  139.5 27.4 %collective-permute-start.14 = (bf16[144,2048]{1,0:T(8,128)(2,1)}, bf16[144,2048]{1,0:T(8,128)(2,1)}, u32[]{:S(2)}, u32[]{:S(2)}) collective-permute-start(bf16[144,2048]{1,0:T(8,128)(2,1)} %get-tuple-element.114), channel_id=1, source_target_pairs={{0,16},{8,24},{16,0},{24,8},{1,17},{9,25},{17,1},{25,9},{2,18},{10... | collective-permute-start | bytes 1769480 | tf_op jit(solution)/shard_map/ppermute | solution.py:67
  140.4 26.5 %collective-permute-start.15 = (bf16[144,2048]{1,0:T(8,128)(2,1)}, bf16[144,2048]{1,0:T(8,128)(2,1)}, u32[]{:S(2)}, u32[]{:S(2)}) collective-permute-start(bf16[144,2048]{1,0:T(8,128)(2,1)} %get-tuple-element.115), channel_id=1, source_target_pairs={{0,24},{8,16},{16,8},{24,0},{1,25},{9,17},{17,9},{25,1},{2,26},{10... | collective-permute-start | bytes 1769480 | tf_op jit(solution)/shard_map/ppermute | solution.py:67
  142.5 9.5 %all-to-all-start.2 = ((f32[8,4,256]{2,1,0:T(4,128)}), f32[8,4,256]{2,1,0:T(4,128)S(1)}, u32[]{:S(2)}, u32[]{:S(2)}) async-start(f32[8,4,256]{2,1,0:T(4,128)} %fusion.23), calls=%async_computation.2 | async-start | bytes 65536 | tf_op jit(solution)/shard_map/all_to_all | solution.py:930
  145.8 132.2 %all-gather.13.cloned.1.call-start = ((), (), s32[]{:S(2)}) async-start(), calls=%async_computation.7 | async-start | bytes 9437184 | tf_op jit(solution)/shard_map/all_gather | solution.py:102
  171.5 16.5 %collective-permute-start.16 = (bf16[144,2048]{1,0:T(8,128)(2,1)}, bf16[144,2048]{1,0:T(8,128)(2,1)S(1)}, u32[]{:S(2)}, u32[]{:S(2)}) collective-permute-start(bf16[144,2048]{1,0:T(8,128)(2,1)} %get-tuple-element.117.refs_0_), channel_id=1, source_target_pairs={{0,8},{8,0},{16,24},{24,16},{1,9},{9,1},{17,25},{25,17},{2,10},{10... | collective-permute-start | bytes 1769480 | tf_op jit(solution)/shard_map/ppermute | solution.py:67
  172.2 25.8 %collective-permute-start.17 = (bf16[144,2048]{1,0:T(8,128)(2,1)}, bf16[144,2048]{1,0:T(8,128)(2,1)S(1)}, u32[]{:S(2)}, u32[]{:S(2)}) collective-permute-start(bf16[144,2048]{1,0:T(8,128)(2,1)} %get-tuple-element.117.refs_0_), channel_id=1, source_target_pairs={{0,16},{8,24},{16,0},{24,8},{1,17},{9,25},{17,1},{25,9},{2,18},{10... | collective-permute-start | bytes 1769480 | tf_op jit(solution)/shard_map/ppermute | solution.py:67
  173.6 24.4 %collective-permute-start.18 = (bf16[144,2048]{1,0:T(8,128)(2,1)}, bf16[144,2048]{1,0:T(8,128)(2,1)S(1)}, u32[]{:S(2)}, u32[]{:S(2)}) collective-permute-start(bf16[144,2048]{1,0:T(8,128)(2,1)} %get-tuple-element.117.refs_0_), channel_id=1, source_target_pairs={{0,24},{8,16},{16,8},{24,0},{1,25},{9,17},{17,9},{25,1},{2,26},{10... | collective-permute-start | bytes 1769480 | tf_op jit(solution)/shard_map/ppermute | solution.py:67
  198.0 177.4 %all-gather.15.cloned.1.call-start = ((), (), s32[]{:S(2)}) async-start(), calls=%async_computation.8 | async-start | bytes 9437184 | tf_op jit(solution)/shard_map/all_gather | solution.py:102
  213.1 16.5 %collective-permute-start.19 = (bf16[144,2048]{1,0:T(8,128)(2,1)}, bf16[144,2048]{1,0:T(8,128)(2,1)S(1)}, u32[]{:S(2)}, u32[]{:S(2)}) collective-permute-start(bf16[144,2048]{1,0:T(8,128)(2,1)} %get-tuple-element.122), channel_id=1, source_target_pairs={{0,8},{8,0},{16,24},{24,16},{1,9},{9,1},{17,25},{25,17},{2,10},{10... | collective-permute-start | bytes 1769480 | tf_op jit(solution)/shard_map/ppermute | solution.py:67
  214.2 24.7 %collective-permute-start.20 = (bf16[144,2048]{1,0:T(8,128)(2,1)}, bf16[144,2048]{1,0:T(8,128)(2,1)S(1)}, u32[]{:S(2)}, u32[]{:S(2)}) collective-permute-start(bf16[144,2048]{1,0:T(8,128)(2,1)} %get-tuple-element.123), channel_id=1, source_target_pairs={{0,16},{8,24},{16,0},{24,8},{1,17},{9,25},{17,1},{25,9},{2,18},{10... | collective-permute-start | bytes 1769480 | tf_op jit(solution)/shard_map/ppermute | solution.py:67
  215.0 24.0 %collective-permute-start.21 = (bf16[144,2048]{1,0:T(8,128)(2,1)}, bf16[144,2048]{1,0:T(8,128)(2,1)S(1)}, u32[]{:S(2)}, u32[]{:S(2)}) collective-permute-start(bf16[144,2048]{1,0:T(8,128)(2,1)} %get-tuple-element.124), channel_id=1, source_target_pairs={{0,24},{8,16},{16,8},{24,0},{1,25},{9,17},{17,9},{25,1},{2,26},{10... | collective-permute-start | bytes 1769480 | tf_op jit(solution)/shard_map/ppermute | solution.py:67
  244.5 15.8 %collective-permute-start.22 = (bf16[144,2048]{1,0:T(8,128)(2,1)}, bf16[144,2048]{1,0:T(8,128)(2,1)S(1)}, u32[]{:S(2)}, u32[]{:S(2)}) collective-permute-start(bf16[144,2048]{1,0:T(8,128)(2,1)} %get-tuple-element.155.refs_0_), channel_id=1, source_target_pairs={{0,8},{8,0},{16,24},{24,16},{1,9},{9,1},{17,25},{25,17},{2,10},{10... | collective-permute-start | bytes 1769480 | tf_op jit(solution)/shard_map/ppermute | solution.py:67
  244.9 23.4 %collective-permute-start.23 = (bf16[144,2048]{1,0:T(8,128)(2,1)}, bf16[144,2048]{1,0:T(8,128)(2,1)S(1)}, u32[]{:S(2)}, u32[]{:S(2)}) collective-permute-start(bf16[144,2048]{1,0:T(8,128)(2,1)} %get-tuple-element.155.refs_0_), channel_id=1, source_target_pairs={{0,16},{8,24},{16,0},{24,8},{1,17},{9,25},{17,1},{25,9},{2,18},{10... | collective-permute-start | bytes 1769480 | tf_op jit(solution)/shard_map/ppermute | solution.py:67
  246.1 22.2 %collective-permute-start.24 = (bf16[144,2048]{1,0:T(8,128)(2,1)}, bf16[144,2048]{1,0:T(8,128)(2,1)S(1)}, u32[]{:S(2)}, u32[]{:S(2)}) collective-permute-start(bf16[144,2048]{1,0:T(8,128)(2,1)} %get-tuple-element.155.refs_0_), channel_id=1, source_target_pairs={{0,24},{8,16},{16,8},{24,0},{1,25},{9,17},{17,9},{25,1},{2,26},{10... | collective-permute-start | bytes 1769480 | tf_op jit(solution)/shard_map/ppermute | solution.py:67
  260.4 18.4 %copy-start.5 = (bf16[144,2048]{1,0:T(8,128)(2,1)}, bf16[144,2048]{1,0:T(8,128)(2,1)S(1)}, u32[]{:S(2)}) copy-start(bf16[144,2048]{1,0:T(8,128)(2,1)S(1)} %collective-permute-done.22.refs_1_) | copy-start | bytes 1769476
  286.6 4.2 collective-permute-start.25
  288.2 4.1 collective-permute-start.26
  289.7 5.0 %collective-permute-start.27 = (f32[4,2048]{1,0:T(4,128)}, f32[4,2048]{1,0:T(4,128)S(1)}, u32[]{:S(2)}, u32[]{:S(2)}) collective-permute-start(f32[4,2048]{1,0:T(4,128)} %get-tuple-element.131.refs_0_), channel_id=1, source_target_pairs={{0,24},{8,16},{16,8},{24,0},{1,25},{9,17},{17,9},{25,1},{2,26},{10... | collective-permute-start | bytes 98312 | tf_op jit(solution)/shard_map/ppermute | solution.py:67
  301.9 11.1 %collective-permute-start.28 = (f32[4,2048]{1,0:T(4,128)}, f32[4,2048]{1,0:T(4,128)S(1)}, u32[]{:S(2)}, u32[]{:S(2)}) collective-permute-start(f32[4,2048]{1,0:T(4,128)} %get-tuple-element.149.refs_0_), channel_id=1, source_target_pairs={{0,8},{8,0},{16,24},{24,16},{1,9},{9,1},{17,25},{25,17},{2,10},{10... | collective-permute-start | bytes 98312 | tf_op jit(solution)/shard_map/ppermute | solution.py:67
  302.4 10.5 %collective-permute-start.29 = (f32[4,2048]{1,0:T(4,128)}, f32[4,2048]{1,0:T(4,128)S(1)}, u32[]{:S(2)}, u32[]{:S(2)}) collective-permute-start(f32[4,2048]{1,0:T(4,128)} %get-tuple-element.149.refs_0_), channel_id=1, source_target_pairs={{0,16},{8,24},{16,0},{24,8},{1,17},{9,25},{17,1},{25,9},{2,18},{10... | collective-permute-start | bytes 98312 | tf_op jit(solution)/shard_map/ppermute | solution.py:67
  303.0 10.0 %collective-permute-start.30 = (f32[4,2048]{1,0:T(4,128)}, f32[4,2048]{1,0:T(4,128)S(1)}, u32[]{:S(2)}, u32[]{:S(2)}) collective-permute-start(f32[4,2048]{1,0:T(4,128)} %get-tuple-element.149.refs_0_), channel_id=1, source_target_pairs={{0,24},{8,16},{16,8},{24,0},{1,25},{9,17},{17,9},{25,1},{2,26},{10... | collective-permute-start | bytes 98312 | tf_op jit(solution)/shard_map/ppermute | solution.py:67
  324.6 11.2 %collective-permute-start.31 = (bf16[4,12288]{1,0:T(4,128)(2,1)}, bf16[4,12288]{1,0:T(4,128)(2,1)S(1)}, u32[]{:S(2)}, u32[]{:S(2)}) collective-permute-start(bf16[4,12288]{1,0:T(4,128)(2,1)} %get-tuple-element.164.refs_0_), channel_id=1, source_target_pairs={{0,1},{1,0},{2,3},{3,2},{4,5},{5,4},{6,7},{7,6},{8,9},{9,8},{10,11... | collective-permute-start | bytes 294920 | tf_op jit(solution)/shard_map/ppermute | solution.py:73
  324.7 23.5 %collective-permute-start.34 = (bf16[32,2176]{1,0:T(8,128)(2,1)}, bf16[32,2176]{1,0:T(8,128)(2,1)S(1)}, u32[]{:S(2)}, u32[]{:S(2)}) collective-permute-start(bf16[32,2176]{1,0:T(8,128)(2,1)} %get-tuple-element.161), channel_id=1, source_target_pairs={{0,8},{8,0},{16,24},{24,16},{1,9},{9,1},{17,25},{25,17},{2,10},{10... | collective-permute-start | bytes 417800 | tf_op jit(solution)/shard_map/ppermute | solution.py:67
  325.3 23.0 %collective-permute-start.35 = (bf16[32,2176]{1,0:T(8,128)(2,1)}, bf16[32,2176]{1,0:T(8,128)(2,1)S(1)}, u32[]{:S(2)}, u32[]{:S(2)}) collective-permute-start(bf16[32,2176]{1,0:T(8,128)(2,1)} %get-tuple-element.162), channel_id=1, source_target_pairs={{0,16},{8,24},{16,0},{24,8},{1,17},{9,25},{17,1},{25,9},{2,18},{10... | collective-permute-start | bytes 417800 | tf_op jit(solution)/shard_map/ppermute | solution.py:67
  325.8 22.4 %collective-permute-start.36 = (bf16[32,2176]{1,0:T(8,128)(2,1)}, bf16[32,2176]{1,0:T(8,128)(2,1)S(1)}, u32[]{:S(2)}, u32[]{:S(2)}) collective-permute-start(bf16[32,2176]{1,0:T(8,128)(2,1)} %get-tuple-element.163), channel_id=1, source_target_pairs={{0,24},{8,16},{16,8},{24,0},{1,25},{9,17},{17,9},{25,1},{2,26},{10... | collective-permute-start | bytes 417800 | tf_op jit(solution)/shard_map/ppermute | solution.py:67
  328.3 19.9 %collective-permute-start.32 = (bf16[4,12288]{1,0:T(4,128)(2,1)}, bf16[4,12288]{1,0:T(4,128)(2,1)S(1)}, u32[]{:S(2)}, u32[]{:S(2)}) collective-permute-start(bf16[4,12288]{1,0:T(4,128)(2,1)} %get-tuple-element.164.refs_0_), channel_id=1, source_target_pairs={{0,2},{1,3},{2,0},{3,1},{4,6},{5,7},{6,4},{7,5},{8,10},{9,11},{10,... | collective-permute-start | bytes 294920 | tf_op jit(solution)/shard_map/ppermute | solution.py:73
  335.9 12.3 %copy-start.33 = (bf16[4,12288]{1,0:T(4,128)(2,1)}, bf16[4,12288]{1,0:T(4,128)(2,1)S(1)}, u32[]{:S(2)}) copy-start(bf16[4,12288]{1,0:T(4,128)(2,1)S(1)} %collective-permute-done.31.refs_1_) | copy-start | bytes 294916
  335.9 12.3 %collective-permute-start.33 = (bf16[4,12288]{1,0:T(4,128)(2,1)}, bf16[4,12288]{1,0:T(4,128)(2,1)S(1)}, u32[]{:S(2)}, u32[]{:S(2)}) collective-permute-start(bf16[4,12288]{1,0:T(4,128)(2,1)} %get-tuple-element.164.refs_0_), channel_id=1, source_target_pairs={{0,3},{1,2},{2,1},{3,0},{4,7},{5,6},{6,5},{7,4},{8,11},{9,10},{10,... | collective-permute-start | bytes 294920 | tf_op jit(solution)/shard_map/ppermute | solution.py:73
  350.7 6.6 %collective-permute-start.37 = (bf16[4,4,12288]{2,1,0:T(4,128)(2,1)}, bf16[4,4,12288]{2,1,0:T(4,128)(2,1)S(1)}, u32[]{:S(2)}, u32[]{:S(2)}) collective-permute-start(bf16[4,4,12288]{2,1,0:T(4,128)(2,1)} %stack.53.planes), channel_id=1, source_target_pairs={{0,4},{4,0},{1,5},{5,1},{2,6},{6,2},{3,7},{7,3},{8,12},{12,8},{9,1... | collective-permute-start | bytes 1179656 | tf_op jit(solution)/shard_map/ppermute | solution.py:70
  351.5 20.9 %all-to-all-start.4 = ((bf16[32,40,128]{2,1,0:T(8,128)(2,1)}), bf16[32,40,128]{2,1,0:T(8,128)(2,1)S(1)}, u32[]{:S(2)}, u32[]{:S(2)}) async-start(bf16[32,40,128]{2,1,0:T(8,128)(2,1)} %get-tuple-element.169), calls=%async_computation.4 | async-start | bytes 655360 | tf_op jit(solution)/shard_map/all_to_all | solution.py:91
  360.3 28.5 %collective-permute-start.41 = (bf16[32,5120]{1,0:T(8,128)(2,1)}, bf16[32,5120]{1,0:T(8,128)(2,1)S(1)}, u32[]{:S(2)}, u32[]{:S(2)}) collective-permute-start(bf16[32,5120]{1,0:T(8,128)(2,1)} %get-tuple-element.168.refs_0_), channel_id=1, source_target_pairs={{0,8},{8,0},{16,24},{24,16},{1,9},{9,1},{17,25},{25,17},{2,10},{10... | collective-permute-start | bytes 983048 | tf_op jit(solution)/shard_map/ppermute | solution.py:67
  362.2 33.7 %collective-permute-start.42 = (bf16[32,5120]{1,0:T(8,128)(2,1)}, bf16[32,5120]{1,0:T(8,128)(2,1)}, u32[]{:S(2)}, u32[]{:S(2)}) collective-permute-start(bf16[32,5120]{1,0:T(8,128)(2,1)} %get-tuple-element.168.refs_0_), channel_id=1, source_target_pairs={{0,16},{8,24},{16,0},{24,8},{1,17},{9,25},{17,1},{25,9},{2,18},{10... | collective-permute-start | bytes 983048 | tf_op jit(solution)/shard_map/ppermute | solution.py:67
  363.7 32.3 %collective-permute-start.43 = (bf16[32,5120]{1,0:T(8,128)(2,1)}, bf16[32,5120]{1,0:T(8,128)(2,1)}, u32[]{:S(2)}, u32[]{:S(2)}) collective-permute-start(bf16[32,5120]{1,0:T(8,128)(2,1)} %get-tuple-element.168.refs_0_), channel_id=1, source_target_pairs={{0,24},{8,16},{16,8},{24,0},{1,25},{9,17},{17,9},{25,1},{2,26},{10... | collective-permute-start | bytes 983048 | tf_op jit(solution)/shard_map/ppermute | solution.py:67
  385.5 16.4 %collective-permute-start.38 = (bf16[144,2048]{1,0:T(8,128)(2,1)}, bf16[144,2048]{1,0:T(8,128)(2,1)S(1)}, u32[]{:S(2)}, u32[]{:S(2)}) collective-permute-start(bf16[144,2048]{1,0:T(8,128)(2,1)} %get-tuple-element.174), channel_id=1, source_target_pairs={{0,8},{8,0},{16,24},{24,16},{1,9},{9,1},{17,25},{25,17},{2,10},{10... | collective-permute-start | bytes 1769480 | tf_op jit(solution)/shard_map/ppermute | solution.py:67
  387.0 28.1 %collective-permute-start.39 = (bf16[144,2048]{1,0:T(8,128)(2,1)}, bf16[144,2048]{1,0:T(8,128)(2,1)S(1)}, u32[]{:S(2)}, u32[]{:S(2)}) collective-permute-start(bf16[144,2048]{1,0:T(8,128)(2,1)} %get-tuple-element.175), channel_id=1, source_target_pairs={{0,16},{8,24},{16,0},{24,8},{1,17},{9,25},{17,1},{25,9},{2,18},{10... | collective-permute-start | bytes 1769480 | tf_op jit(solution)/shard_map/ppermute | solution.py:67
  388.7 26.4 %collective-permute-start.40 = (bf16[144,2048]{1,0:T(8,128)(2,1)}, bf16[144,2048]{1,0:T(8,128)(2,1)}, u32[]{:S(2)}, u32[]{:S(2)}) collective-permute-start(bf16[144,2048]{1,0:T(8,128)(2,1)} %get-tuple-element.176), channel_id=1, source_target_pairs={{0,24},{8,16},{16,8},{24,0},{1,25},{9,17},{17,9},{25,1},{2,26},{10... | collective-permute-start | bytes 1769480 | tf_op jit(solution)/shard_map/ppermute | solution.py:67
  395.3 19.8 %copy-start.17 = (f32[144,2048]{1,0:T(8,128)S(1)}, f32[144,2048]{1,0:T(8,128)}, u32[]{:S(2)}) copy-start(f32[144,2048]{1,0:T(8,128)} %get-tuple-element.125) | copy-start | bytes 3538948
  395.3 19.8 %copy-start.19 = (bf16[144,2048]{1,0:T(8,128)(2,1)S(1)}, bf16[144,2048]{1,0:T(8,128)(2,1)}, u32[]{:S(2)}) copy-start(bf16[144,2048]{1,0:T(8,128)(2,1)} %get-tuple-element.184) | copy-start | bytes 1769476
  (36 other events, 203.1 us)
Sparse Core Ops, SparseCore 0:
  27.5 82.3 all-gather.8
  112.1 81.2 all-gather.10
  198.2 79.8 all-gather.12
  279.5 95.8 all-gather.14

commit v2 on v1

--- a/solution.py
+++ b/solution.py
@@ -123,6 +123,20 @@
     )[0]
 
 
+def parts_kernel(tp, kinds, place, shard, *parts):
+    size = shard.shape[1] // (kinds * tp)
+    for j in range(tp):
+        for kind in range(kinds):
+            begin = pl.multiple_of((kind * tp + (place[0] ^ j)) * size, HDIM)
+            parts[j][:, kind * size : (kind + 1) * size] = shard[:, pl.ds(begin, size)]
+
+
+def assemble_kernel(tp, place, *refs):
+    parts, whole = refs[:tp], refs[tp]
+    for j in range(tp):
+        whole[place[0] ^ j] = parts[j][...]
+
+
 def block(weights, t, columns):
     part = weights[:, t, :, columns]
     return part.reshape(part.shape[0] * part.shape[1], part.shape[2])
@@ -161,13 +175,14 @@
 
 
 def self_kernel(tp, local, count, *refs):
-    entries, masked_entries, gathered = refs[:tp], refs[tp], refs[tp + 1]
-    partial = refs[tp + 2 : 2 * tp + 2]
-    packed, mix_out, probs_out, weight, held, mixed, sems = refs[2 * tp + 2 :]
+    entries, masked_entries, gathered, out_w = refs[:tp], refs[tp], refs[tp + 1], refs[tp + 2]
+    partial = refs[tp + 3 : 2 * tp + 3]
+    packed, mix_out, probs_out, weight, out_weight, held, mixed, sems = refs[2 * tp + 3 :]
     free, rows, span = entries[0].shape[0], packed.shape[1], local * HDIM
     pairs = [(ref, held.at[i * free : (i + 1) * free]) for i, ref in enumerate(entries)]
-    pairs += [(masked_entries, held.at[tp * free :]), (gathered, weight)]
-    for copy in start_copies(pairs, sems):
+    pairs += [(masked_entries, held.at[tp * free :]), (gathered, weight), (out_w, out_weight)]
+    copies = start_copies(pairs, sems)
+    for copy in copies[:-1]:
         copy.wait()
     for k in range(3):
         cols = slice(k * span, (k + 1) * span)
@@ -187,7 +202,14 @@
             mixture = mixture + one.astype(BF).astype(F32) * values[free : free + 1].astype(F32)
             mixed[i * rows : (i + 1) * rows, cols[0]] = mixture.astype(BF)
         mix_out[i] = mixed[i * rows + free : (i + 1) * rows]
-    write_out(tp, mixed, weight, partial)
+    copies[-1].wait()
+    rows = packed.shape[1]
+    for begin in range(0, partial[0].shape[1], 512):
+        cols = slice(begin, begin + 512)
+        part = out_weight[:, :, cols]
+        added = dot(mixed[...], part.reshape(-1, 512)).astype(BF)
+        for i in range(tp):
+            partial[i][:, cols] = added[i * rows : (i + 1) * rows]
 
 
 def write_out(tp, mixed, weight, partial):
@@ -415,15 +437,14 @@
 
 def self_back_kernel(
     tp, local, base, rows, gain, packed, probs, masked_entries, text_lefts, text_factors,
-    gain_a, embed, gain_m_row, gathered, *refs,
+    gain_a, embed, gain_m_row, gathered, out_w, *refs,
 ):
     parts, entries, text_sent = refs[:tp], refs[tp : 2 * tp], refs[2 * tp : 3 * tp]
     sent, refs = refs[3 * tp : 4 * tp], refs[4 * tp :]
-    payload, factors, weight, held, spreads, lefts, small, sems = refs
+    payload, factors, weight, out_weight, held, spreads, lefts, small, sems = refs
     width = lefts.shape[1]
-    span, free = weight.shape[3] // 4, entries[0].shape[0]
-    copy = pltpu.make_async_copy(gathered, weight, sems.at[0])
-    copy.start()
+    span, free = weight.shape[3] // 3, entries[0].shape[0]
+    copies = start_copies([(out_w, out_weight), (gathered, weight)], sems)
     ff = (text_factors.shape[1] - 5 * span - width) // 2
     cut = ff + 3 * span
     factors[:, :cut] = text_factors[:, :cut]
@@ -435,8 +456,9 @@
         row_back(parts, rows, gain, base, i, held, small.at[2:3])
     small[0:1] = held[0:1]
     factors[:, -width:] = held[:tp].astype(BF)
-    copy.wait()
-    mixed = out_back(held[...].astype(BF), weight, slice(3 * span, 4 * span))
+    copies[0].wait()
+    part = out_weight[...]
+    mixed = dot_t(held[...].astype(BF), part.reshape(span, width)).astype(BF).astype(F32)
     factors[:, cut : cut + span] = mixed[:tp].astype(BF)
     mask = head_mask(span)
     held[...] = jnp.zeros_like(held)
@@ -473,6 +495,7 @@
     value_spread = spreads[...].astype(BF)
     step = width // tp
     field, scale = normed(embed[...])
+    copies[1].wait()
     for t in range(tp):
         cols = slice(t * step, (t + 1) * step)
         keys = dot_t(key_spread, block(weight, t, slice(span, 2 * span))) * HDIM ** (-0.5)
@@ -594,22 +617,23 @@
     )(*operands)
 
 
-def self_forward(local, count, entries, masked_entries, gathered):
+def self_forward(local, count, entries, masked_entries, gathered, out_w):
     tp, (free, width) = len(entries), entries[0].shape
     span, rows = local * HDIM, free + PAD
     found = in_vmem(
         functools.partial(self_kernel, tp, local, count),
         "self_attention",
-        [*entries, masked_entries, gathered],
+        [*entries, masked_entries, gathered, out_w],
         [((rows, width), BF)] * tp
         + [((tp, rows, 3 * span), BF), ((tp, PAD, span), BF), ((tp, 8, free + TILE), F32)],
         [
             pltpu.VMEM(gathered.shape, BF),
+            pltpu.VMEM(out_w.shape, BF),
             pltpu.VMEM((tp * free + PAD, width), BF),
             pltpu.VMEM((tp * rows, span), BF),
-            pltpu.SemaphoreType.DMA((tp + 2,)),
-        ],
-        [(k, pl.ANY) for k in range(tp + 2)],
+            pltpu.SemaphoreType.DMA((tp + 3,)),
+        ],
+        [(k, pl.ANY) for k in range(tp + 3)],
     )
     return found[:tp], *found[tp:]
 
@@ -761,13 +785,13 @@
     return found[:tp], *found[tp:]
 
 
-def self_back(local, world, small_operands, gathered, parts, entries, text_sent):
+def self_back(local, world, small_operands, gathered, out_w, parts, entries, text_sent):
     tp, width = small_operands[0].shape
     text_lefts, text_factors = small_operands[6], small_operands[7]
     _, _, own, columns = gathered.shape
-    span, free = columns // 4, entries[0].shape[0]
+    span, free = columns // 3, entries[0].shape[0]
     count = 2 * tp * local + text_lefts.shape[0] + 8
-    operands = [*small_operands, gathered, *parts, *entries, *text_sent]
+    operands = [*small_operands, gathered, out_w, *parts, *entries, *text_sent]
     found = in_vmem(
         functools.partial(self_back_kernel, tp, local),
         "self_back",
@@ -776,13 +800,14 @@
         + [((world, count // 2, 2 * own), BF), ((tp, text_factors.shape[1] + 3 * span + width), BF)],
         [
             pltpu.VMEM(gathered.shape, BF),
+            pltpu.VMEM(out_w.shape, BF),
             pltpu.VMEM((8, width), F32),
             pltpu.VMEM((8 * tp, span), F32),
             pltpu.VMEM((count, width), F32),
             pltpu.VMEM((8, width), F32),
-            pltpu.SemaphoreType.DMA((1,)),
-        ],
-        ((len(small_operands), pl.ANY),),
+            pltpu.SemaphoreType.DMA((2,)),
+        ],
+        [(len(small_operands) + k, pl.ANY) for k in range(2)],
     )
     return found[:tp], *found[tp:]
 
@@ -881,22 +906,35 @@
 
     span = local * HDIM
 
-    qkv_sent = me.shuffle([(w_qkv, 3)])
-    attn_w = jnp.concatenate([qkv_sent, column_blocks(tp, [(w_attn_out, 1)])], axis=2)
-    attn_w = me.gather_blocks(attn_w)
-
-    def natural(value):
-        split = value.reshape(value.shape[:-1] + (2 * planes, tp, own))
-        return split.swapaxes(-3, -2).reshape(value.shape)
+    out_w = me.gather_blocks(w_attn_out)
+    corner = me.c * planes + me.z
+    place_at = jnp.stack([me.t, corner]).astype(jnp.int32)
+    in_smem = ((0, pltpu.SMEM),)
+    parts = in_vmem(
+        functools.partial(parts_kernel, tp, 3),
+        "parts",
+        [place_at, w_qkv],
+        [((own, 3 * span), BF)] * tp,
+        held=in_smem,
+    )
+    attn_sent = in_vmem(
+        functools.partial(assemble_kernel, tp),
+        "assemble",
+        [place_at, *me.to_owner(parts)],
+        [((tp, own, 3 * span), BF)],
+        held=in_smem,
+    )[0]
 
     cot_sum = jnp.sum(cotangent[0].astype(F32), axis=0)
     vectors = jnp.concatenate([mask_embed, gain_attn, gain_cross, gain_mlp]).astype(F32)
     fill = TILE - vectors.shape[0] % TILE
     length = jnp.broadcast_to(text_lengths.astype(F32), (fill,))
-    gathered = me.tp_direct(me.gather_cz(jnp.concatenate([cot_sum, vectors, length])))
-    others = after((w_cross_kv, w_cross_q, w_cross_out), (gathered, qkv_sent))
+    gathered = after(jnp.concatenate([cot_sum, vectors, length]), attn_sent)
+    gathered = me.tp_direct(me.gather_cz(gathered))
+    others = after((w_cross_kv, w_cross_q, w_cross_out), (gathered, attn_sent))
     kvq_sent = me.shuffle([(others[0], 2), (others[1], 1)])
     cross_sent = jnp.concatenate([kvq_sent, column_blocks(tp, [(others[2], 1)])], axis=2)
+    attn_w = me.gather_blocks(after(attn_sent, (out_w, gathered)))
     vectors = gathered[:, :, width : width + 4 * own].reshape(world, 4, own)
     vectors = xor_order(vectors, device, world).transpose(1, 0, 2).reshape(4, width)
     embed, gain_a, gain_c, gain_m = vectors[0], vectors[1], vectors[2], vectors[3]
@@ -938,7 +976,7 @@
     up_sent = me.shuffle([(after(w_up, (entries_all, kvq_sent)), 1)])
     cross_w = me.gather_blocks(after(cross_sent, (attn_w, entries_all, up_sent, place, masked_entries, text_bias)))
     partial, packed, mixed_one, probs_one = self_forward(
-        local, masked_count, entries_all, masked_entries, attn_w
+        local, masked_count, entries_all, masked_entries, attn_w, out_w
     )
     after_attn, cross_entries = join(after(start, (grad_active, place)), me.collect(after(tuple(partial), text_rows)), gain_c)
 
@@ -950,7 +988,8 @@
     after_cross, mlp_entries = join(after_attn, me.collect(partial), gain_m)
 
     mlp_all = me.spread(mlp_entries)
-    down = me.gather_blocks(after(w_down, (up, mlp_all)))
+    most = width * 3 // 4
+    down = me.gather_blocks(after(w_down[:, :most], (up, mlp_all)))
 
     active_one, grad_pre, grad_entry, mlp_one, cross_stream = mlp_back(
         mlp_all, jnp.pad(grad_active, ((0, PAD - tp), (0, 0))), up
@@ -994,13 +1033,13 @@
             grad_gain_m,
         ],
         attn_w,
+        out_w,
         me.tp_parts(grad_entry),
         entries_all,
         text_sent,
     )
     came = me.to_owner(sent)
 
-    corner = me.c * planes + me.z
     ff = grad_pre.shape[1]
     active = mlp_up(after(tuple(mlp_all), payload), up)
     pieces = [factors] + [me.other_plane(factors, k) for k in range(1, planes)]
@@ -1009,19 +1048,11 @@
     right, group = unpack(planes_of, me.other_core(planes_of), ff + 6 * span)
     right = [right] + [me.hop(right, j) for j in range(1, tp)]
 
-    def mine(stack):
-        size = stack.shape[1] // (2 * planes)
-        return lax.dynamic_slice_in_dim(stack, corner * size, size, axis=1)
-
-    cuts = [span, 2 * span, 2 * span + ff, 2 * span + ff + width]
-    mixed_f, cross_f, active_f, mid_f, attn_f = jnp.split(group, cuts, axis=1)
-    cot_f = gathered[:, :, :width].astype(BF).swapaxes(0, 1).reshape(world, width)
-    grad_w_out = dot_sum(mine(mixed_f), attn_f)
-    grad_w_cout = dot_sum(mine(cross_f), mid_f)
-    grad_w_down = dot_sum(mine(active_f), cot_f)
-    active = after(active, (right[0], lefts, grad_w_out, grad_w_cout, grad_w_down))
+    active, _ = lax.optimization_barrier((active, right[0]))
+    down_rest = me.gather_blocks(after(w_down[:, most:], (down, active)))
     partial = mlp_down(tp, active, down)
     collected = me.collect(partial)
+    active = after(active, tuple(partial))
 
     grad_tokens, grad_text = in_vmem(
         functools.partial(tokens_back_kernel, tp),
@@ -1029,6 +1060,9 @@
         [start, gain_a[None], pick.T, *after(tuple(came), partial)],
         [((seq, width), BF), ((txt, width), BF)],
     )
+
+    partial = mlp_down(tp, after(active, grad_tokens), down_rest)
+    collected_rest = me.collect(partial)
 
     heads = 2 * tp * local
     lefts = after(lefts, partial)
@@ -1045,18 +1079,29 @@
     small = jnp.sum(lefts[:, 2 * heads + 2 * tp :].astype(F32), axis=0)
     small = small[:4] + small[4:]
     entry_own = lax.dynamic_slice_in_dim(entries[free], device * own, own).astype(F32)
-    place_at = jnp.stack([me.t, corner]).astype(jnp.int32)
     grad_w_qkv, grad_w_kv, grad_w_cq, grad_w_up = in_vmem(
         functools.partial(columns_kernel, local),
         "columns",
         [place_at, attn_left, text_left, one_left, entry_own[:, None], *right],
         [((own, 3 * width), F32), ((own, 2 * width), F32), ((own, width), F32), ((own, tp * ff), F32)],
-        held=((0, pltpu.SMEM),),
-    )
-
-    collected = after(tuple(collected), (grad_tokens, grad_w_qkv, small))
-    output = sum(part.astype(F32) for part in collected)
-    output = dot(place, (after_cross + output).astype(BF)).astype(BF)
+        held=in_smem,
+    )
+
+    def mine(stack):
+        size = stack.shape[1] // (2 * planes)
+        return lax.dynamic_slice_in_dim(stack, corner * size, size, axis=1)
+
+    group = after(group, partial)
+    cuts = [span, 2 * span, 2 * span + ff, 2 * span + ff + width]
+    mixed_f, cross_f, active_f, mid_f, attn_f = jnp.split(group, cuts, axis=1)
+    cot_f = gathered[:, :, :width].astype(BF).swapaxes(0, 1).reshape(world, width)
+    grad_w_out = dot_sum(mine(mixed_f), attn_f)
+    grad_w_cout = dot_sum(mine(cross_f), mid_f)
+    grad_w_down = dot_sum(mine(active_f), cot_f)
+    collected_rest = after(tuple(collected_rest), (grad_w_qkv, grad_w_out, grad_w_cout, grad_w_down, small))
+    output = [sum(p.astype(F32) for p in parts) for parts in (collected, collected_rest)]
+    output = after_cross + jnp.concatenate(output, axis=1)
+    output = dot(place, output.astype(BF)).astype(BF)
     return (
         output,
         grad_tokens,

time: 431 us -> 426 us (0.988)
  waiting for transfers between devices: 184 us -> 169 us
  local copies, waits for them, and re-layouts: 18.7 us -> 25.9 us
    all_to_all x3 -> x2, waiting for transfers between devices: 16.9 us -> 7.88 us  [shuffle(): lax.all_to_all(column_blocks(self.tp, shards), 'tp', 0, 0, tiled=True)]
    ppermute x36 -> x42, starting transfers between devices: 42.7 us -> 50.6 us  [hop(): return lax.ppermute(value, 'tp', [(i, i ^ j) for i in range(self.tp)])]
    ppermute x36 -> x42, waiting for transfers between devices: 133 us -> 127 us  [hop(): return lax.ppermute(value, 'tp', [(i, i ^ j) for i in range(self.tp)])]
    all_to_all x3 -> x2, starting transfers between devices: 12.2 us -> 7.02 us  [shuffle(): lax.all_to_all(column_blocks(self.tp, shards), 'tp', 0, 0, tiled=True)]
    unnamed x94 -> x130, local copies, waits for them, and re-layouts: 6.03 us -> 9.13 us
    pallas_call x16 -> x17, Pallas kernels: 96.7 us -> 98.8 us  [in_vmem(): pl.pallas_call(kernel, in_specs=[pl.BlockSpec(memory_space=spaces.get(k,...]
    all_gather x4 -> x6, waiting for transfers between devices: 14.3 us -> 12.7 us  [gather_blocks(): return lax.all_gather(shard, ('core', 'fsdp'), axis=0)]
  transfers between devices with their start and end apart: 53 -> 60, of which waited for: 28 -> 30; matrix products, arithmetic and copies ran while one was open for 6% -> 8% of each run, Pallas kernels for 27% -> 28%
where the time goes in v2:
time: 426 us; the launch traced here: 420 us
  waiting for transfers between devices  169 us (40%)
  Pallas kernels  119 us (28%)
  starting transfers between devices  73 us (17%)
  local copies, waits for them, and re-layouts  25.9 us (6%)
  between operations  16.2 us (4%)
  other arithmetic  10.6 us (2%)
  matrix products  6.37 us (1%)
    ppermute x42, waiting for transfers between devices, hop(): return lax.ppermute(value, 'tp', [(i, i ^ j) for i in range(self.tp)])  127 us
    pallas_call x17, Pallas kernels, in_vmem(): pl.pallas_call(kernel, in_specs=[pl.BlockSpec(memory_space=spaces.get(k,...  98.8 us
    ppermute x42, starting transfers between devices, hop(): return lax.ppermute(value, 'tp', [(i, i ^ j) for i in range(self.tp)])  50.6 us
    all_gather x6, waiting for transfers between devices, gather_blocks(): return lax.all_gather(shard, ('core', 'fsdp'), axis=0)  12.7 us
    ppermute x6, waiting for transfers between devices, other_plane(): return lax.ppermute(value, 'fsdp', [(i, i ^ k) for i in range(self.planes)])  11.7 us
    pallas_call x1, Pallas kernels, mlp_up(): pl.pallas_call(functools.partial(up_kernel, tp), grid=(ff // step,), in_s...  11.2 us
    unnamed x130, local copies, waits for them, and re-layouts  9.13 us
    pallas_call x2, Pallas kernels, join(): pl.pallas_call(functools.partial(join_kernel, rows - PAD), grid=(rows //...  9.04 us
  transfers between devices with their start and end apart: 60, of which 30 were waited for; matrix products, arithmetic and copies ran while one was open for 8% of the time, Pallas kernels for 28%

profile of v2, /device:TPU:0, one launch (start us, length us, event | category | flops | bytes accessed | tf_op | source)
XLA Modules:
  0.0 420.2 jit_solution(14993932469048392019)
XLA Ops:
  8.6 2.1 parts.1
  10.7 2.9 collective-permute-start
  13.7 1.5 collective-permute-start.1
  16.1 3.5 collective-permute-done.refs_1_
  19.6 4.8 %collective-permute-done.1.refs_2_ = bf16[64,1536]{1,0:T(8,128)(2,1)S(1)} collective-permute-done((bf16[64,1536]{1,0:T(8,128)(2,1)}, bf16[64,1536]{1,0:T(8,128)(2,1)S(1)}, u32[]{:S(2)}, u32[]{:S(2)}) %collective-permute-start.1) | collective-permute-done | bytes 196640 | tf_op jit(solution)/shard_map/ppermute | solution.py:67
  25.2 2.2 assemble.1
  27.3 1.6 collective-permute-start.3
  28.9 2.6 collective-permute-start.4
  31.8 2.7 collective-permute-done.4
  34.6 2.7 collective-permute-done.5
  38.7 1.6 collective-permute-start.8
  43.2 2.0 collective-permute-done.7
  49.2 2.0 column_blocks.3
  53.8 3.5 all-to-all-start
  59.1 2.0 collective-permute-start.10
  64.1 1.7 column_blocks.4
  66.4 14.4 %collective-permute-done.10.refs_1_.refs_5_ = bf16[128,2048]{1,0:T(8,128)(2,1)S(1)} collective-permute-done((bf16[128,2048]{1,0:T(8,128)(2,1)S(1)}, bf16[128,2048]{1,0:T(8,128)(2,1)S(1)}, u32[]{:S(2)}, u32[]{:S(2)}) %collective-permute-start.10) | collective-permute-done | bytes 524320 | tf_op jit(solution)/shard_map/ppermute | solution.py:67
  81.6 9.8 %collective-permute-done.12.refs_3_.refs_7_ = bf16[128,2048]{1,0:T(8,128)(2,1)} collective-permute-done((bf16[128,2048]{1,0:T(8,128)(2,1)S(1)}, bf16[128,2048]{1,0:T(8,128)(2,1)}, u32[]{:S(2)}, u32[]{:S(2)}) %collective-permute-start.12) | collective-permute-done | bytes 524320 | tf_op jit(solution)/shard_map/ppermute | solution.py:67
  91.5 2.3 column_blocks.5
  93.7 3.5 all-to-all-start.2
  99.9 2.1 pad_maximum_fusion.1
  102.0 7.9 %all-to-all-done.2 = bf16[4,64,2048]{2,1,0:T(8,128)(2,1)S(1)} async-done(((bf16[4,64,2048]{2,1,0:T(8,128)(2,1)}), bf16[4,64,2048]{2,1,0:T(8,128)(2,1)S(1)}, u32[]{:S(2)}, u32[]{:S(2)}) %all-to-all-start.2) | async-done | bytes 1048608 | tf_op jit(solution)/shard_map/all_to_all | solution.py:99
  112.0 1.5 collective-permute-start.13
  114.0 1.5 collective-permute-start.15
  116.2 17.7 %self_attention.1 = (bf16[144,2048]{1,0:T(8,128)(2,1)}, bf16[144,2048]{1,0:T(8,128)(2,1)}, bf16[144,2048]{1,0:T(8,128)(2,1)}, bf16[144,2048]{1,0:T(8,128)(2,1)},...) custom-call(bf16[128,2048]{1,0:T(8,128)(2,1)} %copy-done.2, ...), custom_call_target="tpu_custom_call" | custom-call | flops 1 | bytes 1 | tf_op jit(solution)/shard_map/self_attention/pallas_call | solution.py:606
  133.9 3.4 collective-permute-done.14.refs_6_.refs_15_
  143.0 3.3 all-to-all-start.1
  147.8 6.4 %all-to-all-done.1 = f32[8,4,256]{2,1,0:T(4,128)S(1)} async-done(((f32[8,4,256]{2,1,0:T(4,128)}), f32[8,4,256]{2,1,0:T(4,128)S(1)}, u32[]{:S(2)}, u32[]{:S(2)}) %all-to-all-start.1) | async-done | bytes 32800 | tf_op jit(solution)/shard_map/all_to_all | solution.py:968
  154.6 11.7 %collective-permute-done.17.refs_2_ = bf16[144,2048]{1,0:T(8,128)(2,1)} collective-permute-done((bf16[144,2048]{1,0:T(8,128)(2,1)}, bf16[144,2048]{1,0:T(8,128)(2,1)}, u32[]{:S(2)}, u32[]{:S(2)}) %collective-permute-start.17) | collective-permute-done | bytes 589856 | tf_op jit(solution)/shard_map/ppermute | solution.py:67
  166.3 4.5 %join.2 = (f32[144,2048]{1,0:T(8,128)}, bf16[144,2048]{1,0:T(8,128)(2,1)}) custom-call(f32[144,2048]{1,0:T(8,128)} %get-tuple-element.125.base.rows, f32[1,2048]{1,0:T(1,128)} %slice.170.gain, bf16[144,2048]{1,0:T(8,128)(2,1)} %get-tuple-element.132.refs_0_, bf16[144,2048]{1,0:T(8,128)(2,1)} %copy-done.18, ...), custom_call_target="tpu_custom_call" | custom-call | flops 1 | bytes 1 | tf_op jit(solution)/shard_map/join/pallas_call | solution.py:858
  172.7 1.7 collective-permute-start.21
  174.4 13.0 %collective-permute-done.19.refs_1_ = bf16[144,2048]{1,0:T(8,128)(2,1)S(1)} collective-permute-done((bf16[144,2048]{1,0:T(8,128)(2,1)}, bf16[144,2048]{1,0:T(8,128)(2,1)S(1)}, u32[]{:S(2)}, u32[]{:S(2)}) %collective-permute-start.19) | collective-permute-done | bytes 589856 | tf_op jit(solution)/shard_map/ppermute | solution.py:67
  187.4 9.6 %collective-permute-done.20.refs_2_ = bf16[144,2048]{1,0:T(8,128)(2,1)S(1)} collective-permute-done((bf16[144,2048]{1,0:T(8,128)(2,1)}, bf16[144,2048]{1,0:T(8,128)(2,1)S(1)}, u32[]{:S(2)}, u32[]{:S(2)}) %collective-permute-start.20) | collective-permute-done | bytes 589856 | tf_op jit(solution)/shard_map/ppermute | solution.py:67
  198.0 13.8 %cross_attention.1 = (bf16[144,2048]{1,0:T(8,128)(2,1)}, bf16[144,2048]{1,0:T(8,128)(2,1)}, bf16[144,2048]{1,0:T(8,128)(2,1)}, bf16[144,2048]{1,0:T(8,128)(2,1)}...) custom-call(bf16[144,2048]{1,0:T(8,128)(2,1)} %get-tuple-element.137, ...), custom_call_target="tpu_custom_call" | custom-call | flops 1 | bytes 1 | tf_op jit(solution)/shard_map/cross_attention/pallas_call | solution.py:606
  213.7 1.7 collective-permute-start.24
  216.1 12.3 %collective-permute-done.22.refs_1_ = bf16[144,2048]{1,0:T(8,128)(2,1)S(1)} collective-permute-done((bf16[144,2048]{1,0:T(8,128)(2,1)}, bf16[144,2048]{1,0:T(8,128)(2,1)S(1)}, u32[]{:S(2)}, u32[]{:S(2)}) %collective-permute-start.22) | collective-permute-done | bytes 589856 | tf_op jit(solution)/shard_map/ppermute | solution.py:67
  228.4 9.5 %collective-permute-done.23.refs_2_ = bf16[144,2048]{1,0:T(8,128)(2,1)S(1)} collective-permute-done((bf16[144,2048]{1,0:T(8,128)(2,1)}, bf16[144,2048]{1,0:T(8,128)(2,1)S(1)}, u32[]{:S(2)}, u32[]{:S(2)}) %collective-permute-start.23) | collective-permute-done | bytes 589856 | tf_op jit(solution)/shard_map/ppermute | solution.py:67
  238.8 4.5 %join.3 = (f32[144,2048]{1,0:T(8,128)}, bf16[144,2048]{1,0:T(8,128)(2,1)}) custom-call(f32[144,2048]{1,0:T(8,128)} %get-tuple-element.136.base, f32[1,2048]{1,0:T(1,128)} %slice.175.gain, bf16[144,2048]{1,0:T(8,128)(2,1)} %get-tuple-element.141.refs_0_, bf16[144,2048]{1,0:T(8,128)(2,1)} %copy-done.19, bf16[144,2048]{1,0:T(8,128)(2,1)} %copy-done.20, ...), custom_call_target="tpu_custom_call" | custom-call | flops 1 | bytes 1 | tf_op jit(solution)/shard_map/join/pallas_call | solution.py:858
  244.9 1.9 collective-permute-start.27
  247.8 11.2 %collective-permute-done.25.refs_1_ = bf16[144,2048]{1,0:T(8,128)(2,1)S(1)} collective-permute-done((bf16[144,2048]{1,0:T(8,128)(2,1)}, bf16[144,2048]{1,0:T(8,128)(2,1)S(1)}, u32[]{:S(2)}, u32[]{:S(2)}) %collective-permute-start.25) | collective-permute-done | bytes 589856 | tf_op jit(solution)/shard_map/ppermute | solution.py:67
  259.0 8.3 %collective-permute-done.26.refs_2_ = bf16[144,2048]{1,0:T(8,128)(2,1)S(1)} collective-permute-done((bf16[144,2048]{1,0:T(8,128)(2,1)}, bf16[144,2048]{1,0:T(8,128)(2,1)S(1)}, u32[]{:S(2)}, u32[]{:S(2)}) %collective-permute-start.26) | collective-permute-done | bytes 589856 | tf_op jit(solution)/shard_map/ppermute | solution.py:67
  267.3 10.6 %all-gather.19.cloned.1.call-done = bf16[32,64,2048]{2,1,0:T(8,128)(2,1)} async-done(((bf16[4,64,2048]{2,1,0:T(8,128)(2,1)}), bf16[32,64,2048]{2,1,0:T(8,128)(2,1)}) %all-gather.19.cloned.1.call-update) | async-done | bytes 8388624 | tf_op jit(solution)/shard_map/all_gather | solution.py:102
  278.9 7.7 %mlp_back.1 = (bf16[16,2048]{1,0:T(8,128)(2,1)}, bf16[16,2048]{1,0:T(8,128)(2,1)}, f32[4,2048]{1,0:T(4,128)}, f32[4,2048]{1,0:T(4,128)}, f32[4,2048]{1,0:T(4,128)}) custom-call(bf16[144,2048]{1,0:T(8,128)(2,1)} %get-tuple-element.175.refs_0_, bf16[144,2048]{1,0:T(8,128)(2,1)} %copy-done.5, bf16[144,2048]{1,0:T(8,128)(2,1)} %copy-done.6, ...), custom_call_target="tpu_custom_call" | custom-call | flops 1 | bytes 1 | tf_op jit(solution)/shard_map/mlp_back/pallas_call | solution.py:606
  286.7 1.6 collective-permute-start.28
  292.4 2.4 collective-permute-done.30.refs_3_
  295.4 6.6 %cross_back.1 = (f32[4,2048]{1,0:T(4,128)}, f32[4,512]{1,0:T(4,128)}, f32[4,8,128]{2,1,0:T(8,128)}, f32[4,512]{1,0:T(4,128)}, f32[4,2048]{1,0:T(4,128)}, /*index=5*/f32[1,2048]{1,0:T(1,128)}) custom-call(f32[4,2048]{1,0:T(4,128)} %slice_bitcast_fusion.base, f32[4,2048]{1,0:T(4,128)} %get-tuple-element.148.rows, f32[1,2048]{1,0:T(1,128)} %slice.175.gain, ...), custom_call_target="tpu_custom_call" | custom-call | flops 1 | bytes 1 | tf_op jit(solution)/shard_map/cross_back/pallas_call | solution.py:606
  303.1 2.5 collective-permute-start.33
  306.9 6.2 %text_back.1 = (bf16[16,2176]{1,0:T(8,128)(2,1)}, bf16[16,2176]{1,0:T(8,128)(2,1)}, bf16[16,2176]{1,0:T(8,128)(2,1)}, bf16[16,2176]{1,0:T(8,128)(2,1)}, f32[40,2048]{1,0:T(8,128)}, /*index=5*/bf16[4,8704]{1,0:T(4,128)(2,1)}) custom-call(f32[4,8,128]{2,1,0:T(8,128)} %get-tuple-element.156.refs_0_, f32[4,8,128]{2,1,0:T(8,128)} %get-tuple-element.150.probs.refs_1_, ...), custom_call_target="tpu_custom_call" | custom-call | flops 1 | bytes 1 | tf_op jit(solution)/shard_map/text_back/pallas_call | solution.py:606
  313.8 9.2 %self_back.1 = (bf16[32,2176]{1,0:T(8,128)(2,1)}, bf16[32,2176]{1,0:T(8,128)(2,1)}, bf16[32,2176]{1,0:T(8,128)(2,1)}, bf16[32,2176]{1,0:T(8,128)(2,1)}, bf16[32,...) custom-call(f32[4,2048]{1,0:T(4,128)} %get-tuple-element.152.refs_12_.base, f32[4,2048]{1,0:T(4,128)} %get-tuple-element.153.rows, ...), custom_call_target="tpu_custom_call" | custom-call | flops 1 | bytes 1 | tf_op jit(solution)/shard_map/self_back/pallas_call | solution.py:606
  324.2 2.4 collective-permute-start.39
  327.8 6.3 %collective-permute-done.34.refs_1_ = bf16[4,12288]{1,0:T(4,128)(2,1)S(1)} collective-permute-done((bf16[4,12288]{1,0:T(4,128)(2,1)}, bf16[4,12288]{1,0:T(4,128)(2,1)S(1)}, u32[]{:S(2)}, u32[]{:S(2)}) %collective-permute-start.34) | collective-permute-done | bytes 98336 | tf_op jit(solution)/shard_map/ppermute | solution.py:73
  334.9 11.2 %mlp_up.1.active = bf16[576,2048]{1,0:T(8,128)(2,1)} custom-call(bf16[144,2048]{1,0:T(8,128)(2,1)} %get-tuple-element.175.refs_0_, bf16[144,2048]{1,0:T(8,128)(2,1)} %copy-done.5, bf16[144,2048]{1,0:T(8,128)(2,1)} %copy-done.6, bf16[144,2048]{1,0:T(8,128)(2,1)} %copy-done.7, bf16[8,4,64,2048]{3,2,1,0:T(8,128)(2,1)} %bitcast.124), custom_call_target="tpu_custom_call" | custom-call | flops 1 | bytes 1 | tf_op jit(solution)/shard_map/mlp_up/pallas_call | solution.py:700
  346.7 1.8 stack.53.planes
  351.2 2.2 unpack.1
  353.5 8.5 %mlp_down.2 = (bf16[144,1536]{1,0:T(8,128)(2,1)}, bf16[144,1536]{1,0:T(8,128)(2,1)}, bf16[144,1536]{1,0:T(8,128)(2,1)}, bf16[144,1536]{1,0:T(8,128)(2,1)}) custom-call(bf16[576,2048]{1,0:T(8,128)(2,1)} %mlp_up.1.active, bf16[8,256,1536]{2,1,0:T(8,128)(2,1)} %bitcast.129), custom_call_target="tpu_custom_call" | custom-call | flops 1 | bytes 1 | tf_op jit(solution)/shard_map/mlp_down/pallas_call | solution.py:606
  366.6 4.4 %all-to-all-start.3 = ((bf16[32,40,128]{2,1,0:T(8,128)(2,1)}), bf16[32,40,128]{2,1,0:T(8,128)(2,1)S(1)}, u32[]{:S(2)}, u32[]{:S(2)}) async-start(bf16[32,40,128]{2,1,0:T(8,128)(2,1)} %get-tuple-element.207), calls=%async_computation.3 | async-start | bytes 655360 | tf_op jit(solution)/shard_map/all_to_all | solution.py:91
  371.8 1.8 collective-permute-start.47
  375.1 4.2 %tokens_back.1 = (bf16[256,2048]{1,0:T(8,128)(2,1)}, bf16[128,2048]{1,0:T(8,128)(2,1)}) custom-call(f32[144,2048]{1,0:T(8,128)} %get-tuple-element.125.base.rows, f32[1,2048]{1,0:T(1,128)} %slice.179.gain_a.gain, bf16[256,128]{1,0:T(8,128)(2,1)} %copy-done.17, bf16[32,2176]{1,0:T(8,128)(2,1)} %get-tuple-element.196.refs_0_, bf16[32,2176]{1,0:T(8,128)(2,1)} %copy-done.38, ...), custom_call_target="tpu_custom_call" | custom-call | flops 1 | bytes 1 | tf_op jit(solution)/shard_map/tokens_back/pallas_call | solution.py:606
  379.6 8.0 %collective-permute-done.42 = bf16[144,1536]{1,0:T(8,128)(2,1)S(1)} collective-permute-done((bf16[144,1536]{1,0:T(8,128)(2,1)}, bf16[144,1536]{1,0:T(8,128)(2,1)S(1)}, u32[]{:S(2)}, u32[]{:S(2)}) %collective-permute-start.42) | collective-permute-done | bytes 442400 | tf_op jit(solution)/shard_map/ppermute | solution.py:67
  388.0 2.0 all-gather.23.cloned.1.call-done
  390.0 5.3 %mlp_down.3 = (bf16[144,512]{1,0:T(8,128)(2,1)}, bf16[144,512]{1,0:T(8,128)(2,1)}, bf16[144,512]{1,0:T(8,128)(2,1)}, bf16[144,512]{1,0:T(8,128)(2,1)}) custom-call(bf16[576,2048]{1,0:T(8,128)(2,1)} %mlp_up.1.active, bf16[8,256,512]{2,1,0:T(8,128)(2,1)} %bitcast.130), custom_call_target="tpu_custom_call" | custom-call | flops 1 | bytes 1 | tf_op jit(solution)/shard_map/mlp_down/pallas_call | solution.py:606
  395.3 1.5 collective-permute-start.44
  403.3 1.8 fusion.26
  405.7 5.2 %columns.1 = (f32[64,6144]{1,0:T(8,128)}, f32[64,4096]{1,0:T(8,128)}, f32[64,2048]{1,0:T(8,128)}, f32[64,8192]{1,0:T(8,128)}) custom-call(s32[2]{0:T(128)} %pad_add_fusion.place, bf16[4,2,4,32,64]{4,3,2,1,0:T(8,128)(2,1)} %bitcast.144, bf16[4,2,4,32,64]{4,3,2,1,0:T(8,128)(2,1)} %bitcast.145, bf16[4,2,32,64]{3,2,1,0:T(8,128)(2,1)} %bitcast.155, ...), custom_call_target="tpu_custom_call" | custom-call | flops 1 | bytes 1 | tf_op jit(solution)/shard_map/columns/pallas_call | solution.py:606
  (329 shorter events, 73.3 us)
Async XLA Ops:
  7.2 41.7 %copy-start = (bf16[256,2048]{1,0:T(8,128)(2,1)S(1)}, bf16[256,2048]{1,0:T(8,128)(2,1)}, u32[]{:S(2)}) copy-start(bf16[256,2048]{1,0:T(8,128)(2,1)} %param.16) | copy-start | bytes 3145732
  7.2 39.4 %all-gather.13.cloned.1.call-start = ((), (), s32[]{:S(2)}) async-start(), calls=%async_computation.4 | async-start | bytes 2359296 | tf_op jit(solution)/shard_map/all_gather | solution.py:102
  8.0 101.9 %all-gather.15.cloned.1.call-start = ((), (), s32[]{:S(2)}) async-start(), calls=%async_computation.5 | async-start | bytes 7077888 | tf_op jit(solution)/shard_map/all_gather | solution.py:102
  10.7 8.9 %collective-permute-start = (bf16[64,1536]{1,0:T(8,128)(2,1)}, bf16[64,1536]{1,0:T(8,128)(2,1)S(1)}, u32[]{:S(2)}, u32[]{:S(2)}) collective-permute-start(bf16[64,1536]{1,0:T(8,128)(2,1)} %get-tuple-element.118), channel_id=1, source_target_pairs={{0,8},{8,0},{16,24},{24,16},{1,9},{9,1},{17,25},{25,17},{2,10},{10... | collective-permute-start | bytes 589832 | tf_op jit(solution)/shard_map/ppermute | solution.py:67
  13.7 10.8 %collective-permute-start.1 = (bf16[64,1536]{1,0:T(8,128)(2,1)}, bf16[64,1536]{1,0:T(8,128)(2,1)S(1)}, u32[]{:S(2)}, u32[]{:S(2)}) collective-permute-start(bf16[64,1536]{1,0:T(8,128)(2,1)} %get-tuple-element.119), channel_id=1, source_target_pairs={{0,16},{8,24},{16,0},{24,8},{1,17},{9,25},{17,1},{25,9},{2,18},{10... | collective-permute-start | bytes 589832 | tf_op jit(solution)/shard_map/ppermute | solution.py:67
  15.2 9.3 %collective-permute-start.2 = (bf16[64,1536]{1,0:T(8,128)(2,1)}, bf16[64,1536]{1,0:T(8,128)(2,1)S(1)}, u32[]{:S(2)}, u32[]{:S(2)}) collective-permute-start(bf16[64,1536]{1,0:T(8,128)(2,1)} %get-tuple-element.120), channel_id=1, source_target_pairs={{0,24},{8,16},{16,8},{24,0},{1,25},{9,17},{17,9},{25,1},{2,26},{10... | collective-permute-start | bytes 589832 | tf_op jit(solution)/shard_map/ppermute | solution.py:67
  27.3 4.5 %collective-permute-start.3 = (f32[2432]{0:T(1024)S(1)}, f32[2432]{0:T(1024)S(1)}, u32[]{:S(2)}, u32[]{:S(2)}) collective-permute-start(f32[2432]{0:T(1024)S(1)} %pad_maximum_fusion.13), channel_id=1, source_target_pairs={{0,1},{1,0},{2,3},{3,2},{4,5},{5,4},{6,7},{7,6},{8,9},{9,8},{10,11... | collective-permute-start | bytes 29192 | tf_op jit(solution)/shard_map/ppermute | solution.py:73
  28.9 5.6 %collective-permute-start.4 = (f32[2432]{0:T(1024)S(1)}, f32[2432]{0:T(1024)S(1)}, u32[]{:S(2)}, u32[]{:S(2)}) collective-permute-start(f32[2432]{0:T(1024)S(1)} %pad_maximum_fusion.13), channel_id=1, source_target_pairs={{0,2},{1,3},{2,0},{3,1},{4,6},{5,7},{6,4},{7,5},{8,10},{9,11},{10,... | collective-permute-start | bytes 29192 | tf_op jit(solution)/shard_map/ppermute | solution.py:73
  31.5 5.7 %collective-permute-start.5 = (f32[2432]{0:T(1024)S(1)}, f32[2432]{0:T(1024)S(1)}, u32[]{:S(2)}, u32[]{:S(2)}) collective-permute-start(f32[2432]{0:T(1024)S(1)} %pad_maximum_fusion.13), channel_id=1, source_target_pairs={{0,3},{1,2},{2,1},{3,0},{4,7},{5,6},{6,5},{7,4},{8,11},{9,10},{10,... | collective-permute-start | bytes 29192 | tf_op jit(solution)/shard_map/ppermute | solution.py:73
  37.3 1.3 collective-permute-start.6
  38.7 4.5 %collective-permute-start.8 = (f32[8,2432]{1,0:T(8,128)S(1)}, f32[8,2432]{1,0:T(8,128)S(1)}, u32[]{:S(2)}, u32[]{:S(2)}) collective-permute-start(f32[8,2432]{1,0:T(8,128)S(1)} %concatenate.111), channel_id=1, source_target_pairs={{0,16},{8,24},{16,0},{24,8},{1,17},{9,25},{17,1},{25,9},{2,18},{10... | collective-permute-start | bytes 233480 | tf_op jit(solution)/shard_map/ppermute | solution.py:67
  40.2 5.0 %collective-permute-start.7 = (f32[8,2432]{1,0:T(8,128)S(1)}, f32[8,2432]{1,0:T(8,128)S(1)}, u32[]{:S(2)}, u32[]{:S(2)}) collective-permute-start(f32[8,2432]{1,0:T(8,128)S(1)} %concatenate.111), channel_id=1, source_target_pairs={{0,8},{8,0},{16,24},{24,16},{1,9},{9,1},{17,25},{25,17},{2,10},{10... | collective-permute-start | bytes 233480 | tf_op jit(solution)/shard_map/ppermute | solution.py:67
  40.8 5.5 %collective-permute-start.9 = (f32[8,2432]{1,0:T(8,128)S(1)}, f32[8,2432]{1,0:T(8,128)S(1)}, u32[]{:S(2)}, u32[]{:S(2)}) collective-permute-start(f32[8,2432]{1,0:T(8,128)S(1)} %concatenate.111), channel_id=1, source_target_pairs={{0,24},{8,16},{16,8},{24,0},{1,25},{9,17},{17,9},{25,1},{2,26},{10... | collective-permute-start | bytes 233480 | tf_op jit(solution)/shard_map/ppermute | solution.py:67
  53.8 37.6 %all-to-all-start = ((bf16[4,64,1536]{2,1,0:T(8,128)(2,1)}), bf16[4,64,1536]{2,1,0:T(8,128)(2,1)S(1)}, u32[]{:S(2)}, u32[]{:S(2)}) async-start(bf16[4,64,1536]{2,1,0:T(8,128)(2,1)} %column_blocks.3), calls=%async_computation | async-start | bytes 1572864 | tf_op jit(solution)/shard_map/all_to_all | solution.py:99
  59.1 34.6 %copy-start.2 = (bf16[128,2048]{1,0:T(8,128)(2,1)}, bf16[128,2048]{1,0:T(8,128)(2,1)S(1)}, u32[]{:S(2)}) copy-start(bf16[128,2048]{1,0:T(8,128)(2,1)S(1)} %slice.219.refs_0_.refs_4_) | copy-start | bytes 1572868
  59.1 21.7 %collective-permute-start.10 = (bf16[128,2048]{1,0:T(8,128)(2,1)S(1)}, bf16[128,2048]{1,0:T(8,128)(2,1)S(1)}, u32[]{:S(2)}, u32[]{:S(2)}) collective-permute-start(bf16[128,2048]{1,0:T(8,128)(2,1)S(1)} %slice.219.refs_0_.refs_4_), channel_id=1, source_target_pairs={{0,8},{8,0},{16,24},{24,16},{1,9},{9,1},{17,25},{25,17},{2,10},{10... | collective-permute-start | bytes 1572872 | tf_op jit(solution)/shard_map/ppermute | solution.py:67
  61.2 19.6 %collective-permute-start.11 = (bf16[128,2048]{1,0:T(8,128)(2,1)S(1)}, bf16[128,2048]{1,0:T(8,128)(2,1)S(1)}, u32[]{:S(2)}, u32[]{:S(2)}) collective-permute-start(bf16[128,2048]{1,0:T(8,128)(2,1)S(1)} %slice.219.refs_0_.refs_4_), channel_id=1, source_target_pairs={{0,16},{8,24},{16,0},{24,8},{1,17},{9,25},{17,1},{25,9},{2,18},{10... | collective-permute-start | bytes 1572872 | tf_op jit(solution)/shard_map/ppermute | solution.py:67
  62.6 28.8 %collective-permute-start.12 = (bf16[128,2048]{1,0:T(8,128)(2,1)S(1)}, bf16[128,2048]{1,0:T(8,128)(2,1)}, u32[]{:S(2)}, u32[]{:S(2)}) collective-permute-start(bf16[128,2048]{1,0:T(8,128)(2,1)S(1)} %slice.219.refs_0_.refs_4_), channel_id=1, source_target_pairs={{0,24},{8,16},{16,8},{24,0},{1,25},{9,17},{17,9},{25,1},{2,26},{10... | collective-permute-start | bytes 1572872 | tf_op jit(solution)/shard_map/ppermute | solution.py:67
  93.7 16.1 %all-to-all-start.2 = ((bf16[4,64,2048]{2,1,0:T(8,128)(2,1)}), bf16[4,64,2048]{2,1,0:T(8,128)(2,1)S(1)}, u32[]{:S(2)}, u32[]{:S(2)}) async-start(bf16[4,64,2048]{2,1,0:T(8,128)(2,1)} %column_blocks.5), calls=%async_computation.2 | async-start | bytes 2097152 | tf_op jit(solution)/shard_map/all_to_all | solution.py:99
  97.3 99.7 %all-gather.17.cloned.1.call-start = ((), (), s32[]{:S(2)}) async-start(), calls=%async_computation.6 | async-start | bytes 9437184 | tf_op jit(solution)/shard_map/all_gather | solution.py:102
  112.0 21.9 %collective-permute-start.13 = (bf16[128,2048]{1,0:T(8,128)(2,1)S(1)}, bf16[128,2048]{1,0:T(8,128)(2,1)S(1)}, u32[]{:S(2)}, u32[]{:S(2)}) collective-permute-start(bf16[128,2048]{1,0:T(8,128)(2,1)S(1)} %bitcast.133), channel_id=1, source_target_pairs={{0,8},{8,0},{16,24},{24,16},{1,9},{9,1},{17,25},{25,17},{2,10},{10... | collective-permute-start | bytes 1572872 | tf_op jit(solution)/shard_map/ppermute | solution.py:67
  113.5 23.8 %collective-permute-start.14 = (bf16[128,2048]{1,0:T(8,128)(2,1)S(1)}, bf16[128,2048]{1,0:T(8,128)(2,1)S(1)}, u32[]{:S(2)}, u32[]{:S(2)}) collective-permute-start(bf16[128,2048]{1,0:T(8,128)(2,1)S(1)} %bitcast.134), channel_id=1, source_target_pairs={{0,16},{8,24},{16,0},{24,8},{1,17},{9,25},{17,1},{25,9},{2,18},{10... | collective-permute-start | bytes 1572872 | tf_op jit(solution)/shard_map/ppermute | solution.py:67
  114.0 23.2 %collective-permute-start.15 = (bf16[128,2048]{1,0:T(8,128)(2,1)S(1)}, bf16[128,2048]{1,0:T(8,128)(2,1)S(1)}, u32[]{:S(2)}, u32[]{:S(2)}) collective-permute-start(bf16[128,2048]{1,0:T(8,128)(2,1)S(1)} %bitcast.135), channel_id=1, source_target_pairs={{0,24},{8,16},{16,8},{24,0},{1,25},{9,17},{17,9},{25,1},{2,26},{10... | collective-permute-start | bytes 1572872 | tf_op jit(solution)/shard_map/ppermute | solution.py:67
  133.9 37.0 %copy-start.11 = (bf16[128,2048]{1,0:T(8,128)(2,1)}, bf16[128,2048]{1,0:T(8,128)(2,1)S(1)}, u32[]{:S(2)}) copy-start(bf16[128,2048]{1,0:T(8,128)(2,1)S(1)} %collective-permute-done.13.refs_5_.refs_14_) | copy-start | bytes 1572868
  137.3 33.6 %copy-start.12 = (bf16[128,2048]{1,0:T(8,128)(2,1)}, bf16[128,2048]{1,0:T(8,128)(2,1)S(1)}, u32[]{:S(2)}) copy-start(bf16[128,2048]{1,0:T(8,128)(2,1)S(1)} %collective-permute-done.14.refs_6_.refs_15_) | copy-start | bytes 1572868
  138.1 16.5 %collective-permute-start.16 = (bf16[144,2048]{1,0:T(8,128)(2,1)}, bf16[144,2048]{1,0:T(8,128)(2,1)S(1)}, u32[]{:S(2)}, u32[]{:S(2)}) collective-permute-start(bf16[144,2048]{1,0:T(8,128)(2,1)} %get-tuple-element.133), channel_id=1, source_target_pairs={{0,8},{8,0},{16,24},{24,16},{1,9},{9,1},{17,25},{25,17},{2,10},{10... | collective-permute-start | bytes 1769480 | tf_op jit(solution)/shard_map/ppermute | solution.py:67
  139.3 27.1 %collective-permute-start.17 = (bf16[144,2048]{1,0:T(8,128)(2,1)}, bf16[144,2048]{1,0:T(8,128)(2,1)}, u32[]{:S(2)}, u32[]{:S(2)}) collective-permute-start(bf16[144,2048]{1,0:T(8,128)(2,1)} %get-tuple-element.134), channel_id=1, source_target_pairs={{0,16},{8,24},{16,0},{24,8},{1,17},{9,25},{17,1},{25,9},{2,18},{10... | collective-permute-start | bytes 1769480 | tf_op jit(solution)/shard_map/ppermute | solution.py:67
  140.1 26.2 %collective-permute-start.18 = (bf16[144,2048]{1,0:T(8,128)(2,1)}, bf16[144,2048]{1,0:T(8,128)(2,1)}, u32[]{:S(2)}, u32[]{:S(2)}) collective-permute-start(bf16[144,2048]{1,0:T(8,128)(2,1)} %get-tuple-element.135), channel_id=1, source_target_pairs={{0,24},{8,16},{16,8},{24,0},{1,25},{9,17},{17,9},{25,1},{2,26},{10... | collective-permute-start | bytes 1769480 | tf_op jit(solution)/shard_map/ppermute | solution.py:67
  143.0 11.2 %all-to-all-start.1 = ((f32[8,4,256]{2,1,0:T(4,128)}), f32[8,4,256]{2,1,0:T(4,128)S(1)}, u32[]{:S(2)}, u32[]{:S(2)}) async-start(f32[8,4,256]{2,1,0:T(4,128)} %fusion.25), calls=%async_computation.1 | async-start | bytes 65536 | tf_op jit(solution)/shard_map/all_to_all | solution.py:968
  146.4 131.6 %all-gather.19.cloned.1.call-start = ((), (), s32[]{:S(2)}) async-start(), calls=%async_computation.7 | async-start | bytes 9437184 | tf_op jit(solution)/shard_map/all_gather | solution.py:102
  170.9 16.5 %collective-permute-start.19 = (bf16[144,2048]{1,0:T(8,128)(2,1)}, bf16[144,2048]{1,0:T(8,128)(2,1)S(1)}, u32[]{:S(2)}, u32[]{:S(2)}) collective-permute-start(bf16[144,2048]{1,0:T(8,128)(2,1)} %get-tuple-element.137.refs_0_), channel_id=1, source_target_pairs={{0,8},{8,0},{16,24},{24,16},{1,9},{9,1},{17,25},{25,17},{2,10},{10... | collective-permute-start | bytes 1769480 | tf_op jit(solution)/shard_map/ppermute | solution.py:67
  171.2 25.7 %collective-permute-start.20 = (bf16[144,2048]{1,0:T(8,128)(2,1)}, bf16[144,2048]{1,0:T(8,128)(2,1)S(1)}, u32[]{:S(2)}, u32[]{:S(2)}) collective-permute-start(bf16[144,2048]{1,0:T(8,128)(2,1)} %get-tuple-element.137.refs_0_), channel_id=1, source_target_pairs={{0,16},{8,24},{16,0},{24,8},{1,17},{9,25},{17,1},{25,9},{2,18},{10... | collective-permute-start | bytes 1769480 | tf_op jit(solution)/shard_map/ppermute | solution.py:67
  172.7 24.3 %collective-permute-start.21 = (bf16[144,2048]{1,0:T(8,128)(2,1)}, bf16[144,2048]{1,0:T(8,128)(2,1)S(1)}, u32[]{:S(2)}, u32[]{:S(2)}) collective-permute-start(bf16[144,2048]{1,0:T(8,128)(2,1)} %get-tuple-element.137.refs_0_), channel_id=1, source_target_pairs={{0,24},{8,16},{16,8},{24,0},{1,25},{9,17},{17,9},{25,1},{2,26},{10... | collective-permute-start | bytes 1769480 | tf_op jit(solution)/shard_map/ppermute | solution.py:67
  197.0 156.4 %all-gather.21.cloned.1.call-start = ((), (), s32[]{:S(2)}) async-start(), calls=%async_computation.8 | async-start | bytes 7077888 | tf_op jit(solution)/shard_map/all_gather | solution.py:102
  211.8 16.5 %collective-permute-start.22 = (bf16[144,2048]{1,0:T(8,128)(2,1)}, bf16[144,2048]{1,0:T(8,128)(2,1)S(1)}, u32[]{:S(2)}, u32[]{:S(2)}) collective-permute-start(bf16[144,2048]{1,0:T(8,128)(2,1)} %get-tuple-element.142), channel_id=1, source_target_pairs={{0,8},{8,0},{16,24},{24,16},{1,9},{9,1},{17,25},{25,17},{2,10},{10... | collective-permute-start | bytes 1769480 | tf_op jit(solution)/shard_map/ppermute | solution.py:67
  212.9 24.9 %collective-permute-start.23 = (bf16[144,2048]{1,0:T(8,128)(2,1)}, bf16[144,2048]{1,0:T(8,128)(2,1)S(1)}, u32[]{:S(2)}, u32[]{:S(2)}) collective-permute-start(bf16[144,2048]{1,0:T(8,128)(2,1)} %get-tuple-element.143), channel_id=1, source_target_pairs={{0,16},{8,24},{16,0},{24,8},{1,17},{9,25},{17,1},{25,9},{2,18},{10... | collective-permute-start | bytes 1769480 | tf_op jit(solution)/shard_map/ppermute | solution.py:67
  213.7 24.2 %collective-permute-start.24 = (bf16[144,2048]{1,0:T(8,128)(2,1)}, bf16[144,2048]{1,0:T(8,128)(2,1)S(1)}, u32[]{:S(2)}, u32[]{:S(2)}) collective-permute-start(bf16[144,2048]{1,0:T(8,128)(2,1)} %get-tuple-element.144), channel_id=1, source_target_pairs={{0,24},{8,16},{16,8},{24,0},{1,25},{9,17},{17,9},{25,1},{2,26},{10... | collective-permute-start | bytes 1769480 | tf_op jit(solution)/shard_map/ppermute | solution.py:67
  243.4 15.7 %collective-permute-start.25 = (bf16[144,2048]{1,0:T(8,128)(2,1)}, bf16[144,2048]{1,0:T(8,128)(2,1)S(1)}, u32[]{:S(2)}, u32[]{:S(2)}) collective-permute-start(bf16[144,2048]{1,0:T(8,128)(2,1)} %get-tuple-element.175.refs_0_), channel_id=1, source_target_pairs={{0,8},{8,0},{16,24},{24,16},{1,9},{9,1},{17,25},{25,17},{2,10},{10... | collective-permute-start | bytes 1769480 | tf_op jit(solution)/shard_map/ppermute | solution.py:67
  243.7 23.6 %collective-permute-start.26 = (bf16[144,2048]{1,0:T(8,128)(2,1)}, bf16[144,2048]{1,0:T(8,128)(2,1)S(1)}, u32[]{:S(2)}, u32[]{:S(2)}) collective-permute-start(bf16[144,2048]{1,0:T(8,128)(2,1)} %get-tuple-element.175.refs_0_), channel_id=1, source_target_pairs={{0,16},{8,24},{16,0},{24,8},{1,17},{9,25},{17,1},{25,9},{2,18},{10... | collective-permute-start | bytes 1769480 | tf_op jit(solution)/shard_map/ppermute | solution.py:67
  244.9 22.4 %collective-permute-start.27 = (bf16[144,2048]{1,0:T(8,128)(2,1)}, bf16[144,2048]{1,0:T(8,128)(2,1)S(1)}, u32[]{:S(2)}, u32[]{:S(2)}) collective-permute-start(bf16[144,2048]{1,0:T(8,128)(2,1)} %get-tuple-element.175.refs_0_), channel_id=1, source_target_pairs={{0,24},{8,16},{16,8},{24,0},{1,25},{9,17},{17,9},{25,1},{2,26},{10... | collective-permute-start | bytes 1769480 | tf_op jit(solution)/shard_map/ppermute | solution.py:67
  278.0 112.0 %all-gather.23.cloned.1.call-start = ((), (), s32[]{:S(2)}) async-start(), calls=%async_computation.9 | async-start | bytes 2359296 | tf_op jit(solution)/shard_map/all_gather | solution.py:102
  286.7 4.9 %collective-permute-start.28 = (f32[4,2048]{1,0:T(4,128)}, f32[4,2048]{1,0:T(4,128)S(1)}, u32[]{:S(2)}, u32[]{:S(2)}) collective-permute-start(f32[4,2048]{1,0:T(4,128)} %get-tuple-element.151.refs_0_), channel_id=1, source_target_pairs={{0,8},{8,0},{16,24},{24,16},{1,9},{9,1},{17,25},{25,17},{2,10},{10... | collective-permute-start | bytes 98312 | tf_op jit(solution)/shard_map/ppermute | solution.py:67
  288.2 4.1 collective-permute-start.29
  289.7 5.0 %collective-permute-start.30 = (f32[4,2048]{1,0:T(4,128)}, f32[4,2048]{1,0:T(4,128)S(1)}, u32[]{:S(2)}, u32[]{:S(2)}) collective-permute-start(f32[4,2048]{1,0:T(4,128)} %get-tuple-element.151.refs_0_), channel_id=1, source_target_pairs={{0,24},{8,16},{16,8},{24,0},{1,25},{9,17},{17,9},{25,1},{2,26},{10... | collective-permute-start | bytes 98312 | tf_op jit(solution)/shard_map/ppermute | solution.py:67
  302.0 11.1 %collective-permute-start.31 = (f32[4,2048]{1,0:T(4,128)}, f32[4,2048]{1,0:T(4,128)S(1)}, u32[]{:S(2)}, u32[]{:S(2)}) collective-permute-start(f32[4,2048]{1,0:T(4,128)} %get-tuple-element.169.refs_0_), channel_id=1, source_target_pairs={{0,8},{8,0},{16,24},{24,16},{1,9},{9,1},{17,25},{25,17},{2,10},{10... | collective-permute-start | bytes 98312 | tf_op jit(solution)/shard_map/ppermute | solution.py:67
  302.6 10.5 %collective-permute-start.32 = (f32[4,2048]{1,0:T(4,128)}, f32[4,2048]{1,0:T(4,128)S(1)}, u32[]{:S(2)}, u32[]{:S(2)}) collective-permute-start(f32[4,2048]{1,0:T(4,128)} %get-tuple-element.169.refs_0_), channel_id=1, source_target_pairs={{0,16},{8,24},{16,0},{24,8},{1,17},{9,25},{17,1},{25,9},{2,18},{10... | collective-permute-start | bytes 98312 | tf_op jit(solution)/shard_map/ppermute | solution.py:67
  303.1 10.0 %collective-permute-start.33 = (f32[4,2048]{1,0:T(4,128)}, f32[4,2048]{1,0:T(4,128)S(1)}, u32[]{:S(2)}, u32[]{:S(2)}) collective-permute-start(f32[4,2048]{1,0:T(4,128)} %get-tuple-element.169.refs_0_), channel_id=1, source_target_pairs={{0,24},{8,16},{16,8},{24,0},{1,25},{9,17},{17,9},{25,1},{2,26},{10... | collective-permute-start | bytes 98312 | tf_op jit(solution)/shard_map/ppermute | solution.py:67
  323.0 11.0 %collective-permute-start.34 = (bf16[4,12288]{1,0:T(4,128)(2,1)}, bf16[4,12288]{1,0:T(4,128)(2,1)S(1)}, u32[]{:S(2)}, u32[]{:S(2)}) collective-permute-start(bf16[4,12288]{1,0:T(4,128)(2,1)} %get-tuple-element.184.refs_0_), channel_id=1, source_target_pairs={{0,1},{1,0},{2,3},{3,2},{4,5},{5,4},{6,7},{7,6},{8,9},{9,8},{10,11... | collective-permute-start | bytes 294920 | tf_op jit(solution)/shard_map/ppermute | solution.py:73
  323.1 23.0 %collective-permute-start.37 = (bf16[32,2176]{1,0:T(8,128)(2,1)}, bf16[32,2176]{1,0:T(8,128)(2,1)S(1)}, u32[]{:S(2)}, u32[]{:S(2)}) collective-permute-start(bf16[32,2176]{1,0:T(8,128)(2,1)} %get-tuple-element.181), channel_id=1, source_target_pairs={{0,8},{8,0},{16,24},{24,16},{1,9},{9,1},{17,25},{25,17},{2,10},{10... | collective-permute-start | bytes 417800 | tf_op jit(solution)/shard_map/ppermute | solution.py:67
  323.7 22.4 %collective-permute-start.38 = (bf16[32,2176]{1,0:T(8,128)(2,1)}, bf16[32,2176]{1,0:T(8,128)(2,1)S(1)}, u32[]{:S(2)}, u32[]{:S(2)}) collective-permute-start(bf16[32,2176]{1,0:T(8,128)(2,1)} %get-tuple-element.182), channel_id=1, source_target_pairs={{0,16},{8,24},{16,0},{24,8},{1,17},{9,25},{17,1},{25,9},{2,18},{10... | collective-permute-start | bytes 417800 | tf_op jit(solution)/shard_map/ppermute | solution.py:67
  324.2 21.9 %collective-permute-start.39 = (bf16[32,2176]{1,0:T(8,128)(2,1)}, bf16[32,2176]{1,0:T(8,128)(2,1)S(1)}, u32[]{:S(2)}, u32[]{:S(2)}) collective-permute-start(bf16[32,2176]{1,0:T(8,128)(2,1)} %get-tuple-element.183), channel_id=1, source_target_pairs={{0,24},{8,16},{16,8},{24,0},{1,25},{9,17},{17,9},{25,1},{2,26},{10... | collective-permute-start | bytes 417800 | tf_op jit(solution)/shard_map/ppermute | solution.py:67
  326.6 19.4 %collective-permute-start.35 = (bf16[4,12288]{1,0:T(4,128)(2,1)}, bf16[4,12288]{1,0:T(4,128)(2,1)S(1)}, u32[]{:S(2)}, u32[]{:S(2)}) collective-permute-start(bf16[4,12288]{1,0:T(4,128)(2,1)} %get-tuple-element.184.refs_0_), channel_id=1, source_target_pairs={{0,2},{1,3},{2,0},{3,1},{4,6},{5,7},{6,4},{7,5},{8,10},{9,11},{10,... | collective-permute-start | bytes 294920 | tf_op jit(solution)/shard_map/ppermute | solution.py:73
  334.0 12.0 %collective-permute-start.36 = (bf16[4,12288]{1,0:T(4,128)(2,1)}, bf16[4,12288]{1,0:T(4,128)(2,1)S(1)}, u32[]{:S(2)}, u32[]{:S(2)}) collective-permute-start(bf16[4,12288]{1,0:T(4,128)(2,1)} %get-tuple-element.184.refs_0_), channel_id=1, source_target_pairs={{0,3},{1,2},{2,1},{3,0},{4,7},{5,6},{6,5},{7,4},{8,11},{9,10},{10,... | collective-permute-start | bytes 294920 | tf_op jit(solution)/shard_map/ppermute | solution.py:73
  348.5 1.9 collective-permute-start.40
  362.0 17.3 %collective-permute-start.43 = (bf16[144,1536]{1,0:T(8,128)(2,1)}, bf16[144,1536]{1,0:T(8,128)(2,1)S(1)}, u32[]{:S(2)}, u32[]{:S(2)}) collective-permute-start(bf16[144,1536]{1,0:T(8,128)(2,1)} %get-tuple-element.194), channel_id=1, source_target_pairs={{0,24},{8,16},{16,8},{24,0},{1,25},{9,17},{17,9},{25,1},{2,26},{10... | collective-permute-start | bytes 1327112 | tf_op jit(solution)/shard_map/ppermute | solution.py:67
  363.2 24.5 %collective-permute-start.42 = (bf16[144,1536]{1,0:T(8,128)(2,1)}, bf16[144,1536]{1,0:T(8,128)(2,1)S(1)}, u32[]{:S(2)}, u32[]{:S(2)}) collective-permute-start(bf16[144,1536]{1,0:T(8,128)(2,1)} %get-tuple-element.193), channel_id=1, source_target_pairs={{0,16},{8,24},{16,0},{24,8},{1,17},{9,25},{17,1},{25,9},{2,18},{10... | collective-permute-start | bytes 1327112 | tf_op jit(solution)/shard_map/ppermute | solution.py:67
  364.6 23.1 %collective-permute-start.41 = (bf16[144,1536]{1,0:T(8,128)(2,1)}, bf16[144,1536]{1,0:T(8,128)(2,1)S(1)}, u32[]{:S(2)}, u32[]{:S(2)}) collective-permute-start(bf16[144,1536]{1,0:T(8,128)(2,1)} %get-tuple-element.192), channel_id=1, source_target_pairs={{0,8},{8,0},{16,24},{24,16},{1,9},{9,1},{17,25},{25,17},{2,10},{10... | collective-permute-start | bytes 1327112 | tf_op jit(solution)/shard_map/ppermute | solution.py:67
  366.6 31.7 %all-to-all-start.3 = ((bf16[32,40,128]{2,1,0:T(8,128)(2,1)}), bf16[32,40,128]{2,1,0:T(8,128)(2,1)S(1)}, u32[]{:S(2)}, u32[]{:S(2)}) async-start(bf16[32,40,128]{2,1,0:T(8,128)(2,1)} %get-tuple-element.207), calls=%async_computation.3 | async-start | bytes 655360 | tf_op jit(solution)/shard_map/all_to_all | solution.py:91
  371.8 33.2 %collective-permute-start.47 = (bf16[32,5120]{1,0:T(8,128)(2,1)}, bf16[32,5120]{1,0:T(8,128)(2,1)}, u32[]{:S(2)}, u32[]{:S(2)}) collective-permute-start(bf16[32,5120]{1,0:T(8,128)(2,1)} %get-tuple-element.188.refs_0_), channel_id=1, source_target_pairs={{0,8},{8,0},{16,24},{24,16},{1,9},{9,1},{17,25},{25,17},{2,10},{10... | collective-permute-start | bytes 983048 | tf_op jit(solution)/shard_map/ppermute | solution.py:67
  373.7 32.0 %collective-permute-start.48 = (bf16[32,5120]{1,0:T(8,128)(2,1)}, bf16[32,5120]{1,0:T(8,128)(2,1)}, u32[]{:S(2)}, u32[]{:S(2)}) collective-permute-start(bf16[32,5120]{1,0:T(8,128)(2,1)} %get-tuple-element.188.refs_0_), channel_id=1, source_target_pairs={{0,16},{8,24},{16,0},{24,8},{1,17},{9,25},{17,1},{25,9},{2,18},{10... | collective-permute-start | bytes 983048 | tf_op jit(solution)/shard_map/ppermute | solution.py:67
  379.4 26.4 %collective-permute-start.49 = (bf16[32,5120]{1,0:T(8,128)(2,1)}, bf16[32,5120]{1,0:T(8,128)(2,1)}, u32[]{:S(2)}, u32[]{:S(2)}) collective-permute-start(bf16[32,5120]{1,0:T(8,128)(2,1)} %get-tuple-element.188.refs_0_), channel_id=1, source_target_pairs={{0,24},{8,16},{16,8},{24,0},{1,25},{9,17},{17,9},{25,1},{2,26},{10... | collective-permute-start | bytes 983048 | tf_op jit(solution)/shard_map/ppermute | solution.py:67
  395.3 16.2 %collective-permute-start.44 = (bf16[144,512]{1,0:T(8,128)(2,1)}, bf16[144,512]{1,0:T(8,128)(2,1)S(1)}, u32[]{:S(2)}, u32[]{:S(2)}) collective-permute-start(bf16[144,512]{1,0:T(8,128)(2,1)} %get-tuple-element.204), channel_id=1, source_target_pairs={{0,8},{8,0},{16,24},{24,16},{1,9},{9,1},{17,25},{25,17},{2,10},{10... | collective-permute-start | bytes 442376 | tf_op jit(solution)/shard_map/ppermute | solution.py:67
  396.9 14.7 %collective-permute-start.45 = (bf16[144,512]{1,0:T(8,128)(2,1)}, bf16[144,512]{1,0:T(8,128)(2,1)S(1)}, u32[]{:S(2)}, u32[]{:S(2)}) collective-permute-start(bf16[144,512]{1,0:T(8,128)(2,1)} %get-tuple-element.205), channel_id=1, source_target_pairs={{0,16},{8,24},{16,0},{24,8},{1,17},{9,25},{17,1},{25,9},{2,18},{10... | collective-permute-start | bytes 442376 | tf_op jit(solution)/shard_map/ppermute | solution.py:67
  405.1 6.4 %collective-permute-start.46 = (bf16[144,512]{1,0:T(8,128)(2,1)S(1)}, bf16[144,512]{1,0:T(8,128)(2,1)S(1)}, u32[]{:S(2)}, u32[]{:S(2)}) collective-permute-start(bf16[144,512]{1,0:T(8,128)(2,1)S(1)} %copy-done.63), channel_id=1, source_target_pairs={{0,24},{8,16},{16,8},{24,0},{1,25},{9,17},{17,9},{25,1},{2,26},{10... | collective-permute-start | bytes 442376 | tf_op jit(solution)/shard_map/ppermute | solution.py:67
  (61 other events, 397.6 us)
Sparse Core Ops, SparseCore 0:
  9.7 33.3 all-gather.12
  46.8 62.1 all-gather.14
  111.1 81.3 all-gather.16
  197.1 80.7 all-gather.18
  280.0 71.5 all-gather.20
  353.6 36.3 all-gather.22

commit v3 on v2

--- a/solution.py
+++ b/solution.py
@@ -930,11 +930,12 @@
     fill = TILE - vectors.shape[0] % TILE
     length = jnp.broadcast_to(text_lengths.astype(F32), (fill,))
     gathered = after(jnp.concatenate([cot_sum, vectors, length]), attn_sent)
-    gathered = me.tp_direct(me.gather_cz(gathered))
+    by_plane = me.gather_cz(gathered)
+    gathered = me.tp_direct(by_plane)
     others = after((w_cross_kv, w_cross_q, w_cross_out), (gathered, attn_sent))
     kvq_sent = me.shuffle([(others[0], 2), (others[1], 1)])
     cross_sent = jnp.concatenate([kvq_sent, column_blocks(tp, [(others[2], 1)])], axis=2)
-    attn_w = me.gather_blocks(after(attn_sent, (out_w, gathered)))
+    attn_w = me.gather_blocks(after(attn_sent, (out_w, by_plane)))
     vectors = gathered[:, :, width : width + 4 * own].reshape(world, 4, own)
     vectors = xor_order(vectors, device, world).transpose(1, 0, 2).reshape(4, width)
     embed, gain_a, gain_c, gain_m = vectors[0], vectors[1], vectors[2], vectors[3]

time: 426 us -> 424 us (level)
    ppermute x42, waiting for transfers between devices: 127 us -> 122 us  [hop(): return lax.ppermute(value, 'tp', [(i, i ^ j) for i in range(self.tp)])]
  transfers between devices with their start and end apart: 60 -> 60, of which waited for: 30 -> 32; matrix products, arithmetic and copies ran while one was open for 8% -> 8% of each run, Pallas kernels for 28% -> 28%
where the time goes in v3:
time: 424 us; the launch traced here: 419 us
  waiting for transfers between devices  168 us (40%)
  Pallas kernels  119 us (28%)
  starting transfers between devices  73 us (17%)
  local copies, waits for them, and re-layouts  25.2 us (6%)
  between operations  16.2 us (4%)
  other arithmetic  10.6 us (2%)
  matrix products  6.37 us (2%)
    ppermute x42, waiting for transfers between devices, hop(): return lax.ppermute(value, 'tp', [(i, i ^ j) for i in range(self.tp)])  122 us
    pallas_call x17, Pallas kernels, in_vmem(): pl.pallas_call(kernel, in_specs=[pl.BlockSpec(memory_space=spaces.get(k,...  98.9 us
    ppermute x42, starting transfers between devices, hop(): return lax.ppermute(value, 'tp', [(i, i ^ j) for i in range(self.tp)])  50.6 us
    all_gather x6, waiting for transfers between devices, gather_blocks(): return lax.all_gather(shard, ('core', 'fsdp'), axis=0)  16.7 us
    ppermute x6, waiting for transfers between devices, other_plane(): return lax.ppermute(value, 'fsdp', [(i, i ^ k) for i in range(self.planes)])  11.7 us
    pallas_call x1, Pallas kernels, mlp_up(): pl.pallas_call(functools.partial(up_kernel, tp), grid=(ff // step,), in_s...  11.2 us
    pallas_call x2, Pallas kernels, join(): pl.pallas_call(functools.partial(join_kernel, rows - PAD), grid=(rows //...  9.05 us
  transfers between devices with their start and end apart: 60, of which 32 were waited for; matrix products, arithmetic and copies ran while one was open for 8% of the time, Pallas kernels for 28%

profile of v3, /device:TPU:0, one launch (start us, length us, event | category | flops | bytes accessed | tf_op | source)
XLA Modules:
  0.0 418.5 jit_solution(17767784181703866351)
XLA Ops:
  8.6 2.1 parts.1
  10.7 2.9 collective-permute-start
  16.1 3.5 collective-permute-done.refs_1_
  19.6 4.8 %collective-permute-done.1.refs_2_ = bf16[64,1536]{1,0:T(8,128)(2,1)S(1)} collective-permute-done((bf16[64,1536]{1,0:T(8,128)(2,1)}, bf16[64,1536]{1,0:T(8,128)(2,1)S(1)}, u32[]{:S(2)}, u32[]{:S(2)}) %collective-permute-start.1) | collective-permute-done | bytes 196640 | tf_op jit(solution)/shard_map/ppermute | solution.py:67
  25.2 2.2 assemble.1
  27.4 1.6 collective-permute-start.3
  28.9 2.6 collective-permute-start.4
  31.9 2.7 collective-permute-done.4
  34.6 2.7 collective-permute-done.5
  38.7 4.4 %all-gather.13.cloned.1.call-done = bf16[512,2048]{1,0:T(8,128)(2,1)} async-done(((bf16[64,2048]{1,0:T(8,128)(2,1)}), bf16[512,2048]{1,0:T(8,128)(2,1)}) %all-gather.13.cloned.1.call-update) | async-done | bytes 2097168 | tf_op jit(solution)/shard_map/all_gather | solution.py:102
  43.4 2.4 collective-permute-start.9
  48.7 1.8 collective-permute-done.8
  51.2 2.2 column_blocks.3
  56.0 3.5 all-to-all-start
  61.3 2.0 collective-permute-start.10
  66.2 1.7 column_blocks.4
  68.5 14.4 %collective-permute-done.10.refs_1_.refs_5_ = bf16[128,2048]{1,0:T(8,128)(2,1)S(1)} collective-permute-done((bf16[128,2048]{1,0:T(8,128)(2,1)S(1)}, bf16[128,2048]{1,0:T(8,128)(2,1)S(1)}, u32[]{:S(2)}, u32[]{:S(2)}) %collective-permute-start.10) | collective-permute-done | bytes 524320 | tf_op jit(solution)/shard_map/ppermute | solution.py:67
  83.8 9.8 %collective-permute-done.12.refs_3_.refs_7_ = bf16[128,2048]{1,0:T(8,128)(2,1)} collective-permute-done((bf16[128,2048]{1,0:T(8,128)(2,1)S(1)}, bf16[128,2048]{1,0:T(8,128)(2,1)}, u32[]{:S(2)}, u32[]{:S(2)}) %collective-permute-start.12) | collective-permute-done | bytes 524320 | tf_op jit(solution)/shard_map/ppermute | solution.py:67
  93.6 2.3 column_blocks.5
  95.9 3.5 all-to-all-start.2
  102.0 2.1 pad_maximum_fusion.1
  104.1 7.9 %all-to-all-done.2 = bf16[4,64,2048]{2,1,0:T(8,128)(2,1)S(1)} async-done(((bf16[4,64,2048]{2,1,0:T(8,128)(2,1)}), bf16[4,64,2048]{2,1,0:T(8,128)(2,1)S(1)}, u32[]{:S(2)}, u32[]{:S(2)}) %all-to-all-start.2) | async-done | bytes 1048608 | tf_op jit(solution)/shard_map/all_to_all | solution.py:99
  118.3 17.2 %self_attention.1 = (bf16[144,2048]{1,0:T(8,128)(2,1)}, bf16[144,2048]{1,0:T(8,128)(2,1)}, bf16[144,2048]{1,0:T(8,128)(2,1)}, bf16[144,2048]{1,0:T(8,128)(2,1)},...) custom-call(bf16[128,2048]{1,0:T(8,128)(2,1)} %copy-done.2, ...), custom_call_target="tpu_custom_call" | custom-call | flops 1 | bytes 1 | tf_op jit(solution)/shard_map/self_attention/pallas_call | solution.py:606
  135.5 2.8 collective-permute-done.14.refs_6_.refs_15_
  139.2 1.7 collective-permute-start.16
  141.1 1.5 collective-permute-start.18
  144.1 3.3 all-to-all-start.1
  148.8 6.2 %all-to-all-done.1 = f32[8,4,256]{2,1,0:T(4,128)S(1)} async-done(((f32[8,4,256]{2,1,0:T(4,128)}), f32[8,4,256]{2,1,0:T(4,128)S(1)}, u32[]{:S(2)}, u32[]{:S(2)}) %all-to-all-start.1) | async-done | bytes 32800 | tf_op jit(solution)/shard_map/all_to_all | solution.py:969
  155.6 8.8 %collective-permute-done.17.refs_2_ = bf16[144,2048]{1,0:T(8,128)(2,1)} collective-permute-done((bf16[144,2048]{1,0:T(8,128)(2,1)}, bf16[144,2048]{1,0:T(8,128)(2,1)}, u32[]{:S(2)}, u32[]{:S(2)}) %collective-permute-start.17) | collective-permute-done | bytes 589856 | tf_op jit(solution)/shard_map/ppermute | solution.py:67
  164.4 1.9 collective-permute-done.18.refs_3_
  166.3 4.5 %join.2 = (f32[144,2048]{1,0:T(8,128)}, bf16[144,2048]{1,0:T(8,128)(2,1)}) custom-call(f32[144,2048]{1,0:T(8,128)} %get-tuple-element.125.base.rows, f32[1,2048]{1,0:T(1,128)} %slice.170.gain, bf16[144,2048]{1,0:T(8,128)(2,1)} %get-tuple-element.132.refs_0_, bf16[144,2048]{1,0:T(8,128)(2,1)} %copy-done.18, ...), custom_call_target="tpu_custom_call" | custom-call | flops 1 | bytes 1 | tf_op jit(solution)/shard_map/join/pallas_call | solution.py:858
  171.5 1.7 collective-permute-start.20
  174.4 13.0 %collective-permute-done.19.refs_1_ = bf16[144,2048]{1,0:T(8,128)(2,1)S(1)} collective-permute-done((bf16[144,2048]{1,0:T(8,128)(2,1)}, bf16[144,2048]{1,0:T(8,128)(2,1)S(1)}, u32[]{:S(2)}, u32[]{:S(2)}) %collective-permute-start.19) | collective-permute-done | bytes 589856 | tf_op jit(solution)/shard_map/ppermute | solution.py:67
  187.4 9.0 %collective-permute-done.20.refs_2_ = bf16[144,2048]{1,0:T(8,128)(2,1)S(1)} collective-permute-done((bf16[144,2048]{1,0:T(8,128)(2,1)}, bf16[144,2048]{1,0:T(8,128)(2,1)S(1)}, u32[]{:S(2)}, u32[]{:S(2)}) %collective-permute-start.20) | collective-permute-done | bytes 589856 | tf_op jit(solution)/shard_map/ppermute | solution.py:67
  197.4 14.2 %cross_attention.1 = (bf16[144,2048]{1,0:T(8,128)(2,1)}, bf16[144,2048]{1,0:T(8,128)(2,1)}, bf16[144,2048]{1,0:T(8,128)(2,1)}, bf16[144,2048]{1,0:T(8,128)(2,1)}...) custom-call(bf16[144,2048]{1,0:T(8,128)(2,1)} %get-tuple-element.137, ...), custom_call_target="tpu_custom_call" | custom-call | flops 1 | bytes 1 | tf_op jit(solution)/shard_map/cross_attention/pallas_call | solution.py:606
  211.6 1.7 collective-permute-start.22
  213.3 1.9 collective-permute-start.24
  215.8 12.3 %collective-permute-done.22.refs_1_ = bf16[144,2048]{1,0:T(8,128)(2,1)S(1)} collective-permute-done((bf16[144,2048]{1,0:T(8,128)(2,1)}, bf16[144,2048]{1,0:T(8,128)(2,1)S(1)}, u32[]{:S(2)}, u32[]{:S(2)}) %collective-permute-start.22) | collective-permute-done | bytes 589856 | tf_op jit(solution)/shard_map/ppermute | solution.py:67
  228.1 7.0 %collective-permute-done.23.refs_2_ = bf16[144,2048]{1,0:T(8,128)(2,1)S(1)} collective-permute-done((bf16[144,2048]{1,0:T(8,128)(2,1)}, bf16[144,2048]{1,0:T(8,128)(2,1)S(1)}, u32[]{:S(2)}, u32[]{:S(2)}) %collective-permute-start.23) | collective-permute-done | bytes 589856 | tf_op jit(solution)/shard_map/ppermute | solution.py:67
  236.8 4.5 %join.3 = (f32[144,2048]{1,0:T(8,128)}, bf16[144,2048]{1,0:T(8,128)(2,1)}) custom-call(f32[144,2048]{1,0:T(8,128)} %get-tuple-element.136.base, f32[1,2048]{1,0:T(1,128)} %slice.175.gain, bf16[144,2048]{1,0:T(8,128)(2,1)} %get-tuple-element.141.refs_0_, bf16[144,2048]{1,0:T(8,128)(2,1)} %copy-done.19, bf16[144,2048]{1,0:T(8,128)(2,1)} %copy-done.20, ...), custom_call_target="tpu_custom_call" | custom-call | flops 1 | bytes 1 | tf_op jit(solution)/shard_map/join/pallas_call | solution.py:858
  245.8 12.0 %collective-permute-done.25.refs_1_ = bf16[144,2048]{1,0:T(8,128)(2,1)S(1)} collective-permute-done((bf16[144,2048]{1,0:T(8,128)(2,1)}, bf16[144,2048]{1,0:T(8,128)(2,1)S(1)}, u32[]{:S(2)}, u32[]{:S(2)}) %collective-permute-start.25) | collective-permute-done | bytes 589856 | tf_op jit(solution)/shard_map/ppermute | solution.py:67
  257.8 8.2 %collective-permute-done.26.refs_2_ = bf16[144,2048]{1,0:T(8,128)(2,1)S(1)} collective-permute-done((bf16[144,2048]{1,0:T(8,128)(2,1)}, bf16[144,2048]{1,0:T(8,128)(2,1)S(1)}, u32[]{:S(2)}, u32[]{:S(2)}) %collective-permute-start.26) | collective-permute-done | bytes 589856 | tf_op jit(solution)/shard_map/ppermute | solution.py:67
  266.1 10.2 %all-gather.19.cloned.1.call-done = bf16[32,64,2048]{2,1,0:T(8,128)(2,1)} async-done(((bf16[4,64,2048]{2,1,0:T(8,128)(2,1)}), bf16[32,64,2048]{2,1,0:T(8,128)(2,1)}) %all-gather.19.cloned.1.call-update) | async-done | bytes 8388624 | tf_op jit(solution)/shard_map/all_gather | solution.py:102
  277.2 7.7 %mlp_back.1 = (bf16[16,2048]{1,0:T(8,128)(2,1)}, bf16[16,2048]{1,0:T(8,128)(2,1)}, f32[4,2048]{1,0:T(4,128)}, f32[4,2048]{1,0:T(4,128)}, f32[4,2048]{1,0:T(4,128)}) custom-call(bf16[144,2048]{1,0:T(8,128)(2,1)} %get-tuple-element.175.refs_0_, bf16[144,2048]{1,0:T(8,128)(2,1)} %copy-done.5, bf16[144,2048]{1,0:T(8,128)(2,1)} %copy-done.6, ...), custom_call_target="tpu_custom_call" | custom-call | flops 1 | bytes 1 | tf_op jit(solution)/shard_map/mlp_back/pallas_call | solution.py:606
  285.0 1.6 collective-permute-start.28
  290.7 2.4 collective-permute-done.30.refs_3_
  293.7 6.6 %cross_back.1 = (f32[4,2048]{1,0:T(4,128)}, f32[4,512]{1,0:T(4,128)}, f32[4,8,128]{2,1,0:T(8,128)}, f32[4,512]{1,0:T(4,128)}, f32[4,2048]{1,0:T(4,128)}, /*index=5*/f32[1,2048]{1,0:T(1,128)}) custom-call(f32[4,2048]{1,0:T(4,128)} %slice_bitcast_fusion.base, f32[4,2048]{1,0:T(4,128)} %get-tuple-element.148.rows, f32[1,2048]{1,0:T(1,128)} %slice.175.gain, ...), custom_call_target="tpu_custom_call" | custom-call | flops 1 | bytes 1 | tf_op jit(solution)/shard_map/cross_back/pallas_call | solution.py:606
  301.4 2.5 collective-permute-start.33
  305.2 6.2 %text_back.1 = (bf16[16,2176]{1,0:T(8,128)(2,1)}, bf16[16,2176]{1,0:T(8,128)(2,1)}, bf16[16,2176]{1,0:T(8,128)(2,1)}, bf16[16,2176]{1,0:T(8,128)(2,1)}, f32[40,2048]{1,0:T(8,128)}, /*index=5*/bf16[4,8704]{1,0:T(4,128)(2,1)}) custom-call(f32[4,8,128]{2,1,0:T(8,128)} %get-tuple-element.156.refs_0_, f32[4,8,128]{2,1,0:T(8,128)} %get-tuple-element.150.probs.refs_1_, ...), custom_call_target="tpu_custom_call" | custom-call | flops 1 | bytes 1 | tf_op jit(solution)/shard_map/text_back/pallas_call | solution.py:606
  312.1 9.2 %self_back.1 = (bf16[32,2176]{1,0:T(8,128)(2,1)}, bf16[32,2176]{1,0:T(8,128)(2,1)}, bf16[32,2176]{1,0:T(8,128)(2,1)}, bf16[32,2176]{1,0:T(8,128)(2,1)}, bf16[32,...) custom-call(f32[4,2048]{1,0:T(4,128)} %get-tuple-element.152.refs_12_.base, f32[4,2048]{1,0:T(4,128)} %get-tuple-element.153.rows, ...), custom_call_target="tpu_custom_call" | custom-call | flops 1 | bytes 1 | tf_op jit(solution)/shard_map/self_back/pallas_call | solution.py:606
  322.5 2.4 collective-permute-start.39
  326.1 6.3 %collective-permute-done.34.refs_1_ = bf16[4,12288]{1,0:T(4,128)(2,1)S(1)} collective-permute-done((bf16[4,12288]{1,0:T(4,128)(2,1)}, bf16[4,12288]{1,0:T(4,128)(2,1)S(1)}, u32[]{:S(2)}, u32[]{:S(2)}) %collective-permute-start.34) | collective-permute-done | bytes 98336 | tf_op jit(solution)/shard_map/ppermute | solution.py:73
  333.2 11.2 %mlp_up.1.active = bf16[576,2048]{1,0:T(8,128)(2,1)} custom-call(bf16[144,2048]{1,0:T(8,128)(2,1)} %get-tuple-element.175.refs_0_, bf16[144,2048]{1,0:T(8,128)(2,1)} %copy-done.5, bf16[144,2048]{1,0:T(8,128)(2,1)} %copy-done.6, bf16[144,2048]{1,0:T(8,128)(2,1)} %copy-done.7, bf16[8,4,64,2048]{3,2,1,0:T(8,128)(2,1)} %bitcast.124), custom_call_target="tpu_custom_call" | custom-call | flops 1 | bytes 1 | tf_op jit(solution)/shard_map/mlp_up/pallas_call | solution.py:700
  345.0 1.8 stack.53.planes
  349.5 2.2 unpack.1
  351.8 8.5 %mlp_down.2 = (bf16[144,1536]{1,0:T(8,128)(2,1)}, bf16[144,1536]{1,0:T(8,128)(2,1)}, bf16[144,1536]{1,0:T(8,128)(2,1)}, bf16[144,1536]{1,0:T(8,128)(2,1)}) custom-call(bf16[576,2048]{1,0:T(8,128)(2,1)} %mlp_up.1.active, bf16[8,256,1536]{2,1,0:T(8,128)(2,1)} %bitcast.129), custom_call_target="tpu_custom_call" | custom-call | flops 1 | bytes 1 | tf_op jit(solution)/shard_map/mlp_down/pallas_call | solution.py:606
  364.9 4.4 %all-to-all-start.3 = ((bf16[32,40,128]{2,1,0:T(8,128)(2,1)}), bf16[32,40,128]{2,1,0:T(8,128)(2,1)S(1)}, u32[]{:S(2)}, u32[]{:S(2)}) async-start(bf16[32,40,128]{2,1,0:T(8,128)(2,1)} %get-tuple-element.207), calls=%async_computation.3 | async-start | bytes 655360 | tf_op jit(solution)/shard_map/all_to_all | solution.py:91
  370.2 1.8 collective-permute-start.47
  373.5 4.2 %tokens_back.1 = (bf16[256,2048]{1,0:T(8,128)(2,1)}, bf16[128,2048]{1,0:T(8,128)(2,1)}) custom-call(f32[144,2048]{1,0:T(8,128)} %get-tuple-element.125.base.rows, f32[1,2048]{1,0:T(1,128)} %slice.179.gain_a.gain, bf16[256,128]{1,0:T(8,128)(2,1)} %copy-done.17, bf16[32,2176]{1,0:T(8,128)(2,1)} %get-tuple-element.196.refs_0_, bf16[32,2176]{1,0:T(8,128)(2,1)} %copy-done.38, ...), custom_call_target="tpu_custom_call" | custom-call | flops 1 | bytes 1 | tf_op jit(solution)/shard_map/tokens_back/pallas_call | solution.py:606
  377.9 8.0 %collective-permute-done.42 = bf16[144,1536]{1,0:T(8,128)(2,1)S(1)} collective-permute-done((bf16[144,1536]{1,0:T(8,128)(2,1)}, bf16[144,1536]{1,0:T(8,128)(2,1)S(1)}, u32[]{:S(2)}, u32[]{:S(2)}) %collective-permute-start.42) | collective-permute-done | bytes 442400 | tf_op jit(solution)/shard_map/ppermute | solution.py:67
  386.3 2.0 all-gather.23.cloned.1.call-done
  388.3 5.3 %mlp_down.3 = (bf16[144,512]{1,0:T(8,128)(2,1)}, bf16[144,512]{1,0:T(8,128)(2,1)}, bf16[144,512]{1,0:T(8,128)(2,1)}, bf16[144,512]{1,0:T(8,128)(2,1)}) custom-call(bf16[576,2048]{1,0:T(8,128)(2,1)} %mlp_up.1.active, bf16[8,256,512]{2,1,0:T(8,128)(2,1)} %bitcast.130), custom_call_target="tpu_custom_call" | custom-call | flops 1 | bytes 1 | tf_op jit(solution)/shard_map/mlp_down/pallas_call | solution.py:606
  401.6 1.8 fusion.26
  404.1 5.2 %columns.1 = (f32[64,6144]{1,0:T(8,128)}, f32[64,4096]{1,0:T(8,128)}, f32[64,2048]{1,0:T(8,128)}, f32[64,8192]{1,0:T(8,128)}) custom-call(s32[2]{0:T(128)} %pad_add_fusion.place, bf16[4,2,4,32,64]{4,3,2,1,0:T(8,128)(2,1)} %bitcast.144, bf16[4,2,4,32,64]{4,3,2,1,0:T(8,128)(2,1)} %bitcast.145, bf16[4,2,32,64]{3,2,1,0:T(8,128)(2,1)} %bitcast.155, ...), custom_call_target="tpu_custom_call" | custom-call | flops 1 | bytes 1 | tf_op jit(solution)/shard_map/columns/pallas_call | solution.py:606
  (329 shorter events, 74.1 us)
Async XLA Ops:
  7.2 39.8 %copy-start = (bf16[256,2048]{1,0:T(8,128)(2,1)S(1)}, bf16[256,2048]{1,0:T(8,128)(2,1)}, u32[]{:S(2)}) copy-start(bf16[256,2048]{1,0:T(8,128)(2,1)} %param.16) | copy-start | bytes 3145732
  7.2 35.8 %all-gather.13.cloned.1.call-start = ((), (), s32[]{:S(2)}) async-start(), calls=%async_computation.4 | async-start | bytes 2359296 | tf_op jit(solution)/shard_map/all_gather | solution.py:102
  8.0 104.0 %all-gather.15.cloned.1.call-start = ((), (), s32[]{:S(2)}) async-start(), calls=%async_computation.5 | async-start | bytes 7077888 | tf_op jit(solution)/shard_map/all_gather | solution.py:102
  10.7 8.9 %collective-permute-start = (bf16[64,1536]{1,0:T(8,128)(2,1)}, bf16[64,1536]{1,0:T(8,128)(2,1)S(1)}, u32[]{:S(2)}, u32[]{:S(2)}) collective-permute-start(bf16[64,1536]{1,0:T(8,128)(2,1)} %get-tuple-element.118), channel_id=1, source_target_pairs={{0,8},{8,0},{16,24},{24,16},{1,9},{9,1},{17,25},{25,17},{2,10},{10... | collective-permute-start | bytes 589832 | tf_op jit(solution)/shard_map/ppermute | solution.py:67
  13.7 10.8 %collective-permute-start.1 = (bf16[64,1536]{1,0:T(8,128)(2,1)}, bf16[64,1536]{1,0:T(8,128)(2,1)S(1)}, u32[]{:S(2)}, u32[]{:S(2)}) collective-permute-start(bf16[64,1536]{1,0:T(8,128)(2,1)} %get-tuple-element.119), channel_id=1, source_target_pairs={{0,16},{8,24},{16,0},{24,8},{1,17},{9,25},{17,1},{25,9},{2,18},{10... | collective-permute-start | bytes 589832 | tf_op jit(solution)/shard_map/ppermute | solution.py:67
  15.2 9.3 %collective-permute-start.2 = (bf16[64,1536]{1,0:T(8,128)(2,1)}, bf16[64,1536]{1,0:T(8,128)(2,1)S(1)}, u32[]{:S(2)}, u32[]{:S(2)}) collective-permute-start(bf16[64,1536]{1,0:T(8,128)(2,1)} %get-tuple-element.120), channel_id=1, source_target_pairs={{0,24},{8,16},{16,8},{24,0},{1,25},{9,17},{17,9},{25,1},{2,26},{10... | collective-permute-start | bytes 589832 | tf_op jit(solution)/shard_map/ppermute | solution.py:67
  27.4 4.5 %collective-permute-start.3 = (f32[2432]{0:T(1024)S(1)}, f32[2432]{0:T(1024)S(1)}, u32[]{:S(2)}, u32[]{:S(2)}) collective-permute-start(f32[2432]{0:T(1024)S(1)} %pad_maximum_fusion.13), channel_id=1, source_target_pairs={{0,1},{1,0},{2,3},{3,2},{4,5},{5,4},{6,7},{7,6},{8,9},{9,8},{10,11... | collective-permute-start | bytes 29192 | tf_op jit(solution)/shard_map/ppermute | solution.py:73
  28.9 5.6 %collective-permute-start.4 = (f32[2432]{0:T(1024)S(1)}, f32[2432]{0:T(1024)S(1)}, u32[]{:S(2)}, u32[]{:S(2)}) collective-permute-start(f32[2432]{0:T(1024)S(1)} %pad_maximum_fusion.13), channel_id=1, source_target_pairs={{0,2},{1,3},{2,0},{3,1},{4,6},{5,7},{6,4},{7,5},{8,10},{9,11},{10,... | collective-permute-start | bytes 29192 | tf_op jit(solution)/shard_map/ppermute | solution.py:73
  31.5 5.7 %collective-permute-start.5 = (f32[2432]{0:T(1024)S(1)}, f32[2432]{0:T(1024)S(1)}, u32[]{:S(2)}, u32[]{:S(2)}) collective-permute-start(f32[2432]{0:T(1024)S(1)} %pad_maximum_fusion.13), channel_id=1, source_target_pairs={{0,3},{1,2},{2,1},{3,0},{4,7},{5,6},{6,5},{7,4},{8,11},{9,10},{10,... | collective-permute-start | bytes 29192 | tf_op jit(solution)/shard_map/ppermute | solution.py:73
  37.3 1.3 collective-permute-start.6
  43.4 7.4 %collective-permute-start.9 = (f32[8,2432]{1,0:T(8,128)S(1)}, f32[8,2432]{1,0:T(8,128)S(1)}, u32[]{:S(2)}, u32[]{:S(2)}) collective-permute-start(f32[8,2432]{1,0:T(8,128)S(1)} %concatenate.111), channel_id=1, source_target_pairs={{0,24},{8,16},{16,8},{24,0},{1,25},{9,17},{17,9},{25,1},{2,26},{10... | collective-permute-start | bytes 233480 | tf_op jit(solution)/shard_map/ppermute | solution.py:67
  45.8 4.7 %collective-permute-start.8 = (f32[8,2432]{1,0:T(8,128)S(1)}, f32[8,2432]{1,0:T(8,128)S(1)}, u32[]{:S(2)}, u32[]{:S(2)}) collective-permute-start(f32[8,2432]{1,0:T(8,128)S(1)} %concatenate.111), channel_id=1, source_target_pairs={{0,16},{8,24},{16,0},{24,8},{1,17},{9,25},{17,1},{25,9},{2,18},{10... | collective-permute-start | bytes 233480 | tf_op jit(solution)/shard_map/ppermute | solution.py:67
  46.4 4.4 %collective-permute-start.7 = (f32[8,2432]{1,0:T(8,128)S(1)}, f32[8,2432]{1,0:T(8,128)S(1)}, u32[]{:S(2)}, u32[]{:S(2)}) collective-permute-start(f32[8,2432]{1,0:T(8,128)S(1)} %concatenate.111), channel_id=1, source_target_pairs={{0,8},{8,0},{16,24},{24,16},{1,9},{9,1},{17,25},{25,17},{2,10},{10... | collective-permute-start | bytes 233480 | tf_op jit(solution)/shard_map/ppermute | solution.py:67
  56.0 37.6 %all-to-all-start = ((bf16[4,64,1536]{2,1,0:T(8,128)(2,1)}), bf16[4,64,1536]{2,1,0:T(8,128)(2,1)S(1)}, u32[]{:S(2)}, u32[]{:S(2)}) async-start(bf16[4,64,1536]{2,1,0:T(8,128)(2,1)} %column_blocks.3), calls=%async_computation | async-start | bytes 1572864 | tf_op jit(solution)/shard_map/all_to_all | solution.py:99
  61.3 34.6 %copy-start.2 = (bf16[128,2048]{1,0:T(8,128)(2,1)}, bf16[128,2048]{1,0:T(8,128)(2,1)S(1)}, u32[]{:S(2)}) copy-start(bf16[128,2048]{1,0:T(8,128)(2,1)S(1)} %slice.219.refs_0_.refs_4_) | copy-start | bytes 1572868
  61.3 21.7 %collective-permute-start.10 = (bf16[128,2048]{1,0:T(8,128)(2,1)S(1)}, bf16[128,2048]{1,0:T(8,128)(2,1)S(1)}, u32[]{:S(2)}, u32[]{:S(2)}) collective-permute-start(bf16[128,2048]{1,0:T(8,128)(2,1)S(1)} %slice.219.refs_0_.refs_4_), channel_id=1, source_target_pairs={{0,8},{8,0},{16,24},{24,16},{1,9},{9,1},{17,25},{25,17},{2,10},{10... | collective-permute-start | bytes 1572872 | tf_op jit(solution)/shard_map/ppermute | solution.py:67
  63.3 19.6 %collective-permute-start.11 = (bf16[128,2048]{1,0:T(8,128)(2,1)S(1)}, bf16[128,2048]{1,0:T(8,128)(2,1)S(1)}, u32[]{:S(2)}, u32[]{:S(2)}) collective-permute-start(bf16[128,2048]{1,0:T(8,128)(2,1)S(1)} %slice.219.refs_0_.refs_4_), channel_id=1, source_target_pairs={{0,16},{8,24},{16,0},{24,8},{1,17},{9,25},{17,1},{25,9},{2,18},{10... | collective-permute-start | bytes 1572872 | tf_op jit(solution)/shard_map/ppermute | solution.py:67
  64.8 28.8 %collective-permute-start.12 = (bf16[128,2048]{1,0:T(8,128)(2,1)S(1)}, bf16[128,2048]{1,0:T(8,128)(2,1)}, u32[]{:S(2)}, u32[]{:S(2)}) collective-permute-start(bf16[128,2048]{1,0:T(8,128)(2,1)S(1)} %slice.219.refs_0_.refs_4_), channel_id=1, source_target_pairs={{0,24},{8,16},{16,8},{24,0},{1,25},{9,17},{17,9},{25,1},{2,26},{10... | collective-permute-start | bytes 1572872 | tf_op jit(solution)/shard_map/ppermute | solution.py:67
  95.9 16.1 %all-to-all-start.2 = ((bf16[4,64,2048]{2,1,0:T(8,128)(2,1)}), bf16[4,64,2048]{2,1,0:T(8,128)(2,1)S(1)}, u32[]{:S(2)}, u32[]{:S(2)}) async-start(bf16[4,64,2048]{2,1,0:T(8,128)(2,1)} %column_blocks.5), calls=%async_computation.2 | async-start | bytes 2097152 | tf_op jit(solution)/shard_map/all_to_all | solution.py:99
  99.4 96.9 %all-gather.17.cloned.1.call-start = ((), (), s32[]{:S(2)}) async-start(), calls=%async_computation.6 | async-start | bytes 9437184 | tf_op jit(solution)/shard_map/all_gather | solution.py:102
  114.1 21.4 %collective-permute-start.13 = (bf16[128,2048]{1,0:T(8,128)(2,1)S(1)}, bf16[128,2048]{1,0:T(8,128)(2,1)S(1)}, u32[]{:S(2)}, u32[]{:S(2)}) collective-permute-start(bf16[128,2048]{1,0:T(8,128)(2,1)S(1)} %bitcast.133), channel_id=1, source_target_pairs={{0,8},{8,0},{16,24},{24,16},{1,9},{9,1},{17,25},{25,17},{2,10},{10... | collective-permute-start | bytes 1572872 | tf_op jit(solution)/shard_map/ppermute | solution.py:67
  115.6 22.7 %collective-permute-start.14 = (bf16[128,2048]{1,0:T(8,128)(2,1)S(1)}, bf16[128,2048]{1,0:T(8,128)(2,1)S(1)}, u32[]{:S(2)}, u32[]{:S(2)}) collective-permute-start(bf16[128,2048]{1,0:T(8,128)(2,1)S(1)} %bitcast.134), channel_id=1, source_target_pairs={{0,16},{8,24},{16,0},{24,8},{1,17},{9,25},{17,1},{25,9},{2,18},{10... | collective-permute-start | bytes 1572872 | tf_op jit(solution)/shard_map/ppermute | solution.py:67
  116.1 22.2 %collective-permute-start.15 = (bf16[128,2048]{1,0:T(8,128)(2,1)S(1)}, bf16[128,2048]{1,0:T(8,128)(2,1)S(1)}, u32[]{:S(2)}, u32[]{:S(2)}) collective-permute-start(bf16[128,2048]{1,0:T(8,128)(2,1)S(1)} %bitcast.135), channel_id=1, source_target_pairs={{0,24},{8,16},{16,8},{24,0},{1,25},{9,17},{17,9},{25,1},{2,26},{10... | collective-permute-start | bytes 1572872 | tf_op jit(solution)/shard_map/ppermute | solution.py:67
  135.5 35.3 %copy-start.11 = (bf16[128,2048]{1,0:T(8,128)(2,1)}, bf16[128,2048]{1,0:T(8,128)(2,1)S(1)}, u32[]{:S(2)}) copy-start(bf16[128,2048]{1,0:T(8,128)(2,1)S(1)} %collective-permute-done.13.refs_5_.refs_14_) | copy-start | bytes 1572868
  138.3 32.5 %copy-start.12 = (bf16[128,2048]{1,0:T(8,128)(2,1)}, bf16[128,2048]{1,0:T(8,128)(2,1)S(1)}, u32[]{:S(2)}) copy-start(bf16[128,2048]{1,0:T(8,128)(2,1)S(1)} %collective-permute-done.14.refs_6_.refs_15_) | copy-start | bytes 1572868
  139.2 16.5 %collective-permute-start.16 = (bf16[144,2048]{1,0:T(8,128)(2,1)}, bf16[144,2048]{1,0:T(8,128)(2,1)S(1)}, u32[]{:S(2)}, u32[]{:S(2)}) collective-permute-start(bf16[144,2048]{1,0:T(8,128)(2,1)} %get-tuple-element.133), channel_id=1, source_target_pairs={{0,8},{8,0},{16,24},{24,16},{1,9},{9,1},{17,25},{25,17},{2,10},{10... | collective-permute-start | bytes 1769480 | tf_op jit(solution)/shard_map/ppermute | solution.py:67
  140.8 23.6 %collective-permute-start.17 = (bf16[144,2048]{1,0:T(8,128)(2,1)}, bf16[144,2048]{1,0:T(8,128)(2,1)}, u32[]{:S(2)}, u32[]{:S(2)}) collective-permute-start(bf16[144,2048]{1,0:T(8,128)(2,1)} %get-tuple-element.134), channel_id=1, source_target_pairs={{0,16},{8,24},{16,0},{24,8},{1,17},{9,25},{17,1},{25,9},{2,18},{10... | collective-permute-start | bytes 1769480 | tf_op jit(solution)/shard_map/ppermute | solution.py:67
  141.1 25.2 %collective-permute-start.18 = (bf16[144,2048]{1,0:T(8,128)(2,1)}, bf16[144,2048]{1,0:T(8,128)(2,1)}, u32[]{:S(2)}, u32[]{:S(2)}) collective-permute-start(bf16[144,2048]{1,0:T(8,128)(2,1)} %get-tuple-element.135), channel_id=1, source_target_pairs={{0,24},{8,16},{16,8},{24,0},{1,25},{9,17},{17,9},{25,1},{2,26},{10... | collective-permute-start | bytes 1769480 | tf_op jit(solution)/shard_map/ppermute | solution.py:67
  144.1 11.0 %all-to-all-start.1 = ((f32[8,4,256]{2,1,0:T(4,128)}), f32[8,4,256]{2,1,0:T(4,128)S(1)}, u32[]{:S(2)}, u32[]{:S(2)}) async-start(f32[8,4,256]{2,1,0:T(4,128)} %fusion.25), calls=%async_computation.1 | async-start | bytes 65536 | tf_op jit(solution)/shard_map/all_to_all | solution.py:969
  147.4 128.9 %all-gather.19.cloned.1.call-start = ((), (), s32[]{:S(2)}) async-start(), calls=%async_computation.7 | async-start | bytes 9437184 | tf_op jit(solution)/shard_map/all_gather | solution.py:102
  170.8 16.5 %collective-permute-start.19 = (bf16[144,2048]{1,0:T(8,128)(2,1)}, bf16[144,2048]{1,0:T(8,128)(2,1)S(1)}, u32[]{:S(2)}, u32[]{:S(2)}) collective-permute-start(bf16[144,2048]{1,0:T(8,128)(2,1)} %get-tuple-element.137.refs_0_), channel_id=1, source_target_pairs={{0,8},{8,0},{16,24},{24,16},{1,9},{9,1},{17,25},{25,17},{2,10},{10... | collective-permute-start | bytes 1769480 | tf_op jit(solution)/shard_map/ppermute | solution.py:67
  171.5 24.9 %collective-permute-start.20 = (bf16[144,2048]{1,0:T(8,128)(2,1)}, bf16[144,2048]{1,0:T(8,128)(2,1)S(1)}, u32[]{:S(2)}, u32[]{:S(2)}) collective-permute-start(bf16[144,2048]{1,0:T(8,128)(2,1)} %get-tuple-element.137.refs_0_), channel_id=1, source_target_pairs={{0,16},{8,24},{16,0},{24,8},{1,17},{9,25},{17,1},{25,9},{2,18},{10... | collective-permute-start | bytes 1769480 | tf_op jit(solution)/shard_map/ppermute | solution.py:67
  173.2 23.1 %collective-permute-start.21 = (bf16[144,2048]{1,0:T(8,128)(2,1)}, bf16[144,2048]{1,0:T(8,128)(2,1)S(1)}, u32[]{:S(2)}, u32[]{:S(2)}) collective-permute-start(bf16[144,2048]{1,0:T(8,128)(2,1)} %get-tuple-element.137.refs_0_), channel_id=1, source_target_pairs={{0,24},{8,16},{16,8},{24,0},{1,25},{9,17},{17,9},{25,1},{2,26},{10... | collective-permute-start | bytes 1769480 | tf_op jit(solution)/shard_map/ppermute | solution.py:67
  196.4 155.4 %all-gather.21.cloned.1.call-start = ((), (), s32[]{:S(2)}) async-start(), calls=%async_computation.8 | async-start | bytes 7077888 | tf_op jit(solution)/shard_map/all_gather | solution.py:102
  211.6 16.5 %collective-permute-start.22 = (bf16[144,2048]{1,0:T(8,128)(2,1)}, bf16[144,2048]{1,0:T(8,128)(2,1)S(1)}, u32[]{:S(2)}, u32[]{:S(2)}) collective-permute-start(bf16[144,2048]{1,0:T(8,128)(2,1)} %get-tuple-element.142), channel_id=1, source_target_pairs={{0,8},{8,0},{16,24},{24,16},{1,9},{9,1},{17,25},{25,17},{2,10},{10... | collective-permute-start | bytes 1769480 | tf_op jit(solution)/shard_map/ppermute | solution.py:67
  213.3 21.9 %collective-permute-start.23 = (bf16[144,2048]{1,0:T(8,128)(2,1)}, bf16[144,2048]{1,0:T(8,128)(2,1)S(1)}, u32[]{:S(2)}, u32[]{:S(2)}) collective-permute-start(bf16[144,2048]{1,0:T(8,128)(2,1)} %get-tuple-element.143), channel_id=1, source_target_pairs={{0,16},{8,24},{16,0},{24,8},{1,17},{9,25},{17,1},{25,9},{2,18},{10... | collective-permute-start | bytes 1769480 | tf_op jit(solution)/shard_map/ppermute | solution.py:67
  213.3 22.7 %collective-permute-start.24 = (bf16[144,2048]{1,0:T(8,128)(2,1)}, bf16[144,2048]{1,0:T(8,128)(2,1)S(1)}, u32[]{:S(2)}, u32[]{:S(2)}) collective-permute-start(bf16[144,2048]{1,0:T(8,128)(2,1)} %get-tuple-element.144), channel_id=1, source_target_pairs={{0,24},{8,16},{16,8},{24,0},{1,25},{9,17},{17,9},{25,1},{2,26},{10... | collective-permute-start | bytes 1769480 | tf_op jit(solution)/shard_map/ppermute | solution.py:67
  241.3 16.5 %collective-permute-start.25 = (bf16[144,2048]{1,0:T(8,128)(2,1)}, bf16[144,2048]{1,0:T(8,128)(2,1)S(1)}, u32[]{:S(2)}, u32[]{:S(2)}) collective-permute-start(bf16[144,2048]{1,0:T(8,128)(2,1)} %get-tuple-element.175.refs_0_), channel_id=1, source_target_pairs={{0,8},{8,0},{16,24},{24,16},{1,9},{9,1},{17,25},{25,17},{2,10},{10... | collective-permute-start | bytes 1769480 | tf_op jit(solution)/shard_map/ppermute | solution.py:67
  242.5 23.6 %collective-permute-start.26 = (bf16[144,2048]{1,0:T(8,128)(2,1)}, bf16[144,2048]{1,0:T(8,128)(2,1)S(1)}, u32[]{:S(2)}, u32[]{:S(2)}) collective-permute-start(bf16[144,2048]{1,0:T(8,128)(2,1)} %get-tuple-element.175.refs_0_), channel_id=1, source_target_pairs={{0,16},{8,24},{16,0},{24,8},{1,17},{9,25},{17,1},{25,9},{2,18},{10... | collective-permute-start | bytes 1769480 | tf_op jit(solution)/shard_map/ppermute | solution.py:67
  243.8 22.3 %collective-permute-start.27 = (bf16[144,2048]{1,0:T(8,128)(2,1)}, bf16[144,2048]{1,0:T(8,128)(2,1)S(1)}, u32[]{:S(2)}, u32[]{:S(2)}) collective-permute-start(bf16[144,2048]{1,0:T(8,128)(2,1)} %get-tuple-element.175.refs_0_), channel_id=1, source_target_pairs={{0,24},{8,16},{16,8},{24,0},{1,25},{9,17},{17,9},{25,1},{2,26},{10... | collective-permute-start | bytes 1769480 | tf_op jit(solution)/shard_map/ppermute | solution.py:67
  276.3 112.0 %all-gather.23.cloned.1.call-start = ((), (), s32[]{:S(2)}) async-start(), calls=%async_computation.9 | async-start | bytes 2359296 | tf_op jit(solution)/shard_map/all_gather | solution.py:102
  285.0 4.9 %collective-permute-start.28 = (f32[4,2048]{1,0:T(4,128)}, f32[4,2048]{1,0:T(4,128)S(1)}, u32[]{:S(2)}, u32[]{:S(2)}) collective-permute-start(f32[4,2048]{1,0:T(4,128)} %get-tuple-element.151.refs_0_), channel_id=1, source_target_pairs={{0,8},{8,0},{16,24},{24,16},{1,9},{9,1},{17,25},{25,17},{2,10},{10... | collective-permute-start | bytes 98312 | tf_op jit(solution)/shard_map/ppermute | solution.py:67
  286.6 4.1 collective-permute-start.29
  288.0 5.0 %collective-permute-start.30 = (f32[4,2048]{1,0:T(4,128)}, f32[4,2048]{1,0:T(4,128)S(1)}, u32[]{:S(2)}, u32[]{:S(2)}) collective-permute-start(f32[4,2048]{1,0:T(4,128)} %get-tuple-element.151.refs_0_), channel_id=1, source_target_pairs={{0,24},{8,16},{16,8},{24,0},{1,25},{9,17},{17,9},{25,1},{2,26},{10... | collective-permute-start | bytes 98312 | tf_op jit(solution)/shard_map/ppermute | solution.py:67
  300.3 11.1 %collective-permute-start.31 = (f32[4,2048]{1,0:T(4,128)}, f32[4,2048]{1,0:T(4,128)S(1)}, u32[]{:S(2)}, u32[]{:S(2)}) collective-permute-start(f32[4,2048]{1,0:T(4,128)} %get-tuple-element.169.refs_0_), channel_id=1, source_target_pairs={{0,8},{8,0},{16,24},{24,16},{1,9},{9,1},{17,25},{25,17},{2,10},{10... | collective-permute-start | bytes 98312 | tf_op jit(solution)/shard_map/ppermute | solution.py:67
  300.9 10.5 %collective-permute-start.32 = (f32[4,2048]{1,0:T(4,128)}, f32[4,2048]{1,0:T(4,128)S(1)}, u32[]{:S(2)}, u32[]{:S(2)}) collective-permute-start(f32[4,2048]{1,0:T(4,128)} %get-tuple-element.169.refs_0_), channel_id=1, source_target_pairs={{0,16},{8,24},{16,0},{24,8},{1,17},{9,25},{17,1},{25,9},{2,18},{10... | collective-permute-start | bytes 98312 | tf_op jit(solution)/shard_map/ppermute | solution.py:67
  301.4 10.0 %collective-permute-start.33 = (f32[4,2048]{1,0:T(4,128)}, f32[4,2048]{1,0:T(4,128)S(1)}, u32[]{:S(2)}, u32[]{:S(2)}) collective-permute-start(f32[4,2048]{1,0:T(4,128)} %get-tuple-element.169.refs_0_), channel_id=1, source_target_pairs={{0,24},{8,16},{16,8},{24,0},{1,25},{9,17},{17,9},{25,1},{2,26},{10... | collective-permute-start | bytes 98312 | tf_op jit(solution)/shard_map/ppermute | solution.py:67
  321.3 11.0 %collective-permute-start.34 = (bf16[4,12288]{1,0:T(4,128)(2,1)}, bf16[4,12288]{1,0:T(4,128)(2,1)S(1)}, u32[]{:S(2)}, u32[]{:S(2)}) collective-permute-start(bf16[4,12288]{1,0:T(4,128)(2,1)} %get-tuple-element.184.refs_0_), channel_id=1, source_target_pairs={{0,1},{1,0},{2,3},{3,2},{4,5},{5,4},{6,7},{7,6},{8,9},{9,8},{10,11... | collective-permute-start | bytes 294920 | tf_op jit(solution)/shard_map/ppermute | solution.py:73
  321.4 23.0 %collective-permute-start.37 = (bf16[32,2176]{1,0:T(8,128)(2,1)}, bf16[32,2176]{1,0:T(8,128)(2,1)S(1)}, u32[]{:S(2)}, u32[]{:S(2)}) collective-permute-start(bf16[32,2176]{1,0:T(8,128)(2,1)} %get-tuple-element.181), channel_id=1, source_target_pairs={{0,8},{8,0},{16,24},{24,16},{1,9},{9,1},{17,25},{25,17},{2,10},{10... | collective-permute-start | bytes 417800 | tf_op jit(solution)/shard_map/ppermute | solution.py:67
  322.0 22.4 %collective-permute-start.38 = (bf16[32,2176]{1,0:T(8,128)(2,1)}, bf16[32,2176]{1,0:T(8,128)(2,1)S(1)}, u32[]{:S(2)}, u32[]{:S(2)}) collective-permute-start(bf16[32,2176]{1,0:T(8,128)(2,1)} %get-tuple-element.182), channel_id=1, source_target_pairs={{0,16},{8,24},{16,0},{24,8},{1,17},{9,25},{17,1},{25,9},{2,18},{10... | collective-permute-start | bytes 417800 | tf_op jit(solution)/shard_map/ppermute | solution.py:67
  322.5 21.9 %collective-permute-start.39 = (bf16[32,2176]{1,0:T(8,128)(2,1)}, bf16[32,2176]{1,0:T(8,128)(2,1)S(1)}, u32[]{:S(2)}, u32[]{:S(2)}) collective-permute-start(bf16[32,2176]{1,0:T(8,128)(2,1)} %get-tuple-element.183), channel_id=1, source_target_pairs={{0,24},{8,16},{16,8},{24,0},{1,25},{9,17},{17,9},{25,1},{2,26},{10... | collective-permute-start | bytes 417800 | tf_op jit(solution)/shard_map/ppermute | solution.py:67
  324.9 19.4 %collective-permute-start.35 = (bf16[4,12288]{1,0:T(4,128)(2,1)}, bf16[4,12288]{1,0:T(4,128)(2,1)S(1)}, u32[]{:S(2)}, u32[]{:S(2)}) collective-permute-start(bf16[4,12288]{1,0:T(4,128)(2,1)} %get-tuple-element.184.refs_0_), channel_id=1, source_target_pairs={{0,2},{1,3},{2,0},{3,1},{4,6},{5,7},{6,4},{7,5},{8,10},{9,11},{10,... | collective-permute-start | bytes 294920 | tf_op jit(solution)/shard_map/ppermute | solution.py:73
  332.3 12.0 %collective-permute-start.36 = (bf16[4,12288]{1,0:T(4,128)(2,1)}, bf16[4,12288]{1,0:T(4,128)(2,1)S(1)}, u32[]{:S(2)}, u32[]{:S(2)}) collective-permute-start(bf16[4,12288]{1,0:T(4,128)(2,1)} %get-tuple-element.184.refs_0_), channel_id=1, source_target_pairs={{0,3},{1,2},{2,1},{3,0},{4,7},{5,6},{6,5},{7,4},{8,11},{9,10},{10,... | collective-permute-start | bytes 294920 | tf_op jit(solution)/shard_map/ppermute | solution.py:73
  346.8 1.9 collective-permute-start.40
  360.3 17.3 %collective-permute-start.43 = (bf16[144,1536]{1,0:T(8,128)(2,1)}, bf16[144,1536]{1,0:T(8,128)(2,1)S(1)}, u32[]{:S(2)}, u32[]{:S(2)}) collective-permute-start(bf16[144,1536]{1,0:T(8,128)(2,1)} %get-tuple-element.194), channel_id=1, source_target_pairs={{0,24},{8,16},{16,8},{24,0},{1,25},{9,17},{17,9},{25,1},{2,26},{10... | collective-permute-start | bytes 1327112 | tf_op jit(solution)/shard_map/ppermute | solution.py:67
  361.5 24.5 %collective-permute-start.42 = (bf16[144,1536]{1,0:T(8,128)(2,1)}, bf16[144,1536]{1,0:T(8,128)(2,1)S(1)}, u32[]{:S(2)}, u32[]{:S(2)}) collective-permute-start(bf16[144,1536]{1,0:T(8,128)(2,1)} %get-tuple-element.193), channel_id=1, source_target_pairs={{0,16},{8,24},{16,0},{24,8},{1,17},{9,25},{17,1},{25,9},{2,18},{10... | collective-permute-start | bytes 1327112 | tf_op jit(solution)/shard_map/ppermute | solution.py:67
  362.9 23.1 %collective-permute-start.41 = (bf16[144,1536]{1,0:T(8,128)(2,1)}, bf16[144,1536]{1,0:T(8,128)(2,1)S(1)}, u32[]{:S(2)}, u32[]{:S(2)}) collective-permute-start(bf16[144,1536]{1,0:T(8,128)(2,1)} %get-tuple-element.192), channel_id=1, source_target_pairs={{0,8},{8,0},{16,24},{24,16},{1,9},{9,1},{17,25},{25,17},{2,10},{10... | collective-permute-start | bytes 1327112 | tf_op jit(solution)/shard_map/ppermute | solution.py:67
  364.9 31.7 %all-to-all-start.3 = ((bf16[32,40,128]{2,1,0:T(8,128)(2,1)}), bf16[32,40,128]{2,1,0:T(8,128)(2,1)S(1)}, u32[]{:S(2)}, u32[]{:S(2)}) async-start(bf16[32,40,128]{2,1,0:T(8,128)(2,1)} %get-tuple-element.207), calls=%async_computation.3 | async-start | bytes 655360 | tf_op jit(solution)/shard_map/all_to_all | solution.py:91
  370.2 33.2 %collective-permute-start.47 = (bf16[32,5120]{1,0:T(8,128)(2,1)}, bf16[32,5120]{1,0:T(8,128)(2,1)}, u32[]{:S(2)}, u32[]{:S(2)}) collective-permute-start(bf16[32,5120]{1,0:T(8,128)(2,1)} %get-tuple-element.188.refs_0_), channel_id=1, source_target_pairs={{0,8},{8,0},{16,24},{24,16},{1,9},{9,1},{17,25},{25,17},{2,10},{10... | collective-permute-start | bytes 983048 | tf_op jit(solution)/shard_map/ppermute | solution.py:67
  372.0 32.1 %collective-permute-start.48 = (bf16[32,5120]{1,0:T(8,128)(2,1)}, bf16[32,5120]{1,0:T(8,128)(2,1)}, u32[]{:S(2)}, u32[]{:S(2)}) collective-permute-start(bf16[32,5120]{1,0:T(8,128)(2,1)} %get-tuple-element.188.refs_0_), channel_id=1, source_target_pairs={{0,16},{8,24},{16,0},{24,8},{1,17},{9,25},{17,1},{25,9},{2,18},{10... | collective-permute-start | bytes 983048 | tf_op jit(solution)/shard_map/ppermute | solution.py:67
  377.7 26.4 %collective-permute-start.49 = (bf16[32,5120]{1,0:T(8,128)(2,1)}, bf16[32,5120]{1,0:T(8,128)(2,1)}, u32[]{:S(2)}, u32[]{:S(2)}) collective-permute-start(bf16[32,5120]{1,0:T(8,128)(2,1)} %get-tuple-element.188.refs_0_), channel_id=1, source_target_pairs={{0,24},{8,16},{16,8},{24,0},{1,25},{9,17},{17,9},{25,1},{2,26},{10... | collective-permute-start | bytes 983048 | tf_op jit(solution)/shard_map/ppermute | solution.py:67
  393.6 16.2 %collective-permute-start.44 = (bf16[144,512]{1,0:T(8,128)(2,1)}, bf16[144,512]{1,0:T(8,128)(2,1)S(1)}, u32[]{:S(2)}, u32[]{:S(2)}) collective-permute-start(bf16[144,512]{1,0:T(8,128)(2,1)} %get-tuple-element.204), channel_id=1, source_target_pairs={{0,8},{8,0},{16,24},{24,16},{1,9},{9,1},{17,25},{25,17},{2,10},{10... | collective-permute-start | bytes 442376 | tf_op jit(solution)/shard_map/ppermute | solution.py:67
  395.2 14.7 %collective-permute-start.45 = (bf16[144,512]{1,0:T(8,128)(2,1)}, bf16[144,512]{1,0:T(8,128)(2,1)S(1)}, u32[]{:S(2)}, u32[]{:S(2)}) collective-permute-start(bf16[144,512]{1,0:T(8,128)(2,1)} %get-tuple-element.205), channel_id=1, source_target_pairs={{0,16},{8,24},{16,0},{24,8},{1,17},{9,25},{17,1},{25,9},{2,18},{10... | collective-permute-start | bytes 442376 | tf_op jit(solution)/shard_map/ppermute | solution.py:67
  403.4 6.4 %collective-permute-start.46 = (bf16[144,512]{1,0:T(8,128)(2,1)S(1)}, bf16[144,512]{1,0:T(8,128)(2,1)S(1)}, u32[]{:S(2)}, u32[]{:S(2)}) collective-permute-start(bf16[144,512]{1,0:T(8,128)(2,1)S(1)} %copy-done.63), channel_id=1, source_target_pairs={{0,24},{8,16},{16,8},{24,0},{1,25},{9,17},{17,9},{25,1},{2,26},{10... | collective-permute-start | bytes 442376 | tf_op jit(solution)/shard_map/ppermute | solution.py:67
  (61 other events, 400.3 us)
Sparse Core Ops, SparseCore 0:
  9.7 33.3 all-gather.12
  45.3 63.6 all-gather.14
  112.1 80.4 all-gather.16
  196.5 79.7 all-gather.18
  278.3 71.5 all-gather.20
  351.9 36.3 all-gather.22

commit v4 on v3

--- a/solution.py
+++ b/solution.py
@@ -448,7 +448,7 @@
     ff = (text_factors.shape[1] - 5 * span - width) // 2
     cut = ff + 3 * span
     factors[:, :cut] = text_factors[:, :cut]
-    factors[:, cut + 3 * span : -width] = text_factors[:, cut:]
+    factors[:, cut + 2 * span : -width] = text_factors[:, cut:]
     small[...] = jnp.zeros_like(small)
     small[3:4] = gain_m_row[...]
     held[...] = jnp.zeros_like(held)
@@ -490,7 +490,6 @@
     factors[:, cut + span : cut + 2 * span] = held[:tp, :span].astype(BF)
     queries = held[:, :span].astype(BF)
     zero_query = packed[0, free:, :span].astype(F32)[:1]
-    factors[:, cut + 2 * span : cut + 3 * span] = jnp.broadcast_to(zero_query, (tp, span)).astype(BF)
     key_spread = jnp.where(mask, zero_query, 0.0).astype(BF)
     value_spread = spreads[...].astype(BF)
     step = width // tp
@@ -548,13 +547,21 @@
         refs[-1][k] = ref[...]
 
 
-def unpack_kernel(planes, others, right, group, held):
+def unpack_kernel(local, planes, others, query, right, group, held):
     count, tp = planes.shape[:2]
     for k in range(count):
         held[k * tp : (k + 1) * tp] = planes[k].astype(F32)
         held[(count + k) * tp : (count + k + 1) * tp] = others[k].astype(F32)
-    right[...] = held[:, : right.shape[1]].astype(BF)
-    group[...] = held[:, right.shape[1] :].astype(BF)
+    cut, span = right.shape[1] - TILE, local * HDIM
+    right[:, :cut] = held[:, :cut].astype(BF)
+    total = jnp.sum(held[:, cut : cut + span], axis=0, keepdims=True)
+    group[...] = held[:, cut + span :].astype(BF)
+    held[:, :TILE] = jnp.zeros((held.shape[0], TILE), F32)
+    for h in range(local):
+        cols = slice(h * HDIM, (h + 1) * HDIM)
+        held[h : h + 1, :TILE] = total[:, cols]
+        held[local + h : local + h + 1, :TILE] = query[:1, cols].astype(F32)
+    right[:, cut:] = held[:, :TILE].astype(BF)
 
 
 def aligned(right, corner, tp):
@@ -568,7 +575,7 @@
 def columns_kernel(local, place, attn_left, text_left, one_left, entry, *refs):
     right, (grad_qkv, grad_kv, grad_cq, grad_up) = refs[:-4], refs[-4:]
     tp, span = len(right), local * HDIM
-    ff = right[0].shape[1] - 6 * span
+    ff = right[0].shape[1] - 4 * span - TILE
     ones = jnp.ones((right[0].shape[0], HDIM), BF)
     scale = HDIM ** (-0.5)
 
@@ -577,13 +584,11 @@
 
     for j in range(tp):
         at = place[0] ^ j
-        rows = aligned(right[j][...], place[1], tp)
-        part = [rows[:, ff + k * span : ff + (k + 1) * span] for k in range(6)]
+        rows = aligned(right[j][:, : ff + 4 * span], place[1], tp)
+        part = [rows[:, ff + k * span : ff + (k + 1) * span] for k in range(4)]
+        extra = right[j][:, ff + 4 * span :].astype(F32)
         grad_up[:, at_columns(at * ff, ff)] = dot_sum(one_left[at, 1], rows[:, :ff])
         grad_cq[:, at_columns(at * span, span)] = dot_sum(one_left[at, 0], part[0])
-        total = jnp.sum(part[4].astype(F32), axis=0, keepdims=True)
-        grad_qkv[:, at_columns(at * span, span)] = entry[...] * total
-        queries = part[5].astype(F32)[:1] * scale
         for h in range(local):
             cols = slice(h * HDIM, (h + 1) * HDIM)
             begin = at * span + h * HDIM
@@ -591,7 +596,8 @@
             grad_kv[:, at_columns(begin, HDIM)] = outer * scale
             outer = dot_sum(text_left[at, 1, h], part[2][:, cols])
             grad_kv[:, at_columns(tp * span + begin, HDIM)] = outer
-            outer = dot_sum(attn_left[at, 0, h], ones) * queries[:, cols]
+            grad_qkv[:, at_columns(begin, HDIM)] = entry[...] * extra[h : h + 1]
+            outer = dot_sum(attn_left[at, 0, h], ones) * (extra[local + h : local + h + 1] * scale)
             grad_qkv[:, at_columns(tp * span + begin, HDIM)] = outer
             outer = dot_sum(attn_left[at, 1, h], part[3][:, cols])
             grad_qkv[:, at_columns(2 * tp * span + begin, HDIM)] = outer
@@ -797,7 +803,7 @@
         "self_back",
         operands,
         [((2 * PAD, width + free), BF)] * tp
-        + [((world, count // 2, 2 * own), BF), ((tp, text_factors.shape[1] + 3 * span + width), BF)],
+        + [((world, count // 2, 2 * own), BF), ((tp, text_factors.shape[1] + 2 * span + width), BF)],
         [
             pltpu.VMEM(gathered.shape, BF),
             pltpu.VMEM(out_w.shape, BF),
@@ -817,14 +823,15 @@
     return in_vmem(stack_kernel, "stack", pieces, [(shape, BF)])[0]
 
 
-def unpack(planes, others, cut):
+def unpack(local, planes, others, query, cut):
     count, tp, wide = planes.shape
+    span = local * HDIM
     rows = 2 * count * tp
     return in_vmem(
-        unpack_kernel,
+        functools.partial(unpack_kernel, local),
         "unpack",
-        [planes, others],
-        [((rows, cut), BF), ((rows, wide - cut), BF)],
+        [planes, others, query],
+        [((rows, cut + TILE), BF), ((rows, wide - cut - span), BF)],
         [pltpu.VMEM((rows, wide), F32)],
     )
 
@@ -1046,7 +1053,9 @@
     pieces = [factors] + [me.other_plane(factors, k) for k in range(1, planes)]
     planes_of = stacked(after(tuple(pieces), (active, came)))
     lefts = me.to_rows(after(payload, planes_of))
-    right, group = unpack(planes_of, me.other_core(planes_of), ff + 6 * span)
+    right, group = unpack(
+        local, planes_of, me.other_core(planes_of), packed[0, free:, :span], ff + 4 * span
+    )
     right = [right] + [me.hop(right, j) for j in range(1, tp)]
 
     active, _ = lax.optimization_barrier((active, right[0]))

time: 424 us -> 424 us (level)
  transfers between devices with their start and end apart: 60 -> 60, of which waited for: 32 -> 30; matrix products, arithmetic and copies ran while one was open for 8% -> 8% of each run, Pallas kernels for 28% -> 28%
where the time goes in v4:
time: 424 us; the launch traced here: 418 us
  waiting for transfers between devices  167 us (39%)
  Pallas kernels  119 us (28%)
  starting transfers between devices  72.6 us (17%)
  local copies, waits for them, and re-layouts  26.6 us (6%)
  between operations  16.2 us (4%)
  other arithmetic  10.6 us (2%)
  matrix products  6.36 us (2%)
    ppermute x42, waiting for transfers between devices, hop(): return lax.ppermute(value, 'tp', [(i, i ^ j) for i in range(self.tp)])  123 us
    pallas_call x17, Pallas kernels, in_vmem(): pl.pallas_call(kernel, in_specs=[pl.BlockSpec(memory_space=spaces.get(k,...  98.9 us
    ppermute x42, starting transfers between devices, hop(): return lax.ppermute(value, 'tp', [(i, i ^ j) for i in range(self.tp)])  50.5 us
    all_gather x6, waiting for transfers between devices, gather_blocks(): return lax.all_gather(shard, ('core', 'fsdp'), axis=0)  16.3 us
    ppermute x6, waiting for transfers between devices, other_plane(): return lax.ppermute(value, 'fsdp', [(i, i ^ k) for i in range(self.planes)])  11.5 us
    pallas_call x1, Pallas kernels, mlp_up(): pl.pallas_call(functools.partial(up_kernel, tp), grid=(ff // step,), in_s...  11.2 us
    pallas_call x2, Pallas kernels, join(): pl.pallas_call(functools.partial(join_kernel, rows - PAD), grid=(rows //...  9.05 us
  transfers between devices with their start and end apart: 60, of which 30 were waited for; matrix products, arithmetic and copies ran while one was open for 8% of the time, Pallas kernels for 28%

profile of v4, /device:TPU:0, one launch (start us, length us, event | category | flops | bytes accessed | tf_op | source)
XLA Modules:
  0.0 418.2 jit_solution(17078171808250775102)
XLA Ops:
  8.6 2.1 parts.1
  10.7 2.9 collective-permute-start
  16.1 3.5 collective-permute-done.refs_1_
  19.6 4.8 %collective-permute-done.1.refs_2_ = bf16[64,1536]{1,0:T(8,128)(2,1)S(1)} collective-permute-done((bf16[64,1536]{1,0:T(8,128)(2,1)}, bf16[64,1536]{1,0:T(8,128)(2,1)S(1)}, u32[]{:S(2)}, u32[]{:S(2)}) %collective-permute-start.1) | collective-permute-done | bytes 196640 | tf_op jit(solution)/shard_map/ppermute | solution.py:67
  25.2 2.2 assemble.1
  27.4 1.6 collective-permute-start.3
  28.9 2.6 collective-permute-start.4
  31.9 2.7 collective-permute-done.4
  34.6 2.7 collective-permute-done.5
  38.7 4.4 %all-gather.13.cloned.1.call-done = bf16[512,2048]{1,0:T(8,128)(2,1)} async-done(((bf16[64,2048]{1,0:T(8,128)(2,1)}), bf16[512,2048]{1,0:T(8,128)(2,1)}) %all-gather.13.cloned.1.call-update) | async-done | bytes 2097168 | tf_op jit(solution)/shard_map/all_gather | solution.py:102
  43.4 2.4 collective-permute-start.9
  48.7 1.8 collective-permute-done.8
  51.2 2.2 column_blocks.3
  56.0 3.5 all-to-all-start
  61.3 2.0 collective-permute-start.10
  66.2 1.7 column_blocks.4
  68.5 14.4 %collective-permute-done.10.refs_1_.refs_5_ = bf16[128,2048]{1,0:T(8,128)(2,1)S(1)} collective-permute-done((bf16[128,2048]{1,0:T(8,128)(2,1)S(1)}, bf16[128,2048]{1,0:T(8,128)(2,1)S(1)}, u32[]{:S(2)}, u32[]{:S(2)}) %collective-permute-start.10) | collective-permute-done | bytes 524320 | tf_op jit(solution)/shard_map/ppermute | solution.py:67
  83.8 9.8 %collective-permute-done.12.refs_3_.refs_7_ = bf16[128,2048]{1,0:T(8,128)(2,1)} collective-permute-done((bf16[128,2048]{1,0:T(8,128)(2,1)S(1)}, bf16[128,2048]{1,0:T(8,128)(2,1)}, u32[]{:S(2)}, u32[]{:S(2)}) %collective-permute-start.12) | collective-permute-done | bytes 524320 | tf_op jit(solution)/shard_map/ppermute | solution.py:67
  93.6 2.3 column_blocks.5
  95.9 3.5 all-to-all-start.2
  102.0 2.1 pad_maximum_fusion.1
  104.1 7.9 %all-to-all-done.2 = bf16[4,64,2048]{2,1,0:T(8,128)(2,1)S(1)} async-done(((bf16[4,64,2048]{2,1,0:T(8,128)(2,1)}), bf16[4,64,2048]{2,1,0:T(8,128)(2,1)S(1)}, u32[]{:S(2)}, u32[]{:S(2)}) %all-to-all-start.2) | async-done | bytes 1048608 | tf_op jit(solution)/shard_map/all_to_all | solution.py:99
  118.3 17.2 %self_attention.1 = (bf16[144,2048]{1,0:T(8,128)(2,1)}, bf16[144,2048]{1,0:T(8,128)(2,1)}, bf16[144,2048]{1,0:T(8,128)(2,1)}, bf16[144,2048]{1,0:T(8,128)(2,1)},...) custom-call(bf16[128,2048]{1,0:T(8,128)(2,1)} %copy-done.2, ...), custom_call_target="tpu_custom_call" | custom-call | flops 1 | bytes 1 | tf_op jit(solution)/shard_map/self_attention/pallas_call | solution.py:612
  135.5 2.8 collective-permute-done.14.refs_6_.refs_15_
  139.2 1.7 collective-permute-start.16
  144.1 3.3 all-to-all-start.1
  148.8 6.2 %all-to-all-done.1 = f32[8,4,256]{2,1,0:T(4,128)S(1)} async-done(((f32[8,4,256]{2,1,0:T(4,128)}), f32[8,4,256]{2,1,0:T(4,128)S(1)}, u32[]{:S(2)}, u32[]{:S(2)}) %all-to-all-start.1) | async-done | bytes 32800 | tf_op jit(solution)/shard_map/all_to_all | solution.py:976
  155.6 8.8 %collective-permute-done.17.refs_2_ = bf16[144,2048]{1,0:T(8,128)(2,1)} collective-permute-done((bf16[144,2048]{1,0:T(8,128)(2,1)}, bf16[144,2048]{1,0:T(8,128)(2,1)}, u32[]{:S(2)}, u32[]{:S(2)}) %collective-permute-start.17) | collective-permute-done | bytes 589856 | tf_op jit(solution)/shard_map/ppermute | solution.py:67
  164.4 1.9 collective-permute-done.18.refs_3_
  166.3 4.5 %join.2 = (f32[144,2048]{1,0:T(8,128)}, bf16[144,2048]{1,0:T(8,128)(2,1)}) custom-call(f32[144,2048]{1,0:T(8,128)} %get-tuple-element.125.base.rows, f32[1,2048]{1,0:T(1,128)} %slice.173.gain, bf16[144,2048]{1,0:T(8,128)(2,1)} %get-tuple-element.132.refs_0_, bf16[144,2048]{1,0:T(8,128)(2,1)} %copy-done.18, ...), custom_call_target="tpu_custom_call" | custom-call | flops 1 | bytes 1 | tf_op jit(solution)/shard_map/join/pallas_call | solution.py:865
  171.5 1.7 collective-permute-start.20
  174.4 13.0 %collective-permute-done.19.refs_1_ = bf16[144,2048]{1,0:T(8,128)(2,1)S(1)} collective-permute-done((bf16[144,2048]{1,0:T(8,128)(2,1)}, bf16[144,2048]{1,0:T(8,128)(2,1)S(1)}, u32[]{:S(2)}, u32[]{:S(2)}) %collective-permute-start.19) | collective-permute-done | bytes 589856 | tf_op jit(solution)/shard_map/ppermute | solution.py:67
  187.4 9.0 %collective-permute-done.20.refs_2_ = bf16[144,2048]{1,0:T(8,128)(2,1)S(1)} collective-permute-done((bf16[144,2048]{1,0:T(8,128)(2,1)}, bf16[144,2048]{1,0:T(8,128)(2,1)S(1)}, u32[]{:S(2)}, u32[]{:S(2)}) %collective-permute-start.20) | collective-permute-done | bytes 589856 | tf_op jit(solution)/shard_map/ppermute | solution.py:67
  197.4 14.2 %cross_attention.1 = (bf16[144,2048]{1,0:T(8,128)(2,1)}, bf16[144,2048]{1,0:T(8,128)(2,1)}, bf16[144,2048]{1,0:T(8,128)(2,1)}, bf16[144,2048]{1,0:T(8,128)(2,1)}...) custom-call(bf16[144,2048]{1,0:T(8,128)(2,1)} %get-tuple-element.137, ...), custom_call_target="tpu_custom_call" | custom-call | flops 1 | bytes 1 | tf_op jit(solution)/shard_map/cross_attention/pallas_call | solution.py:612
  211.6 1.7 collective-permute-start.22
  213.3 1.9 collective-permute-start.24
  215.8 12.3 %collective-permute-done.22.refs_1_ = bf16[144,2048]{1,0:T(8,128)(2,1)S(1)} collective-permute-done((bf16[144,2048]{1,0:T(8,128)(2,1)}, bf16[144,2048]{1,0:T(8,128)(2,1)S(1)}, u32[]{:S(2)}, u32[]{:S(2)}) %collective-permute-start.22) | collective-permute-done | bytes 589856 | tf_op jit(solution)/shard_map/ppermute | solution.py:67
  228.1 7.0 %collective-permute-done.23.refs_2_ = bf16[144,2048]{1,0:T(8,128)(2,1)S(1)} collective-permute-done((bf16[144,2048]{1,0:T(8,128)(2,1)}, bf16[144,2048]{1,0:T(8,128)(2,1)S(1)}, u32[]{:S(2)}, u32[]{:S(2)}) %collective-permute-start.23) | collective-permute-done | bytes 589856 | tf_op jit(solution)/shard_map/ppermute | solution.py:67
  236.8 4.5 %join.3 = (f32[144,2048]{1,0:T(8,128)}, bf16[144,2048]{1,0:T(8,128)(2,1)}) custom-call(f32[144,2048]{1,0:T(8,128)} %get-tuple-element.136.base, f32[1,2048]{1,0:T(1,128)} %slice.178.gain, bf16[144,2048]{1,0:T(8,128)(2,1)} %get-tuple-element.141.refs_0_, bf16[144,2048]{1,0:T(8,128)(2,1)} %copy-done.19, bf16[144,2048]{1,0:T(8,128)(2,1)} %copy-done.20, ...), custom_call_target="tpu_custom_call" | custom-call | flops 1 | bytes 1 | tf_op jit(solution)/shard_map/join/pallas_call | solution.py:865
  245.8 12.0 %collective-permute-done.25.refs_1_ = bf16[144,2048]{1,0:T(8,128)(2,1)S(1)} collective-permute-done((bf16[144,2048]{1,0:T(8,128)(2,1)}, bf16[144,2048]{1,0:T(8,128)(2,1)S(1)}, u32[]{:S(2)}, u32[]{:S(2)}) %collective-permute-start.25) | collective-permute-done | bytes 589856 | tf_op jit(solution)/shard_map/ppermute | solution.py:67
  257.8 8.2 %collective-permute-done.26.refs_2_ = bf16[144,2048]{1,0:T(8,128)(2,1)S(1)} collective-permute-done((bf16[144,2048]{1,0:T(8,128)(2,1)}, bf16[144,2048]{1,0:T(8,128)(2,1)S(1)}, u32[]{:S(2)}, u32[]{:S(2)}) %collective-permute-start.26) | collective-permute-done | bytes 589856 | tf_op jit(solution)/shard_map/ppermute | solution.py:67
  266.1 10.2 %all-gather.19.cloned.1.call-done = bf16[32,64,2048]{2,1,0:T(8,128)(2,1)} async-done(((bf16[4,64,2048]{2,1,0:T(8,128)(2,1)}), bf16[32,64,2048]{2,1,0:T(8,128)(2,1)}) %all-gather.19.cloned.1.call-update) | async-done | bytes 8388624 | tf_op jit(solution)/shard_map/all_gather | solution.py:102
  277.2 7.7 %mlp_back.1 = (bf16[16,2048]{1,0:T(8,128)(2,1)}, bf16[16,2048]{1,0:T(8,128)(2,1)}, f32[4,2048]{1,0:T(4,128)}, f32[4,2048]{1,0:T(4,128)}, f32[4,2048]{1,0:T(4,128)}) custom-call(bf16[144,2048]{1,0:T(8,128)(2,1)} %get-tuple-element.175.refs_0_, bf16[144,2048]{1,0:T(8,128)(2,1)} %copy-done.5, bf16[144,2048]{1,0:T(8,128)(2,1)} %copy-done.6, ...), custom_call_target="tpu_custom_call" | custom-call | flops 1 | bytes 1 | tf_op jit(solution)/shard_map/mlp_back/pallas_call | solution.py:612
  285.0 1.6 collective-permute-start.28
  290.7 2.4 collective-permute-done.30.refs_3_
  293.7 6.6 %cross_back.1 = (f32[4,2048]{1,0:T(4,128)}, f32[4,512]{1,0:T(4,128)}, f32[4,8,128]{2,1,0:T(8,128)}, f32[4,512]{1,0:T(4,128)}, f32[4,2048]{1,0:T(4,128)}, /*index=5*/f32[1,2048]{1,0:T(1,128)}) custom-call(f32[4,2048]{1,0:T(4,128)} %slice_bitcast_fusion.base, f32[4,2048]{1,0:T(4,128)} %get-tuple-element.148.rows, f32[1,2048]{1,0:T(1,128)} %slice.178.gain, ...), custom_call_target="tpu_custom_call" | custom-call | flops 1 | bytes 1 | tf_op jit(solution)/shard_map/cross_back/pallas_call | solution.py:612
  301.4 2.5 collective-permute-start.33
  305.2 6.2 %text_back.1 = (bf16[16,2176]{1,0:T(8,128)(2,1)}, bf16[16,2176]{1,0:T(8,128)(2,1)}, bf16[16,2176]{1,0:T(8,128)(2,1)}, bf16[16,2176]{1,0:T(8,128)(2,1)}, f32[40,2048]{1,0:T(8,128)}, /*index=5*/bf16[4,8704]{1,0:T(4,128)(2,1)}) custom-call(f32[4,8,128]{2,1,0:T(8,128)} %get-tuple-element.156.refs_0_, f32[4,8,128]{2,1,0:T(8,128)} %get-tuple-element.150.probs.refs_1_, ...), custom_call_target="tpu_custom_call" | custom-call | flops 1 | bytes 1 | tf_op jit(solution)/shard_map/text_back/pallas_call | solution.py:612
  312.1 9.2 %self_back.1 = (bf16[32,2176]{1,0:T(8,128)(2,1)}, bf16[32,2176]{1,0:T(8,128)(2,1)}, bf16[32,2176]{1,0:T(8,128)(2,1)}, bf16[32,2176]{1,0:T(8,128)(2,1)}, bf16[32,...) custom-call(f32[4,2048]{1,0:T(4,128)} %get-tuple-element.152.refs_12_.base, f32[4,2048]{1,0:T(4,128)} %get-tuple-element.153.rows, ...), custom_call_target="tpu_custom_call" | custom-call | flops 1 | bytes 1 | tf_op jit(solution)/shard_map/self_back/pallas_call | solution.py:612
  322.5 2.4 collective-permute-start.39
  326.1 6.0 %collective-permute-done.34.refs_1_ = bf16[4,11776]{1,0:T(4,128)(2,1)S(1)} collective-permute-done((bf16[4,11776]{1,0:T(4,128)(2,1)}, bf16[4,11776]{1,0:T(4,128)(2,1)S(1)}, u32[]{:S(2)}, u32[]{:S(2)}) %collective-permute-start.34) | collective-permute-done | bytes 94240 | tf_op jit(solution)/shard_map/ppermute | solution.py:73
  332.9 11.2 %mlp_up.1.active = bf16[576,2048]{1,0:T(8,128)(2,1)} custom-call(bf16[144,2048]{1,0:T(8,128)(2,1)} %get-tuple-element.175.refs_0_, bf16[144,2048]{1,0:T(8,128)(2,1)} %copy-done.5, bf16[144,2048]{1,0:T(8,128)(2,1)} %copy-done.6, bf16[144,2048]{1,0:T(8,128)(2,1)} %copy-done.7, bf16[8,4,64,2048]{3,2,1,0:T(8,128)(2,1)} %bitcast.126), custom_call_target="tpu_custom_call" | custom-call | flops 1 | bytes 1 | tf_op jit(solution)/shard_map/mlp_up/pallas_call | solution.py:706
  344.8 1.8 stack.53.planes
  349.4 2.2 unpack.1
  351.6 8.5 %mlp_down.2 = (bf16[144,1536]{1,0:T(8,128)(2,1)}, bf16[144,1536]{1,0:T(8,128)(2,1)}, bf16[144,1536]{1,0:T(8,128)(2,1)}, bf16[144,1536]{1,0:T(8,128)(2,1)}) custom-call(bf16[576,2048]{1,0:T(8,128)(2,1)} %mlp_up.1.active, bf16[8,256,1536]{2,1,0:T(8,128)(2,1)} %bitcast.131), custom_call_target="tpu_custom_call" | custom-call | flops 1 | bytes 1 | tf_op jit(solution)/shard_map/mlp_down/pallas_call | solution.py:612
  364.7 4.1 all-to-all-start.3
  369.7 1.8 collective-permute-start.47
  373.0 4.2 %tokens_back.1 = (bf16[256,2048]{1,0:T(8,128)(2,1)}, bf16[128,2048]{1,0:T(8,128)(2,1)}) custom-call(f32[144,2048]{1,0:T(8,128)} %get-tuple-element.125.base.rows, f32[1,2048]{1,0:T(1,128)} %slice.182.gain_a.gain, bf16[256,128]{1,0:T(8,128)(2,1)} %copy-done.17, bf16[32,2176]{1,0:T(8,128)(2,1)} %get-tuple-element.196.refs_0_, bf16[32,2176]{1,0:T(8,128)(2,1)} %copy-done.38, ...), custom_call_target="tpu_custom_call" | custom-call | flops 1 | bytes 1 | tf_op jit(solution)/shard_map/tokens_back/pallas_call | solution.py:612
  377.4 8.7 %collective-permute-done.42 = bf16[144,1536]{1,0:T(8,128)(2,1)S(1)} collective-permute-done((bf16[144,1536]{1,0:T(8,128)(2,1)}, bf16[144,1536]{1,0:T(8,128)(2,1)S(1)}, u32[]{:S(2)}, u32[]{:S(2)}) %collective-permute-start.42) | collective-permute-done | bytes 442400 | tf_op jit(solution)/shard_map/ppermute | solution.py:67
  386.3 1.7 all-gather.23.cloned.1.call-done
  388.0 5.3 %mlp_down.3 = (bf16[144,512]{1,0:T(8,128)(2,1)}, bf16[144,512]{1,0:T(8,128)(2,1)}, bf16[144,512]{1,0:T(8,128)(2,1)}, bf16[144,512]{1,0:T(8,128)(2,1)}) custom-call(bf16[576,2048]{1,0:T(8,128)(2,1)} %mlp_up.1.active, bf16[8,256,512]{2,1,0:T(8,128)(2,1)} %bitcast.132), custom_call_target="tpu_custom_call" | custom-call | flops 1 | bytes 1 | tf_op jit(solution)/shard_map/mlp_down/pallas_call | solution.py:612
  393.4 1.5 collective-permute-start.44
  401.4 1.8 fusion.26
  403.8 5.2 %columns.1 = (f32[64,6144]{1,0:T(8,128)}, f32[64,4096]{1,0:T(8,128)}, f32[64,2048]{1,0:T(8,128)}, f32[64,8192]{1,0:T(8,128)}) custom-call(s32[2]{0:T(128)} %pad_add_fusion.place, bf16[4,2,4,32,64]{4,3,2,1,0:T(8,128)(2,1)} %bitcast.144, bf16[4,2,4,32,64]{4,3,2,1,0:T(8,128)(2,1)} %bitcast.145, bf16[4,2,32,64]{3,2,1,0:T(8,128)(2,1)} %bitcast.157, ...), custom_call_target="tpu_custom_call" | custom-call | flops 1 | bytes 1 | tf_op jit(solution)/shard_map/columns/pallas_call | solution.py:612
  (330 shorter events, 74.1 us)
Async XLA Ops:
  7.2 39.8 %copy-start = (bf16[256,2048]{1,0:T(8,128)(2,1)S(1)}, bf16[256,2048]{1,0:T(8,128)(2,1)}, u32[]{:S(2)}) copy-start(bf16[256,2048]{1,0:T(8,128)(2,1)} %param.16) | copy-start | bytes 3145732
  7.2 35.8 %all-gather.13.cloned.1.call-start = ((), (), s32[]{:S(2)}) async-start(), calls=%async_computation.4 | async-start | bytes 2359296 | tf_op jit(solution)/shard_map/all_gather | solution.py:102
  8.0 104.0 %all-gather.15.cloned.1.call-start = ((), (), s32[]{:S(2)}) async-start(), calls=%async_computation.5 | async-start | bytes 7077888 | tf_op jit(solution)/shard_map/all_gather | solution.py:102
  10.7 8.9 %collective-permute-start = (bf16[64,1536]{1,0:T(8,128)(2,1)}, bf16[64,1536]{1,0:T(8,128)(2,1)S(1)}, u32[]{:S(2)}, u32[]{:S(2)}) collective-permute-start(bf16[64,1536]{1,0:T(8,128)(2,1)} %get-tuple-element.118), channel_id=1, source_target_pairs={{0,8},{8,0},{16,24},{24,16},{1,9},{9,1},{17,25},{25,17},{2,10},{10... | collective-permute-start | bytes 589832 | tf_op jit(solution)/shard_map/ppermute | solution.py:67
  13.7 10.8 %collective-permute-start.1 = (bf16[64,1536]{1,0:T(8,128)(2,1)}, bf16[64,1536]{1,0:T(8,128)(2,1)S(1)}, u32[]{:S(2)}, u32[]{:S(2)}) collective-permute-start(bf16[64,1536]{1,0:T(8,128)(2,1)} %get-tuple-element.119), channel_id=1, source_target_pairs={{0,16},{8,24},{16,0},{24,8},{1,17},{9,25},{17,1},{25,9},{2,18},{10... | collective-permute-start | bytes 589832 | tf_op jit(solution)/shard_map/ppermute | solution.py:67
  15.2 9.3 %collective-permute-start.2 = (bf16[64,1536]{1,0:T(8,128)(2,1)}, bf16[64,1536]{1,0:T(8,128)(2,1)S(1)}, u32[]{:S(2)}, u32[]{:S(2)}) collective-permute-start(bf16[64,1536]{1,0:T(8,128)(2,1)} %get-tuple-element.120), channel_id=1, source_target_pairs={{0,24},{8,16},{16,8},{24,0},{1,25},{9,17},{17,9},{25,1},{2,26},{10... | collective-permute-start | bytes 589832 | tf_op jit(solution)/shard_map/ppermute | solution.py:67
  27.4 4.5 %collective-permute-start.3 = (f32[2432]{0:T(1024)S(1)}, f32[2432]{0:T(1024)S(1)}, u32[]{:S(2)}, u32[]{:S(2)}) collective-permute-start(f32[2432]{0:T(1024)S(1)} %pad_maximum_fusion.13), channel_id=1, source_target_pairs={{0,1},{1,0},{2,3},{3,2},{4,5},{5,4},{6,7},{7,6},{8,9},{9,8},{10,11... | collective-permute-start | bytes 29192 | tf_op jit(solution)/shard_map/ppermute | solution.py:73
  28.9 5.6 %collective-permute-start.4 = (f32[2432]{0:T(1024)S(1)}, f32[2432]{0:T(1024)S(1)}, u32[]{:S(2)}, u32[]{:S(2)}) collective-permute-start(f32[2432]{0:T(1024)S(1)} %pad_maximum_fusion.13), channel_id=1, source_target_pairs={{0,2},{1,3},{2,0},{3,1},{4,6},{5,7},{6,4},{7,5},{8,10},{9,11},{10,... | collective-permute-start | bytes 29192 | tf_op jit(solution)/shard_map/ppermute | solution.py:73
  31.5 5.7 %collective-permute-start.5 = (f32[2432]{0:T(1024)S(1)}, f32[2432]{0:T(1024)S(1)}, u32[]{:S(2)}, u32[]{:S(2)}) collective-permute-start(f32[2432]{0:T(1024)S(1)} %pad_maximum_fusion.13), channel_id=1, source_target_pairs={{0,3},{1,2},{2,1},{3,0},{4,7},{5,6},{6,5},{7,4},{8,11},{9,10},{10,... | collective-permute-start | bytes 29192 | tf_op jit(solution)/shard_map/ppermute | solution.py:73
  37.3 1.3 collective-permute-start.6
  43.4 7.4 %collective-permute-start.9 = (f32[8,2432]{1,0:T(8,128)S(1)}, f32[8,2432]{1,0:T(8,128)S(1)}, u32[]{:S(2)}, u32[]{:S(2)}) collective-permute-start(f32[8,2432]{1,0:T(8,128)S(1)} %concatenate.111), channel_id=1, source_target_pairs={{0,24},{8,16},{16,8},{24,0},{1,25},{9,17},{17,9},{25,1},{2,26},{10... | collective-permute-start | bytes 233480 | tf_op jit(solution)/shard_map/ppermute | solution.py:67
  45.8 4.7 %collective-permute-start.8 = (f32[8,2432]{1,0:T(8,128)S(1)}, f32[8,2432]{1,0:T(8,128)S(1)}, u32[]{:S(2)}, u32[]{:S(2)}) collective-permute-start(f32[8,2432]{1,0:T(8,128)S(1)} %concatenate.111), channel_id=1, source_target_pairs={{0,16},{8,24},{16,0},{24,8},{1,17},{9,25},{17,1},{25,9},{2,18},{10... | collective-permute-start | bytes 233480 | tf_op jit(solution)/shard_map/ppermute | solution.py:67
  46.4 4.4 %collective-permute-start.7 = (f32[8,2432]{1,0:T(8,128)S(1)}, f32[8,2432]{1,0:T(8,128)S(1)}, u32[]{:S(2)}, u32[]{:S(2)}) collective-permute-start(f32[8,2432]{1,0:T(8,128)S(1)} %concatenate.111), channel_id=1, source_target_pairs={{0,8},{8,0},{16,24},{24,16},{1,9},{9,1},{17,25},{25,17},{2,10},{10... | collective-permute-start | bytes 233480 | tf_op jit(solution)/shard_map/ppermute | solution.py:67
  56.0 37.6 %all-to-all-start = ((bf16[4,64,1536]{2,1,0:T(8,128)(2,1)}), bf16[4,64,1536]{2,1,0:T(8,128)(2,1)S(1)}, u32[]{:S(2)}, u32[]{:S(2)}) async-start(bf16[4,64,1536]{2,1,0:T(8,128)(2,1)} %column_blocks.3), calls=%async_computation | async-start | bytes 1572864 | tf_op jit(solution)/shard_map/all_to_all | solution.py:99
  61.3 34.6 %copy-start.2 = (bf16[128,2048]{1,0:T(8,128)(2,1)}, bf16[128,2048]{1,0:T(8,128)(2,1)S(1)}, u32[]{:S(2)}) copy-start(bf16[128,2048]{1,0:T(8,128)(2,1)S(1)} %slice.223.refs_0_.refs_4_) | copy-start | bytes 1572868
  61.3 21.7 %collective-permute-start.10 = (bf16[128,2048]{1,0:T(8,128)(2,1)S(1)}, bf16[128,2048]{1,0:T(8,128)(2,1)S(1)}, u32[]{:S(2)}, u32[]{:S(2)}) collective-permute-start(bf16[128,2048]{1,0:T(8,128)(2,1)S(1)} %slice.223.refs_0_.refs_4_), channel_id=1, source_target_pairs={{0,8},{8,0},{16,24},{24,16},{1,9},{9,1},{17,25},{25,17},{2,10},{10... | collective-permute-start | bytes 1572872 | tf_op jit(solution)/shard_map/ppermute | solution.py:67
  63.3 19.6 %collective-permute-start.11 = (bf16[128,2048]{1,0:T(8,128)(2,1)S(1)}, bf16[128,2048]{1,0:T(8,128)(2,1)S(1)}, u32[]{:S(2)}, u32[]{:S(2)}) collective-permute-start(bf16[128,2048]{1,0:T(8,128)(2,1)S(1)} %slice.223.refs_0_.refs_4_), channel_id=1, source_target_pairs={{0,16},{8,24},{16,0},{24,8},{1,17},{9,25},{17,1},{25,9},{2,18},{10... | collective-permute-start | bytes 1572872 | tf_op jit(solution)/shard_map/ppermute | solution.py:67
  64.8 28.8 %collective-permute-start.12 = (bf16[128,2048]{1,0:T(8,128)(2,1)S(1)}, bf16[128,2048]{1,0:T(8,128)(2,1)}, u32[]{:S(2)}, u32[]{:S(2)}) collective-permute-start(bf16[128,2048]{1,0:T(8,128)(2,1)S(1)} %slice.223.refs_0_.refs_4_), channel_id=1, source_target_pairs={{0,24},{8,16},{16,8},{24,0},{1,25},{9,17},{17,9},{25,1},{2,26},{10... | collective-permute-start | bytes 1572872 | tf_op jit(solution)/shard_map/ppermute | solution.py:67
  95.9 16.1 %all-to-all-start.2 = ((bf16[4,64,2048]{2,1,0:T(8,128)(2,1)}), bf16[4,64,2048]{2,1,0:T(8,128)(2,1)S(1)}, u32[]{:S(2)}, u32[]{:S(2)}) async-start(bf16[4,64,2048]{2,1,0:T(8,128)(2,1)} %column_blocks.5), calls=%async_computation.2 | async-start | bytes 2097152 | tf_op jit(solution)/shard_map/all_to_all | solution.py:99
  99.4 96.9 %all-gather.17.cloned.1.call-start = ((), (), s32[]{:S(2)}) async-start(), calls=%async_computation.6 | async-start | bytes 9437184 | tf_op jit(solution)/shard_map/all_gather | solution.py:102
  114.1 21.4 %collective-permute-start.13 = (bf16[128,2048]{1,0:T(8,128)(2,1)S(1)}, bf16[128,2048]{1,0:T(8,128)(2,1)S(1)}, u32[]{:S(2)}, u32[]{:S(2)}) collective-permute-start(bf16[128,2048]{1,0:T(8,128)(2,1)S(1)} %bitcast.135), channel_id=1, source_target_pairs={{0,8},{8,0},{16,24},{24,16},{1,9},{9,1},{17,25},{25,17},{2,10},{10... | collective-permute-start | bytes 1572872 | tf_op jit(solution)/shard_map/ppermute | solution.py:67
  115.6 22.7 %collective-permute-start.14 = (bf16[128,2048]{1,0:T(8,128)(2,1)S(1)}, bf16[128,2048]{1,0:T(8,128)(2,1)S(1)}, u32[]{:S(2)}, u32[]{:S(2)}) collective-permute-start(bf16[128,2048]{1,0:T(8,128)(2,1)S(1)} %bitcast.136), channel_id=1, source_target_pairs={{0,16},{8,24},{16,0},{24,8},{1,17},{9,25},{17,1},{25,9},{2,18},{10... | collective-permute-start | bytes 1572872 | tf_op jit(solution)/shard_map/ppermute | solution.py:67
  116.1 22.2 %collective-permute-start.15 = (bf16[128,2048]{1,0:T(8,128)(2,1)S(1)}, bf16[128,2048]{1,0:T(8,128)(2,1)S(1)}, u32[]{:S(2)}, u32[]{:S(2)}) collective-permute-start(bf16[128,2048]{1,0:T(8,128)(2,1)S(1)} %bitcast.137), channel_id=1, source_target_pairs={{0,24},{8,16},{16,8},{24,0},{1,25},{9,17},{17,9},{25,1},{2,26},{10... | collective-permute-start | bytes 1572872 | tf_op jit(solution)/shard_map/ppermute | solution.py:67
  135.5 35.3 %copy-start.11 = (bf16[128,2048]{1,0:T(8,128)(2,1)}, bf16[128,2048]{1,0:T(8,128)(2,1)S(1)}, u32[]{:S(2)}) copy-start(bf16[128,2048]{1,0:T(8,128)(2,1)S(1)} %collective-permute-done.13.refs_5_.refs_14_) | copy-start | bytes 1572868
  138.3 32.5 %copy-start.12 = (bf16[128,2048]{1,0:T(8,128)(2,1)}, bf16[128,2048]{1,0:T(8,128)(2,1)S(1)}, u32[]{:S(2)}) copy-start(bf16[128,2048]{1,0:T(8,128)(2,1)S(1)} %collective-permute-done.14.refs_6_.refs_15_) | copy-start | bytes 1572868
  139.2 16.5 %collective-permute-start.16 = (bf16[144,2048]{1,0:T(8,128)(2,1)}, bf16[144,2048]{1,0:T(8,128)(2,1)S(1)}, u32[]{:S(2)}, u32[]{:S(2)}) collective-permute-start(bf16[144,2048]{1,0:T(8,128)(2,1)} %get-tuple-element.133), channel_id=1, source_target_pairs={{0,8},{8,0},{16,24},{24,16},{1,9},{9,1},{17,25},{25,17},{2,10},{10... | collective-permute-start | bytes 1769480 | tf_op jit(solution)/shard_map/ppermute | solution.py:67
  140.8 23.6 %collective-permute-start.17 = (bf16[144,2048]{1,0:T(8,128)(2,1)}, bf16[144,2048]{1,0:T(8,128)(2,1)}, u32[]{:S(2)}, u32[]{:S(2)}) collective-permute-start(bf16[144,2048]{1,0:T(8,128)(2,1)} %get-tuple-element.134), channel_id=1, source_target_pairs={{0,16},{8,24},{16,0},{24,8},{1,17},{9,25},{17,1},{25,9},{2,18},{10... | collective-permute-start | bytes 1769480 | tf_op jit(solution)/shard_map/ppermute | solution.py:67
  141.1 25.2 %collective-permute-start.18 = (bf16[144,2048]{1,0:T(8,128)(2,1)}, bf16[144,2048]{1,0:T(8,128)(2,1)}, u32[]{:S(2)}, u32[]{:S(2)}) collective-permute-start(bf16[144,2048]{1,0:T(8,128)(2,1)} %get-tuple-element.135), channel_id=1, source_target_pairs={{0,24},{8,16},{16,8},{24,0},{1,25},{9,17},{17,9},{25,1},{2,26},{10... | collective-permute-start | bytes 1769480 | tf_op jit(solution)/shard_map/ppermute | solution.py:67
  144.1 11.0 %all-to-all-start.1 = ((f32[8,4,256]{2,1,0:T(4,128)}), f32[8,4,256]{2,1,0:T(4,128)S(1)}, u32[]{:S(2)}, u32[]{:S(2)}) async-start(f32[8,4,256]{2,1,0:T(4,128)} %fusion.25), calls=%async_computation.1 | async-start | bytes 65536 | tf_op jit(solution)/shard_map/all_to_all | solution.py:976
  147.4 128.9 %all-gather.19.cloned.1.call-start = ((), (), s32[]{:S(2)}) async-start(), calls=%async_computation.7 | async-start | bytes 9437184 | tf_op jit(solution)/shard_map/all_gather | solution.py:102
  170.8 16.5 %collective-permute-start.19 = (bf16[144,2048]{1,0:T(8,128)(2,1)}, bf16[144,2048]{1,0:T(8,128)(2,1)S(1)}, u32[]{:S(2)}, u32[]{:S(2)}) collective-permute-start(bf16[144,2048]{1,0:T(8,128)(2,1)} %get-tuple-element.137.refs_0_), channel_id=1, source_target_pairs={{0,8},{8,0},{16,24},{24,16},{1,9},{9,1},{17,25},{25,17},{2,10},{10... | collective-permute-start | bytes 1769480 | tf_op jit(solution)/shard_map/ppermute | solution.py:67
  171.5 24.9 %collective-permute-start.20 = (bf16[144,2048]{1,0:T(8,128)(2,1)}, bf16[144,2048]{1,0:T(8,128)(2,1)S(1)}, u32[]{:S(2)}, u32[]{:S(2)}) collective-permute-start(bf16[144,2048]{1,0:T(8,128)(2,1)} %get-tuple-element.137.refs_0_), channel_id=1, source_target_pairs={{0,16},{8,24},{16,0},{24,8},{1,17},{9,25},{17,1},{25,9},{2,18},{10... | collective-permute-start | bytes 1769480 | tf_op jit(solution)/shard_map/ppermute | solution.py:67
  173.2 23.1 %collective-permute-start.21 = (bf16[144,2048]{1,0:T(8,128)(2,1)}, bf16[144,2048]{1,0:T(8,128)(2,1)S(1)}, u32[]{:S(2)}, u32[]{:S(2)}) collective-permute-start(bf16[144,2048]{1,0:T(8,128)(2,1)} %get-tuple-element.137.refs_0_), channel_id=1, source_target_pairs={{0,24},{8,16},{16,8},{24,0},{1,25},{9,17},{17,9},{25,1},{2,26},{10... | collective-permute-start | bytes 1769480 | tf_op jit(solution)/shard_map/ppermute | solution.py:67
  196.4 155.2 %all-gather.21.cloned.1.call-start = ((), (), s32[]{:S(2)}) async-start(), calls=%async_computation.8 | async-start | bytes 7077888 | tf_op jit(solution)/shard_map/all_gather | solution.py:102
  211.6 16.5 %collective-permute-start.22 = (bf16[144,2048]{1,0:T(8,128)(2,1)}, bf16[144,2048]{1,0:T(8,128)(2,1)S(1)}, u32[]{:S(2)}, u32[]{:S(2)}) collective-permute-start(bf16[144,2048]{1,0:T(8,128)(2,1)} %get-tuple-element.142), channel_id=1, source_target_pairs={{0,8},{8,0},{16,24},{24,16},{1,9},{9,1},{17,25},{25,17},{2,10},{10... | collective-permute-start | bytes 1769480 | tf_op jit(solution)/shard_map/ppermute | solution.py:67
  213.3 21.9 %collective-permute-start.23 = (bf16[144,2048]{1,0:T(8,128)(2,1)}, bf16[144,2048]{1,0:T(8,128)(2,1)S(1)}, u32[]{:S(2)}, u32[]{:S(2)}) collective-permute-start(bf16[144,2048]{1,0:T(8,128)(2,1)} %get-tuple-element.143), channel_id=1, source_target_pairs={{0,16},{8,24},{16,0},{24,8},{1,17},{9,25},{17,1},{25,9},{2,18},{10... | collective-permute-start | bytes 1769480 | tf_op jit(solution)/shard_map/ppermute | solution.py:67
  213.3 22.7 %collective-permute-start.24 = (bf16[144,2048]{1,0:T(8,128)(2,1)}, bf16[144,2048]{1,0:T(8,128)(2,1)S(1)}, u32[]{:S(2)}, u32[]{:S(2)}) collective-permute-start(bf16[144,2048]{1,0:T(8,128)(2,1)} %get-tuple-element.144), channel_id=1, source_target_pairs={{0,24},{8,16},{16,8},{24,0},{1,25},{9,17},{17,9},{25,1},{2,26},{10... | collective-permute-start | bytes 1769480 | tf_op jit(solution)/shard_map/ppermute | solution.py:67
  241.3 16.5 %collective-permute-start.25 = (bf16[144,2048]{1,0:T(8,128)(2,1)}, bf16[144,2048]{1,0:T(8,128)(2,1)S(1)}, u32[]{:S(2)}, u32[]{:S(2)}) collective-permute-start(bf16[144,2048]{1,0:T(8,128)(2,1)} %get-tuple-element.175.refs_0_), channel_id=1, source_target_pairs={{0,8},{8,0},{16,24},{24,16},{1,9},{9,1},{17,25},{25,17},{2,10},{10... | collective-permute-start | bytes 1769480 | tf_op jit(solution)/shard_map/ppermute | solution.py:67
  242.5 23.6 %collective-permute-start.26 = (bf16[144,2048]{1,0:T(8,128)(2,1)}, bf16[144,2048]{1,0:T(8,128)(2,1)S(1)}, u32[]{:S(2)}, u32[]{:S(2)}) collective-permute-start(bf16[144,2048]{1,0:T(8,128)(2,1)} %get-tuple-element.175.refs_0_), channel_id=1, source_target_pairs={{0,16},{8,24},{16,0},{24,8},{1,17},{9,25},{17,1},{25,9},{2,18},{10... | collective-permute-start | bytes 1769480 | tf_op jit(solution)/shard_map/ppermute | solution.py:67
  243.8 22.3 %collective-permute-start.27 = (bf16[144,2048]{1,0:T(8,128)(2,1)}, bf16[144,2048]{1,0:T(8,128)(2,1)S(1)}, u32[]{:S(2)}, u32[]{:S(2)}) collective-permute-start(bf16[144,2048]{1,0:T(8,128)(2,1)} %get-tuple-element.175.refs_0_), channel_id=1, source_target_pairs={{0,24},{8,16},{16,8},{24,0},{1,25},{9,17},{17,9},{25,1},{2,26},{10... | collective-permute-start | bytes 1769480 | tf_op jit(solution)/shard_map/ppermute | solution.py:67
  276.3 111.7 %all-gather.23.cloned.1.call-start = ((), (), s32[]{:S(2)}) async-start(), calls=%async_computation.9 | async-start | bytes 2359296 | tf_op jit(solution)/shard_map/all_gather | solution.py:102
  285.0 4.9 %collective-permute-start.28 = (f32[4,2048]{1,0:T(4,128)}, f32[4,2048]{1,0:T(4,128)S(1)}, u32[]{:S(2)}, u32[]{:S(2)}) collective-permute-start(f32[4,2048]{1,0:T(4,128)} %get-tuple-element.151.refs_0_), channel_id=1, source_target_pairs={{0,8},{8,0},{16,24},{24,16},{1,9},{9,1},{17,25},{25,17},{2,10},{10... | collective-permute-start | bytes 98312 | tf_op jit(solution)/shard_map/ppermute | solution.py:67
  286.6 4.1 collective-permute-start.29
  288.0 5.0 %collective-permute-start.30 = (f32[4,2048]{1,0:T(4,128)}, f32[4,2048]{1,0:T(4,128)S(1)}, u32[]{:S(2)}, u32[]{:S(2)}) collective-permute-start(f32[4,2048]{1,0:T(4,128)} %get-tuple-element.151.refs_0_), channel_id=1, source_target_pairs={{0,24},{8,16},{16,8},{24,0},{1,25},{9,17},{17,9},{25,1},{2,26},{10... | collective-permute-start | bytes 98312 | tf_op jit(solution)/shard_map/ppermute | solution.py:67
  300.3 11.1 %collective-permute-start.31 = (f32[4,2048]{1,0:T(4,128)}, f32[4,2048]{1,0:T(4,128)S(1)}, u32[]{:S(2)}, u32[]{:S(2)}) collective-permute-start(f32[4,2048]{1,0:T(4,128)} %get-tuple-element.169.refs_0_), channel_id=1, source_target_pairs={{0,8},{8,0},{16,24},{24,16},{1,9},{9,1},{17,25},{25,17},{2,10},{10... | collective-permute-start | bytes 98312 | tf_op jit(solution)/shard_map/ppermute | solution.py:67
  300.9 10.5 %collective-permute-start.32 = (f32[4,2048]{1,0:T(4,128)}, f32[4,2048]{1,0:T(4,128)S(1)}, u32[]{:S(2)}, u32[]{:S(2)}) collective-permute-start(f32[4,2048]{1,0:T(4,128)} %get-tuple-element.169.refs_0_), channel_id=1, source_target_pairs={{0,16},{8,24},{16,0},{24,8},{1,17},{9,25},{17,1},{25,9},{2,18},{10... | collective-permute-start | bytes 98312 | tf_op jit(solution)/shard_map/ppermute | solution.py:67
  301.4 10.0 %collective-permute-start.33 = (f32[4,2048]{1,0:T(4,128)}, f32[4,2048]{1,0:T(4,128)S(1)}, u32[]{:S(2)}, u32[]{:S(2)}) collective-permute-start(f32[4,2048]{1,0:T(4,128)} %get-tuple-element.169.refs_0_), channel_id=1, source_target_pairs={{0,24},{8,16},{16,8},{24,0},{1,25},{9,17},{17,9},{25,1},{2,26},{10... | collective-permute-start | bytes 98312 | tf_op jit(solution)/shard_map/ppermute | solution.py:67
  321.3 10.8 %collective-permute-start.34 = (bf16[4,11776]{1,0:T(4,128)(2,1)}, bf16[4,11776]{1,0:T(4,128)(2,1)S(1)}, u32[]{:S(2)}, u32[]{:S(2)}) collective-permute-start(bf16[4,11776]{1,0:T(4,128)(2,1)} %get-tuple-element.184.refs_0_), channel_id=1, source_target_pairs={{0,1},{1,0},{2,3},{3,2},{4,5},{5,4},{6,7},{7,6},{8,9},{9,8},{10,11... | collective-permute-start | bytes 282632 | tf_op jit(solution)/shard_map/ppermute | solution.py:73
  321.4 22.8 %collective-permute-start.37 = (bf16[32,2176]{1,0:T(8,128)(2,1)}, bf16[32,2176]{1,0:T(8,128)(2,1)S(1)}, u32[]{:S(2)}, u32[]{:S(2)}) collective-permute-start(bf16[32,2176]{1,0:T(8,128)(2,1)} %get-tuple-element.181), channel_id=1, source_target_pairs={{0,8},{8,0},{16,24},{24,16},{1,9},{9,1},{17,25},{25,17},{2,10},{10... | collective-permute-start | bytes 417800 | tf_op jit(solution)/shard_map/ppermute | solution.py:67
  322.0 22.1 %collective-permute-start.38 = (bf16[32,2176]{1,0:T(8,128)(2,1)}, bf16[32,2176]{1,0:T(8,128)(2,1)S(1)}, u32[]{:S(2)}, u32[]{:S(2)}) collective-permute-start(bf16[32,2176]{1,0:T(8,128)(2,1)} %get-tuple-element.182), channel_id=1, source_target_pairs={{0,16},{8,24},{16,0},{24,8},{1,17},{9,25},{17,1},{25,9},{2,18},{10... | collective-permute-start | bytes 417800 | tf_op jit(solution)/shard_map/ppermute | solution.py:67
  322.5 21.7 %collective-permute-start.39 = (bf16[32,2176]{1,0:T(8,128)(2,1)}, bf16[32,2176]{1,0:T(8,128)(2,1)S(1)}, u32[]{:S(2)}, u32[]{:S(2)}) collective-permute-start(bf16[32,2176]{1,0:T(8,128)(2,1)} %get-tuple-element.183), channel_id=1, source_target_pairs={{0,24},{8,16},{16,8},{24,0},{1,25},{9,17},{17,9},{25,1},{2,26},{10... | collective-permute-start | bytes 417800 | tf_op jit(solution)/shard_map/ppermute | solution.py:67
  324.9 19.2 %collective-permute-start.35 = (bf16[4,11776]{1,0:T(4,128)(2,1)}, bf16[4,11776]{1,0:T(4,128)(2,1)S(1)}, u32[]{:S(2)}, u32[]{:S(2)}) collective-permute-start(bf16[4,11776]{1,0:T(4,128)(2,1)} %get-tuple-element.184.refs_0_), channel_id=1, source_target_pairs={{0,2},{1,3},{2,0},{3,1},{4,6},{5,7},{6,4},{7,5},{8,10},{9,11},{10,... | collective-permute-start | bytes 282632 | tf_op jit(solution)/shard_map/ppermute | solution.py:73
  332.1 12.0 %collective-permute-start.36 = (bf16[4,11776]{1,0:T(4,128)(2,1)}, bf16[4,11776]{1,0:T(4,128)(2,1)S(1)}, u32[]{:S(2)}, u32[]{:S(2)}) collective-permute-start(bf16[4,11776]{1,0:T(4,128)(2,1)} %get-tuple-element.184.refs_0_), channel_id=1, source_target_pairs={{0,3},{1,2},{2,1},{3,0},{4,7},{5,6},{6,5},{7,4},{8,11},{9,10},{10,... | collective-permute-start | bytes 282632 | tf_op jit(solution)/shard_map/ppermute | solution.py:73
  346.6 2.1 collective-permute-start.40
  360.2 17.0 %collective-permute-start.43 = (bf16[144,1536]{1,0:T(8,128)(2,1)}, bf16[144,1536]{1,0:T(8,128)(2,1)S(1)}, u32[]{:S(2)}, u32[]{:S(2)}) collective-permute-start(bf16[144,1536]{1,0:T(8,128)(2,1)} %get-tuple-element.194), channel_id=1, source_target_pairs={{0,24},{8,16},{16,8},{24,0},{1,25},{9,17},{17,9},{25,1},{2,26},{10... | collective-permute-start | bytes 1327112 | tf_op jit(solution)/shard_map/ppermute | solution.py:67
  361.2 24.9 %collective-permute-start.42 = (bf16[144,1536]{1,0:T(8,128)(2,1)}, bf16[144,1536]{1,0:T(8,128)(2,1)S(1)}, u32[]{:S(2)}, u32[]{:S(2)}) collective-permute-start(bf16[144,1536]{1,0:T(8,128)(2,1)} %get-tuple-element.193), channel_id=1, source_target_pairs={{0,16},{8,24},{16,0},{24,8},{1,17},{9,25},{17,1},{25,9},{2,18},{10... | collective-permute-start | bytes 1327112 | tf_op jit(solution)/shard_map/ppermute | solution.py:67
  362.7 23.3 %collective-permute-start.41 = (bf16[144,1536]{1,0:T(8,128)(2,1)}, bf16[144,1536]{1,0:T(8,128)(2,1)S(1)}, u32[]{:S(2)}, u32[]{:S(2)}) collective-permute-start(bf16[144,1536]{1,0:T(8,128)(2,1)} %get-tuple-element.192), channel_id=1, source_target_pairs={{0,8},{8,0},{16,24},{24,16},{1,9},{9,1},{17,25},{25,17},{2,10},{10... | collective-permute-start | bytes 1327112 | tf_op jit(solution)/shard_map/ppermute | solution.py:67
  364.7 31.6 %all-to-all-start.3 = ((bf16[32,40,128]{2,1,0:T(8,128)(2,1)}), bf16[32,40,128]{2,1,0:T(8,128)(2,1)S(1)}, u32[]{:S(2)}, u32[]{:S(2)}) async-start(bf16[32,40,128]{2,1,0:T(8,128)(2,1)} %get-tuple-element.207), calls=%async_computation.3 | async-start | bytes 655360 | tf_op jit(solution)/shard_map/all_to_all | solution.py:91
  369.7 33.5 %collective-permute-start.47 = (bf16[32,4224]{1,0:T(8,128)(2,1)}, bf16[32,4224]{1,0:T(8,128)(2,1)}, u32[]{:S(2)}, u32[]{:S(2)}) collective-permute-start(bf16[32,4224]{1,0:T(8,128)(2,1)} %get-tuple-element.188.refs_0_), channel_id=1, source_target_pairs={{0,8},{8,0},{16,24},{24,16},{1,9},{9,1},{17,25},{25,17},{2,10},{10... | collective-permute-start | bytes 811016 | tf_op jit(solution)/shard_map/ppermute | solution.py:67
  371.5 32.2 %collective-permute-start.48 = (bf16[32,4224]{1,0:T(8,128)(2,1)}, bf16[32,4224]{1,0:T(8,128)(2,1)}, u32[]{:S(2)}, u32[]{:S(2)}) collective-permute-start(bf16[32,4224]{1,0:T(8,128)(2,1)} %get-tuple-element.188.refs_0_), channel_id=1, source_target_pairs={{0,16},{8,24},{16,0},{24,8},{1,17},{9,25},{17,1},{25,9},{2,18},{10... | collective-permute-start | bytes 811016 | tf_op jit(solution)/shard_map/ppermute | solution.py:67
  377.2 26.6 %collective-permute-start.49 = (bf16[32,4224]{1,0:T(8,128)(2,1)}, bf16[32,4224]{1,0:T(8,128)(2,1)}, u32[]{:S(2)}, u32[]{:S(2)}) collective-permute-start(bf16[32,4224]{1,0:T(8,128)(2,1)} %get-tuple-element.188.refs_0_), channel_id=1, source_target_pairs={{0,24},{8,16},{16,8},{24,0},{1,25},{9,17},{17,9},{25,1},{2,26},{10... | collective-permute-start | bytes 811016 | tf_op jit(solution)/shard_map/ppermute | solution.py:67
  393.4 16.2 %collective-permute-start.44 = (bf16[144,512]{1,0:T(8,128)(2,1)}, bf16[144,512]{1,0:T(8,128)(2,1)S(1)}, u32[]{:S(2)}, u32[]{:S(2)}) collective-permute-start(bf16[144,512]{1,0:T(8,128)(2,1)} %get-tuple-element.204), channel_id=1, source_target_pairs={{0,8},{8,0},{16,24},{24,16},{1,9},{9,1},{17,25},{25,17},{2,10},{10... | collective-permute-start | bytes 442376 | tf_op jit(solution)/shard_map/ppermute | solution.py:67
  394.9 14.6 %collective-permute-start.45 = (bf16[144,512]{1,0:T(8,128)(2,1)}, bf16[144,512]{1,0:T(8,128)(2,1)S(1)}, u32[]{:S(2)}, u32[]{:S(2)}) collective-permute-start(bf16[144,512]{1,0:T(8,128)(2,1)} %get-tuple-element.205), channel_id=1, source_target_pairs={{0,16},{8,24},{16,0},{24,8},{1,17},{9,25},{17,1},{25,9},{2,18},{10... | collective-permute-start | bytes 442376 | tf_op jit(solution)/shard_map/ppermute | solution.py:67
  403.2 6.4 %collective-permute-start.46 = (bf16[144,512]{1,0:T(8,128)(2,1)S(1)}, bf16[144,512]{1,0:T(8,128)(2,1)S(1)}, u32[]{:S(2)}, u32[]{:S(2)}) collective-permute-start(bf16[144,512]{1,0:T(8,128)(2,1)S(1)} %copy-done.63), channel_id=1, source_target_pairs={{0,24},{8,16},{16,8},{24,0},{1,25},{9,17},{17,9},{25,1},{2,26},{10... | collective-permute-start | bytes 442376 | tf_op jit(solution)/shard_map/ppermute | solution.py:67
  (61 other events, 400.3 us)
Sparse Core Ops, SparseCore 0:
  9.7 33.3 all-gather.12
  45.3 63.6 all-gather.14
  112.1 80.4 all-gather.16
  196.5 79.7 all-gather.18
  278.3 71.1 all-gather.20
  351.7 36.2 all-gather.22
